TPU v7x, 32 devices: a whole 2x2x4 slice. The times are simulated.
32 devices in a mesh: section: 4 (over x, core), expert: 8 (over z, y).
Axes of the slice: x: 2, y: 2, z: 4, core: 2. Of those that a mesh axis runs over, the one named last changes fastest.
Arguments:
- fwd_tokens: bfloat16 [4, 16, 7168], P('section', 'expert'), may hold values from -6 to 6
- fwd_routes: int32 [4, 16, 2], P('section', 'expert'), may hold values from 0 to 3, all different within a row; in each aligned block of 2 rows (0 to 1, 2 to 3, ..., all dimensions but the last counted through in order) at most 2 rows name the same one
- fwd_probs: float32 [4, 16, 2], P('section', 'expert'), may hold values from 0.2 to 1
- bwd_tokens: bfloat16 [4, 16, 7168], P('section', 'expert'), may hold values from -6 to 6
- bwd_routes: int32 [4, 16, 2], P('section', 'expert'), may hold values from 0 to 3, all different within a row; in each aligned block of 2 rows (0 to 1, 2 to 3, ..., all dimensions but the last counted through in order) at most 2 rows name the same one
- bwd_probs: float32 [4, 16, 2], P('section', 'expert'), may hold values from 0.2 to 1
- bwd_grads: bfloat16 [4, 16, 7168], P('section', 'expert'), may hold values from -6 to 6
- w_gate: bfloat16 [7168, 8192], P(None, 'expert'), may hold values from -0.0625 to 0.0625
- w_up: bfloat16 [7168, 8192], P(None, 'expert'), may hold values from -0.0625 to 0.0625
- w_down: bfloat16 [8192, 7168], P('expert'), may hold values from -0.125 to 0.125
Outputs:
- fwd_next: bfloat16 [4, 16, 7168], P('section', 'expert')
- bwd_next: bfloat16 [4, 16, 7168], P('section', 'expert')
Inputs may be any that keep to these rules, and one draw needn't show every extreme that they name: `fwd_routes`: each token names 2 different experts; within the 2 tokens of one device, no expert is named by more than 2 tokens, a bound that some block reaches. `bwd_routes`: as for fwd_routes.
All inputs are finite; a program needn't handle non-finite values.
Results may differ from a plain program's by a relative error of at most 0.0058.
Values may be sent and summed in bfloat16 or wider, within the bound.
No kernel may reach another device: no remote copies, remote signals or barrier semaphores. Data moves between devices by JAX's collectives and lax.ppermute only.
A program may use at most 128 MiB of HBM per device.

v0:
```python
import jax
import jax.numpy as jnp
from jax import lax
from jax.sharding import PartitionSpec as P

GROUPS = 4
CAP = 2


def shifted(block, axis, distance):
    devices = range(lax.axis_size(axis))
    route = [(i - distance, i) for i in devices if i - distance in devices]
    return lax.ppermute(block, axis, route)


def route_tables(routes, probs):
    onehot = (routes[:, :, None] == jnp.arange(GROUPS, dtype=jnp.int32)[None, None, :]).astype(
        jnp.int32
    )
    flat = onehot.reshape(-1, GROUPS)
    rank = jnp.cumsum(flat, axis=0) - flat
    own_rank = jnp.sum(rank * flat, axis=1)
    slot = routes.reshape(-1) * CAP + own_rank
    select = (slot[:, None] == jnp.arange(GROUPS * CAP, dtype=jnp.int32)[None, :]).astype(
        jnp.float32
    )
    select = select.reshape(routes.shape[0], routes.shape[1], GROUPS * CAP)
    picked = jnp.sum(select, axis=1).astype(jnp.bfloat16)
    weighed = jnp.sum(select * probs[:, :, None], axis=1)
    return (picked, weighed)


def pack_rows(picked, tokens, shards):
    packed = lax.dot_general(
        picked, tokens, (((0,), (0,)), ((), ())), preferred_element_type=jnp.float32
    )
    packed = packed.astype(jnp.bfloat16).reshape(GROUPS, 1, CAP, tokens.shape[1])
    packed = jnp.broadcast_to(packed, (GROUPS, shards, CAP, tokens.shape[1]))
    return packed.reshape(GROUPS * shards, CAP, tokens.shape[1])


def unpack_rows(returned, weighed, shards):
    width = returned.shape[2]
    repeated = jnp.broadcast_to(
        weighed.reshape(-1, GROUPS, 1, CAP), (weighed.shape[0], GROUPS, shards, CAP)
    )
    repeated = repeated.reshape(weighed.shape[0], GROUPS * shards * CAP)
    flat = returned.reshape(GROUPS * shards * CAP, width)
    return jnp.dot(
        repeated,
        flat.astype(jnp.float32),
        precision=lax.Precision.HIGHEST,
        preferred_element_type=jnp.float32,
    ).astype(jnp.bfloat16)


def forward_rows(rows, w_gate, w_up, w_down):
    a = jnp.dot(rows, w_gate, preferred_element_type=jnp.float32)
    u = jnp.dot(rows, w_up, preferred_element_type=jnp.float32)
    hidden = (a * jax.nn.sigmoid(a) * u).astype(jnp.bfloat16)
    return jnp.dot(hidden, w_down, preferred_element_type=jnp.float32).astype(jnp.bfloat16)


def backward_rows(rows, grads, w_gate, w_up, w_down):
    a = jnp.dot(rows, w_gate, preferred_element_type=jnp.float32)
    u = jnp.dot(rows, w_up, preferred_element_type=jnp.float32)
    dh = lax.dot_general(
        grads, w_down, (((1,), (1,)), ((), ())), preferred_element_type=jnp.float32
    )
    sig = jax.nn.sigmoid(a)
    d_a = (dh * u * sig * (1.0 + a * (1.0 - sig))).astype(jnp.bfloat16)
    d_u = (dh * a * sig).astype(jnp.bfloat16)
    part = lax.dot_general(
        d_a, w_gate, (((1,), (1,)), ((), ())), preferred_element_type=jnp.float32
    )
    part = part + lax.dot_general(
        d_u, w_up, (((1,), (1,)), ((), ())), preferred_element_type=jnp.float32
    )
    return part.astype(jnp.bfloat16)


def local(
    fwd_tokens,
    fwd_routes,
    fwd_probs,
    bwd_tokens,
    bwd_routes,
    bwd_probs,
    bwd_grads,
    w_gate,
    w_up,
    w_down,
):
    shards = lax.axis_size("expert") // GROUPS
    width = fwd_tokens.shape[2]
    picked_f, weighed_f = route_tables(fwd_routes[0], fwd_probs[0])
    picked_b, weighed_b = route_tables(bwd_routes[0], bwd_probs[0])
    packed_f = pack_rows(picked_f, fwd_tokens[0], shards)
    packed_b = pack_rows(picked_b, bwd_tokens[0], shards)
    packed_g = pack_rows(picked_b, bwd_grads[0], shards)
    received = lax.all_to_all(packed_f, "expert", split_axis=0, concat_axis=0, tiled=True)
    out_f = forward_rows(received.reshape(-1, width), w_gate, w_up, w_down).reshape(received.shape)
    returned_f = lax.all_to_all(out_f, "expert", split_axis=0, concat_axis=0, tiled=True)
    got_b = lax.all_to_all(packed_b, "expert", split_axis=0, concat_axis=0, tiled=True)
    got_g = lax.all_to_all(packed_g, "expert", split_axis=0, concat_axis=0, tiled=True)
    out_b = backward_rows(
        got_b.reshape(-1, width), got_g.reshape(-1, width), w_gate, w_up, w_down
    ).reshape(got_b.shape)
    returned_b = lax.all_to_all(out_b, "expert", split_axis=0, concat_axis=0, tiled=True)
    layer_out = unpack_rows(returned_f, weighed_f, shards)
    input_grad = unpack_rows(returned_b, weighed_b, shards)
    fwd_next = shifted(layer_out, "section", 1)
    bwd_next = shifted(input_grad, "section", -1)
    return (fwd_next[None], bwd_next[None])


def solution(mesh):
    return jax.shard_map(
        local,
        mesh=mesh,
        in_specs=(
            P("section", "expert", None),
            P("section", "expert", None),
            P("section", "expert", None),
            P("section", "expert", None),
            P("section", "expert", None),
            P("section", "expert", None),
            P("section", "expert", None),
            P(None, "expert"),
            P(None, "expert"),
            P("expert", None),
        ),
        out_specs=(P("section", "expert", None), P("section", "expert", None)),
        check_vma=False,
    )
```

profile of v0, /device:TPU:1, one launch (start us, length us, event | category | flops | bytes accessed | tf_op | source)
XLA Modules:
  0.0 116.7 jit_solution(5175600386705291490)
XLA Ops:
  0.6 0.8 eq.67
  1.4 0.1 fusion.20
  1.5 0.2 select_reduce_fusion.1
  1.7 0.1 reduce_sum.63
  1.8 0.7 bitcast_add_fusion
  2.5 0.8 convert_reduce_fusion
  3.2 0.2 convolution_convert_fusion.1
  3.5 0.8 broadcast_in_dim.57
  4.3 6.4 %all-to-all-start.3 = ((bf16[8,2,7168]{2,1,0:T(2,128)(2,1)}), bf16[8,2,7168]{2,1,0:T(2,128)(2,1)S(1)}, u32[]{:S(2)}, u32[]{:S(2)}) async-start(bf16[8,2,7168]{2,1,0:T(2,128)(2,1)} %bitcast.10), calls=%async_computation.3 | async-start | bytes 458752 | tf_op jit(solution)/shard_map/all_to_all | solution.py:104
  10.7 1.0 convolution_convert_fusion.2
  11.7 0.8 eq.60
  12.6 0.2 select_reduce_fusion.3
  12.7 0.1 reduce_sum.59
  12.8 0.7 bitcast_add_fusion.1
  13.6 0.8 convert_reduce_fusion.1
  14.3 1.0 convolution_convert_fusion.3
  15.4 2.3 %all-to-all-done.3 = bf16[8,2,7168]{2,1,0:T(2,128)(2,1)S(1)} async-done(((bf16[8,2,7168]{2,1,0:T(2,128)(2,1)}), bf16[8,2,7168]{2,1,0:T(2,128)(2,1)S(1)}, u32[]{:S(2)}, u32[]{:S(2)}) %all-to-all-start.3) | async-done | bytes 229408 | tf_op jit(solution)/shard_map/all_to_all | solution.py:104
  17.6 0.8 broadcast_in_dim.55
  18.4 4.6 %all-to-all-start.2 = ((bf16[8,2,7168]{2,1,0:T(2,128)(2,1)}), bf16[8,2,7168]{2,1,0:T(2,128)(2,1)S(1)}, u32[]{:S(2)}, u32[]{:S(2)}) async-start(bf16[8,2,7168]{2,1,0:T(2,128)(2,1)} %bitcast.8), calls=%async_computation.2 | async-start | bytes 458752 | tf_op jit(solution)/shard_map/all_to_all | solution.py:105
  23.0 0.1 reshape.109
  23.1 7.2 %fusion.30 = f32[16,1024]{1,0:T(8,128)S(1)} fusion(bf16[16,7168]{1,0:T(8,128)(2,1)S(1)} %reshape.109, bf16[7168,1024]{1,0:T(8,128)(2,1)} %param.17), kind=kOutput, calls=%fused_computation.53 | convolution fusion | flops 234881024 | bytes 14974976 | tf_op jit(solution)/shard_map/dot_general | solution.py:65
  30.3 0.8 broadcast_in_dim.50
  31.1 5.4 %all-to-all-start = ((bf16[8,2,7168]{2,1,0:T(2,128)(2,1)}), bf16[8,2,7168]{2,1,0:T(2,128)(2,1)S(1)}, u32[]{:S(2)}, u32[]{:S(2)}) async-start(bf16[8,2,7168]{2,1,0:T(2,128)(2,1)} %bitcast.3), calls=%async_computation | async-start | bytes 458752 | tf_op jit(solution)/shard_map/all_to_all | solution.py:101
  36.5 0.1 reshape.107
  36.6 9.1 %fusion.29 = f32[16,1024]{1,0:T(8,128)S(1)} fusion(bf16[16,7168]{1,0:T(8,128)(2,1)S(1)} %reshape.107, bf16[1024,7168]{1,0:T(8,128)(2,1)} %param.19), kind=kOutput, calls=%fused_computation.52 | convolution fusion | flops 234881024 | bytes 14974976 | tf_op jit(solution)/shard_map/dot_general | solution.py:67
  45.7 12.4 %fusion.5 = f32[16,7168]{1,0:T(8,128)S(1)} fusion(bf16[7168,1024]{1,0:T(8,128)(2,1)} %param.17, f32[16,1024]{1,0:T(8,128)S(1)} %fusion.29, bf16[16,7168]{1,0:T(8,128)(2,1)S(1)} %reshape.109, bf16[7168,1024]{1,0:T(8,128)(2,1)} %param.18, f32[16,1024]{1,0:T(8,128)S(1)} %fusion.30), kind=kOutput, calls=%fused_computation.14 | convolution fusion | flops 469925888 | bytes 30179328 | tf_op jit(solution)/shard_map/dot_general | solution.py:73
  58.1 9.1 %fusion = bf16[16,7168]{1,0:T(8,128)(2,1)S(1)} fusion(f32[16,7168]{1,0:T(8,128)S(1)} %fusion.5, bf16[7168,1024]{1,0:T(8,128)(2,1)} %param.18, f32[16,1024]{1,0:T(8,128)S(1)} %fusion.29, f32[16,1024]{1,0:T(8,128)S(1)} %fusion.30), kind=kOutput, calls=%fused_computation.1 | convolution fusion | flops 235208704 | bytes 15499264 | tf_op jit(solution)/shard_map/dot_general | solution.py:76
  67.2 0.8 reshape.110
  67.9 5.4 %all-to-all-start.4 = ((bf16[8,2,7168]{2,1,0:T(2,128)(2,1)}), bf16[8,2,7168]{2,1,0:T(2,128)(2,1)S(1)}, u32[]{:S(2)}, u32[]{:S(2)}) async-start(bf16[8,2,7168]{2,1,0:T(2,128)(2,1)} %reshape.110), calls=%async_computation.4 | async-start | bytes 458752 | tf_op jit(solution)/shard_map/all_to_all | solution.py:109
  73.4 0.1 reshape.102
  73.5 7.2 %fusion.28 = f32[16,1024]{1,0:T(8,128)S(1)} fusion(bf16[16,7168]{1,0:T(8,128)(2,1)S(1)} %reshape.102, bf16[7168,1024]{1,0:T(8,128)(2,1)} %param.17), kind=kOutput, calls=%fused_computation.51 | convolution fusion | flops 234881024 | bytes 14974976 | tf_op jit(solution)/shard_map/dot_general | solution.py:58
  80.7 13.3 %convolution_convert_fusion = bf16[16,7168]{1,0:T(8,128)(2,1)S(1)} fusion(bf16[1024,7168]{1,0:T(8,128)(2,1)} %param.19, bf16[16,7168]{1,0:T(8,128)(2,1)S(1)} %reshape.102, bf16[7168,1024]{1,0:T(8,128)(2,1)} %param.18, f32[16,1024]{1,0:T(8,128)S(1)} %fusion.28), kind=kOutput, calls=%fused_computation.2 | convolution fusion | flops 469975040 | bytes 29884416 | tf_op jit(solution)/shard_map/dot_general | solution.py:61
  94.0 0.8 reshape.103
  94.8 5.4 %all-to-all-start.1 = ((bf16[8,2,7168]{2,1,0:T(2,128)(2,1)}), bf16[8,2,7168]{2,1,0:T(2,128)(2,1)S(1)}, u32[]{:S(2)}, u32[]{:S(2)}) async-start(bf16[8,2,7168]{2,1,0:T(2,128)(2,1)} %reshape.103), calls=%async_computation.1 | async-start | bytes 458752 | tf_op jit(solution)/shard_map/all_to_all | solution.py:103
  100.2 0.1 broadcast_in_dim.52
  100.3 0.1 reshape.105
  100.4 0.1 broadcast_in_dim.47
  100.5 0.1 reshape.100
  100.5 0.1 reshape.111
  100.6 0.2 convolution_convert_fusion.4
  100.9 4.8 %collective-permute-start.1 = (bf16[2,7168]{1,0:T(2,128)(2,1)S(1)}, bf16[2,7168]{1,0:T(2,128)(2,1)S(1)}, u32[]{:S(2)}, u32[]{:S(2)}) collective-permute-start(bf16[2,7168]{1,0:T(2,128)(2,1)S(1)} %convolution_convert_fusion.4), channel_id=1, source_target_pairs={{8,0},{16,8},{24,16},{9,1},{17,9},{25,17},{10,2},{18,10},{26,18},{... | collective-permute-start | bytes 86024 | tf_op jit(solution)/shard_map/ppermute | solution.py:13
  105.8 1.3 %all-to-all-done.1 = bf16[8,2,7168]{2,1,0:T(2,128)(2,1)S(1)} async-done(((bf16[8,2,7168]{2,1,0:T(2,128)(2,1)}), bf16[8,2,7168]{2,1,0:T(2,128)(2,1)S(1)}, u32[]{:S(2)}, u32[]{:S(2)}) %all-to-all-start.1) | async-done | bytes 229408 | tf_op jit(solution)/shard_map/all_to_all | solution.py:103
  107.0 0.1 reshape.104
  107.1 0.2 convolution_convert_fusion.5
  107.4 7.1 %collective-permute-start = (bf16[2,7168]{1,0:T(2,128)(2,1)S(1)}, bf16[2,7168]{1,0:T(2,128)(2,1)S(1)}, u32[]{:S(2)}, u32[]{:S(2)}) collective-permute-start(bf16[2,7168]{1,0:T(2,128)(2,1)S(1)} %convolution_convert_fusion.5), channel_id=1, source_target_pairs={{0,8},{8,16},{16,24},{1,9},{9,17},{17,25},{2,10},{10,18},{18,26},{... | collective-permute-start | bytes 86024 | tf_op jit(solution)/shard_map/ppermute | solution.py:13
  114.5 1.0 collective-permute-done
  115.4 0.6 copy.14
  116.1 0.6 copy.15
  (14 shorter events, 0.3 us)
Async XLA Ops:
  0.6 2.6 %copy-start = (bf16[1,2,7168]{2,1,0:T(2,128)(2,1)S(1)}, bf16[1,2,7168]{2,1,0:T(2,128)(2,1)}, u32[]{:S(2)}) copy-start(bf16[1,2,7168]{2,1,0:T(2,128)(2,1)} %param.13) | copy-start | bytes 86020
  4.3 13.3 %all-to-all-start.3 = ((bf16[8,2,7168]{2,1,0:T(2,128)(2,1)}), bf16[8,2,7168]{2,1,0:T(2,128)(2,1)S(1)}, u32[]{:S(2)}, u32[]{:S(2)}) async-start(bf16[8,2,7168]{2,1,0:T(2,128)(2,1)} %bitcast.10), calls=%async_computation.3 | async-start | bytes 458752 | tf_op jit(solution)/shard_map/all_to_all | solution.py:104
  18.4 11.9 %all-to-all-start.2 = ((bf16[8,2,7168]{2,1,0:T(2,128)(2,1)}), bf16[8,2,7168]{2,1,0:T(2,128)(2,1)S(1)}, u32[]{:S(2)}, u32[]{:S(2)}) async-start(bf16[8,2,7168]{2,1,0:T(2,128)(2,1)} %bitcast.8), calls=%async_computation.2 | async-start | bytes 458752 | tf_op jit(solution)/shard_map/all_to_all | solution.py:105
  31.1 36.8 %all-to-all-start = ((bf16[8,2,7168]{2,1,0:T(2,128)(2,1)}), bf16[8,2,7168]{2,1,0:T(2,128)(2,1)S(1)}, u32[]{:S(2)}, u32[]{:S(2)}) async-start(bf16[8,2,7168]{2,1,0:T(2,128)(2,1)} %bitcast.3), calls=%async_computation | async-start | bytes 458752 | tf_op jit(solution)/shard_map/all_to_all | solution.py:101
  67.9 26.8 %all-to-all-start.4 = ((bf16[8,2,7168]{2,1,0:T(2,128)(2,1)}), bf16[8,2,7168]{2,1,0:T(2,128)(2,1)S(1)}, u32[]{:S(2)}, u32[]{:S(2)}) async-start(bf16[8,2,7168]{2,1,0:T(2,128)(2,1)} %reshape.110), calls=%async_computation.4 | async-start | bytes 458752 | tf_op jit(solution)/shard_map/all_to_all | solution.py:109
  94.8 12.3 %all-to-all-start.1 = ((bf16[8,2,7168]{2,1,0:T(2,128)(2,1)}), bf16[8,2,7168]{2,1,0:T(2,128)(2,1)S(1)}, u32[]{:S(2)}, u32[]{:S(2)}) async-start(bf16[8,2,7168]{2,1,0:T(2,128)(2,1)} %reshape.103), calls=%async_computation.1 | async-start | bytes 458752 | tf_op jit(solution)/shard_map/all_to_all | solution.py:103
  100.9 13.6 %collective-permute-start.1 = (bf16[2,7168]{1,0:T(2,128)(2,1)S(1)}, bf16[2,7168]{1,0:T(2,128)(2,1)S(1)}, u32[]{:S(2)}, u32[]{:S(2)}) collective-permute-start(bf16[2,7168]{1,0:T(2,128)(2,1)S(1)} %convolution_convert_fusion.4), channel_id=1, source_target_pairs={{8,0},{16,8},{24,16},{9,1},{17,9},{25,17},{10,2},{18,10},{26,18},{... | collective-permute-start | bytes 86024 | tf_op jit(solution)/shard_map/ppermute | solution.py:13
  107.4 8.1 %collective-permute-start = (bf16[2,7168]{1,0:T(2,128)(2,1)S(1)}, bf16[2,7168]{1,0:T(2,128)(2,1)S(1)}, u32[]{:S(2)}, u32[]{:S(2)}) collective-permute-start(bf16[2,7168]{1,0:T(2,128)(2,1)S(1)} %convolution_convert_fusion.5), channel_id=1, source_target_pairs={{0,8},{8,16},{16,24},{1,9},{9,17},{17,25},{2,10},{10,18},{18,26},{... | collective-permute-start | bytes 86024 | tf_op jit(solution)/shard_map/ppermute | solution.py:13
where the time goes:
time: 118 us; the launch traced here: 117 us
  matrix products  60.8 us (52%)
  starting transfers between devices  39.2 us (33%)
  local copies, waits for them, and re-layouts  7.85 us (7%)
  waiting for transfers between devices  4.53 us (4%)
  other arithmetic  3.5 us (3%)
    dot_general x1, matrix products, forward_rows(): jnp.dot(hidden, w_down, preferred_element_type=jnp.float32)  13.3 us
    dot_general x1, matrix products, backward_rows(): lax.dot_general(d_a, w_gate, (((1,), (1,)), ((), ())), preferred_element_...  12.4 us
    ppermute x2, starting transfers between devices, shifted(): return lax.ppermute(block, axis, route)  11.9 us
    dot_general x1, matrix products, backward_rows(): lax.dot_general(d_u, w_up, (((1,), (1,)), ((), ())), preferred_element_ty...  9.09 us
    dot_general x1, matrix products, backward_rows(): lax.dot_general(grads, w_down, (((1,), (1,)), ((), ())), preferred_elemen...  9.06 us
    dot_general x1, matrix products, backward_rows(): a = jnp.dot(rows, w_gate, preferred_element_type=jnp.float32)  7.19 us
    dot_general x1, matrix products, forward_rows(): a = jnp.dot(rows, w_gate, preferred_element_type=jnp.float32)  7.19 us
    all_to_all x1, starting transfers between devices, local(): lax.all_to_all(packed_b, 'expert', split_axis=0, concat_axis=0, tiled=True)  6.38 us
  transfers between devices with their start and end apart: 7, of which 3 were waited for; matrix products, arithmetic and copies ran while one was open for 56% of the time, Pallas kernels for 0%

commit v1 on v0

v1 whole, which is shorter than its diff:
```python
import functools

import jax
import jax.numpy as jnp
from jax import lax
from jax.experimental import pallas as pl
from jax.experimental.pallas import tpu as pltpu
from jax.sharding import PartitionSpec as P

GROUPS = 4
TILE = 256
F32 = jnp.float32
BF16 = jnp.bfloat16
NT = (((1,), (1,)), ((), ()))


def swap_cores(block):
    sections = range(lax.axis_size("section"))
    return lax.ppermute(block, "section", [(i, i ^ 1) for i in sections])


def shifted(block, distance):
    sections = range(lax.axis_size("section"))
    route = [(i - distance, i) for i in sections if i - distance in sections]
    return lax.ppermute(block, "section", route)


def expert_weights(routes, probs):
    named = routes[:, :, None] == jnp.arange(GROUPS, dtype=jnp.int32)
    return jnp.sum(jnp.where(named, probs[:, :, None], 0.0), axis=1)


def halves(rows, core):
    half = rows.shape[1] // 2
    first, second = rows[:, :half], rows[:, half:]
    return jnp.where(core == 0, first, second), jnp.where(core == 0, second, first)


def by_section(own, other, core):
    return jnp.where(core == 0, jnp.stack([own, other]), jnp.stack([other, own]))


def to_all(block):
    spread = jnp.broadcast_to(block[None], (lax.axis_size("expert"),) + block.shape)
    return lax.all_to_all(spread, "expert", split_axis=0, concat_axis=0, tiled=True)


def interleave(count, inverse=False):
    blocks = count // 8
    out = lax.broadcasted_iota(jnp.int32, (count, count), 1 if inverse else 0)
    src = lax.broadcasted_iota(jnp.int32, (count, count), 0 if inverse else 1)
    want = lax.rem(lax.div(out, 4), 2) * (blocks * 4) + lax.div(out, 8) * 4 + lax.rem(out, 4)
    return jnp.where(want == src, 1.0, 0.0).astype(BF16)


def dot(a, b):
    return jnp.dot(a, b, preferred_element_type=F32)


def dot_nt(a, b):
    return lax.dot_general(a, b, NT, preferred_element_type=F32)


def fwd_up_kernel(core, x, wg0, wg1, wu0, wu1, out):
    n = x.shape[0] // 2
    hid = wg0.shape[1]
    rows = dot(interleave(2 * n, True), x[...]).astype(BF16)
    a = dot(rows[:n], wg0[...]) + dot(rows[n:], wg1[...])
    u = dot(rows[:n], wu0[...]) + dot(rows[n:], wu1[...])

    @pl.when(pl.program_id(0) == 0)
    def _():
        out[...] = jnp.zeros_like(out)

    out[:, :hid] += a
    out[:, hid:] += u


def bwd_up_kernel(core, x0, x1, wg0, wg1, wu0, wu1, wd0, wd1, out):
    n = x0.shape[0] // 2
    hid = wg0.shape[1]
    sel = interleave(2 * n, True)
    rows0 = dot(sel, x0[...]).astype(BF16)
    rows1 = dot(sel, x1[...]).astype(BF16)
    a = dot(rows0[:n], wg0[...]) + dot(rows1[:n], wg1[...])
    u = dot(rows0[:n], wu0[...]) + dot(rows1[:n], wu1[...])
    dh = dot_nt(rows0[n:], wd0[...]) + dot_nt(rows1[n:], wd1[...])

    @pl.when(pl.program_id(0) == 0)
    def _():
        out[...] = jnp.zeros_like(out)

    out[:, :hid] += a
    out[:, hid : 2 * hid] += u
    out[:, 2 * hid :] += dh


def fwd_down_kernel(core, part, other, wd0, wd1, out, h):
    hid = h.shape[1]

    @pl.when(pl.program_id(0) == 0)
    def _():
        both = part[...] + other[...]
        a, u = both[:, :hid], both[:, hid:]
        h[...] = (a * jax.nn.sigmoid(a) * u).astype(BF16)

    y0 = dot(h[...], wd0[...]).astype(BF16)
    y1 = dot(h[...], wd1[...]).astype(BF16)
    cat = jnp.concatenate([y0, y1], axis=0)
    out[...] = dot(interleave(cat.shape[0]), cat).astype(BF16)


def bwd_down_kernel(core, part, other, wg0, wg1, wu0, wu1, out, da, du):
    hid = da.shape[1]

    @pl.when(pl.program_id(0) == 0)
    def _():
        both = part[...] + other[...]
        a, u, dh = both[:, :hid], both[:, hid : 2 * hid], both[:, 2 * hid :]
        s = jax.nn.sigmoid(a)
        da[...] = (dh * u * s * (1.0 + a * (1.0 - s))).astype(BF16)
        du[...] = (dh * a * s).astype(BF16)

    y0 = (dot_nt(da[...], wg0[...]) + dot_nt(du[...], wu0[...])).astype(BF16)
    y1 = (dot_nt(da[...], wg1[...]) + dot_nt(du[...], wu1[...])).astype(BF16)
    cat = jnp.concatenate([y0, y1], axis=0)
    out[...] = dot(interleave(cat.shape[0]), cat).astype(BF16)


def run(kernel, core, steps, operands, specs, out_spec, out_shape, scratch, flops):
    nbytes = sum(b * 2 * steps for b in flops)
    return pl.pallas_call(
        kernel,
        grid_spec=pltpu.PrefetchScalarGridSpec(
            num_scalar_prefetch=1,
            grid=(steps,),
            in_specs=specs,
            out_specs=out_spec,
            scratch_shapes=scratch,
        ),
        out_shape=out_shape,
        compiler_params=pltpu.CompilerParams(vmem_limit_bytes=48 * 2**20),
        cost_estimate=pl.CostEstimate(
            flops=nbytes * 64, bytes_accessed=nbytes, transcendentals=0
        ),
    )(core, *operands)


def local(
    fwd_tokens,
    fwd_routes,
    fwd_probs,
    bwd_tokens,
    bwd_routes,
    bwd_probs,
    bwd_grads,
    w_gate,
    w_up,
    w_down,
):
    ranks = lax.axis_size("expert")
    shards = ranks // GROUPS
    width = fwd_tokens.shape[2]
    hid = w_gate.shape[1]
    quarter = width // 4
    steps = quarter // TILE
    core = lax.axis_index("section") % 2
    which = core.astype(jnp.int32).reshape(1)
    rows = 4 * ranks

    keep, send = halves(jnp.concatenate([bwd_tokens[0], bwd_grads[0]]), core)
    pair = by_section(keep, swap_cores(send), core)
    block_b = jnp.concatenate([pair[:, :2].reshape(4, -1), pair[:, 2:].reshape(4, -1)])
    got_b = to_all(block_b).reshape(2 * rows, width // 2)

    moved = shifted(fwd_tokens[0], 1)
    keep, send = halves(moved, core)
    block_f = by_section(keep, swap_cores(send), core).reshape(4, 2, quarter)
    block_f = block_f.transpose(1, 0, 2).reshape(8, quarter)
    got_f = to_all(block_f).reshape(2 * rows, quarter)

    weights = jnp.stack(
        [
            shifted(expert_weights(fwd_routes[0], fwd_probs[0]), 1),
            expert_weights(bwd_routes[0], bwd_probs[0]),
        ]
    )
    weights = by_section(weights, swap_cores(weights), core)
    weights = weights.transpose(1, 3, 0, 2).reshape(2, GROUPS, 1, 1, 4)
    weights = jnp.broadcast_to(weights, (2, GROUPS, shards, 2, 4)).reshape(2, ranks, 8, 1)

    def tall(q):
        return pl.BlockSpec((TILE, hid), lambda k, c: ((2 * c[0] + q) * steps + k, 0))

    def wide(q):
        return pl.BlockSpec((hid, TILE), lambda k, c: (0, (2 * c[0] + q) * steps + k))

    def cols(q):
        return pl.BlockSpec((2 * rows, TILE), lambda k, c: (0, q * steps + k))

    def whole(n):
        return pl.BlockSpec((rows, n * hid), lambda k, c: (0, 0))

    part_b = run(
        bwd_up_kernel,
        which,
        steps,
        (got_b, got_b, w_gate, w_gate, w_up, w_up, w_down, w_down),
        [cols(0), cols(1), tall(0), tall(1), tall(0), tall(1), wide(0), wide(1)],
        whole(3),
        jax.ShapeDtypeStruct((rows, 3 * hid), F32),
        [],
        [6 * TILE * hid],
    )
    out_b = run(
        bwd_down_kernel,
        which,
        steps,
        (part_b, swap_cores(part_b), w_gate, w_gate, w_up, w_up),
        [whole(3), whole(3), tall(0), tall(1), tall(0), tall(1)],
        cols(0),
        jax.ShapeDtypeStruct((2 * rows, quarter), BF16),
        [pltpu.VMEM((rows, hid), BF16)] * 2,
        [4 * TILE * hid],
    )
    back_b = lax.all_to_all(
        out_b.reshape(ranks, 8, quarter), "expert", split_axis=0, concat_axis=0, tiled=True
    )

    part_f = run(
        fwd_up_kernel,
        which,
        steps,
        (got_f, w_gate, w_gate, w_up, w_up),
        [cols(0), tall(0), tall(1), tall(0), tall(1)],
        whole(2),
        jax.ShapeDtypeStruct((rows, 2 * hid), F32),
        [],
        [4 * TILE * hid],
    )
    out_f = run(
        fwd_down_kernel,
        which,
        steps,
        (part_f, swap_cores(part_f), w_down, w_down),
        [whole(2), whole(2), wide(0), wide(1)],
        cols(0),
        jax.ShapeDtypeStruct((2 * rows, quarter), BF16),
        [pltpu.VMEM((rows, hid), BF16)],
        [2 * TILE * hid],
    )
    back_f = lax.all_to_all(
        out_f.reshape(ranks, 8, quarter), "expert", split_axis=0, concat_axis=0, tiled=True
    )

    def finished(back, weight):
        total = jnp.sum(back.astype(F32) * weight, axis=0).astype(BF16)
        both = total.reshape(2, 2, 2, quarter).transpose(1, 2, 0, 3).reshape(2, 2, width // 2)
        own = jnp.where(core == 0, both[0], both[1])
        other = swap_cores(jnp.where(core == 0, both[1], both[0]))
        return jnp.where(
            core == 0,
            jnp.concatenate([own, other], axis=1),
            jnp.concatenate([other, own], axis=1),
        )

    bwd_next = shifted(finished(back_b, weights[1]), -1)
    fwd_next = finished(back_f, weights[0])
    return (fwd_next[None], bwd_next[None])


def solution(mesh):
    return jax.shard_map(
        local,
        mesh=mesh,
        in_specs=(
            P("section", "expert", None),
            P("section", "expert", None),
            P("section", "expert", None),
            P("section", "expert", None),
            P("section", "expert", None),
            P("section", "expert", None),
            P("section", "expert", None),
            P(None, "expert"),
            P(None, "expert"),
            P("expert", None),
        ),
        out_specs=(P("section", "expert", None), P("section", "expert", None)),
        check_vma=False,
    )
```

time: 118 us -> 102 us (0.86)
  matrix products: 60.8 us -> 0 us
  Pallas kernels: 0 us -> 37.8 us
  waiting for transfers between devices: 4.53 us -> 19.2 us
  local copies, waits for them, and re-layouts: 7.85 us -> 2.67 us
  other arithmetic: 3.5 us -> 2.2 us
  starting transfers between devices: 39.2 us -> 38 us
    dot_general x11 -> x0, matrix products: 60.8 us -> none  [the longest x1 13.3 us: forward_rows(): jnp.dot(hidden, w_down, preferred_element_type=jnp.float32)]
    pallas_call x0 -> x4, Pallas kernels: none -> 37.8 us  [run(): pl.pallas_call(kernel, grid_spec=pltpu.PrefetchScalarGridSpec(num_scalar_...]
    all_to_all x5 -> x4, waiting for transfers between devices: 3.57 us -> 13.9 us  [the longest x2 7.29 us: to_all(): lax.all_to_all(spread, 'expert', split_axis=0, concat_axis=0, tiled=True)]
    all_to_all x5 -> x4, starting transfers between devices: 27.3 us -> 18.8 us  [the longest x2 9.73 us: to_all(): lax.all_to_all(spread, 'expert', split_axis=0, concat_axis=0, tiled=True)]
    ppermute x2 -> x10, starting transfers between devices: 11.9 us -> 19.1 us  [the longest x3 10.9 us: shifted(): return lax.ppermute(block, 'section', route)]
    ppermute x2 -> x10, waiting for transfers between devices: 0.96 us -> 5.33 us  [the longest x3 3.89 us: shifted(): return lax.ppermute(block, 'section', route)]
    reshape x9 -> x2, local copies, waits for them, and re-layouts: 2.2 us -> 0.03 us  [the longest x1 0.02 us: local(): pair[:, 2:].reshape(4, -1)]
    eq x2 -> x0, local copies, waits for them, and re-layouts: 1.53 us -> none  [route_tables(): routes[:, :, None] == jnp.arange(GROUPS, dtype=jnp.int32)[None, None, :]]
  transfers between devices with their start and end apart: 7 -> 14, of which waited for: 3 -> 8; matrix products, arithmetic and copies ran while one was open for 56% -> 2% of each run, Pallas kernels for 0% -> 37%
where the time goes in v1:
time: 102 us; the launch traced here: 101 us
  starting transfers between devices  38 us (37%)
  Pallas kernels  37.8 us (37%)
  waiting for transfers between devices  19.2 us (19%)
  local copies, waits for them, and re-layouts  2.67 us (3%)
  other arithmetic  2.2 us (2%)
    pallas_call x4, Pallas kernels, run(): pl.pallas_call(kernel, grid_spec=pltpu.PrefetchScalarGridSpec(num_scalar_...  37.8 us
    ppermute x3, starting transfers between devices, shifted(): return lax.ppermute(block, 'section', route)  10.9 us
    all_to_all x2, starting transfers between devices, to_all(): lax.all_to_all(spread, 'expert', split_axis=0, concat_axis=0, tiled=True)  9.73 us
    ppermute x7, starting transfers between devices, swap_cores(): return lax.ppermute(block, 'section', [(i, i ^ 1) for i in sections])  8.25 us
    all_to_all x2, waiting for transfers between devices, to_all(): lax.all_to_all(spread, 'expert', split_axis=0, concat_axis=0, tiled=True)  7.29 us
    all_to_all x1, waiting for transfers between devices, local(): lax.all_to_all(out_b.reshape(ranks, 8, quarter), 'expert', split_axis=0,...  6.62 us
    all_to_all x1, starting transfers between devices, local(): lax.all_to_all(out_b.reshape(ranks, 8, quarter), 'expert', split_axis=0,...  5.71 us
    ppermute x3, waiting for transfers between devices, shifted(): return lax.ppermute(block, 'section', route)  3.89 us
  transfers between devices with their start and end apart: 14, of which 8 were waited for; matrix products, arithmetic and copies ran while one was open for 2% of the time, Pallas kernels for 37%

profile of v1, /device:TPU:1, one launch (start us, length us, event | category | flops | bytes accessed | tf_op | source)
XLA Modules:
  0.0 100.8 jit_solution(17247998912752781980)
XLA Ops:
  0.6 4.5 %collective-permute-start = (bf16[2,7168]{1,0:T(2,128)(2,1)}, bf16[2,7168]{1,0:T(2,128)(2,1)S(1)}, u32[]{:S(2)}, u32[]{:S(2)}) collective-permute-start(bf16[2,7168]{1,0:T(2,128)(2,1)} %bitcast.63), channel_id=1, source_target_pairs={{0,8},{8,16},{16,24},{1,9},{9,17},{17,25},{2,10},{10,18},{18,26},{... | collective-permute-start | bytes 86024 | tf_op jit(solution)/shard_map/ppermute | solution.py:25
  5.2 0.9 select_bitcast_fusion
  6.1 0.1 collective-permute-start.6
  6.1 0.2 collective-permute-done
  6.4 0.4 collective-permute-start.1
  6.7 0.6 collective-permute-done.6
  7.5 0.1 collective-permute-done.1
  7.7 0.7 broadcast_in_dim.53
  8.4 5.6 %all-to-all-start = ((bf16[8,8,1792]{2,1,0:T(8,128)(2,1)}), bf16[8,8,1792]{2,1,0:T(8,128)(2,1)S(1)}, u32[]{:S(2)}, u32[]{:S(2)}) async-start(bf16[8,8,1792]{2,1,0:T(8,128)(2,1)} %broadcast_in_dim.53), calls=%async_computation | async-start | bytes 458752 | tf_op jit(solution)/shard_map/all_to_all | solution.py:45
  14.0 7.3 %all-to-all-done = bf16[8,8,1792]{2,1,0:T(8,128)(2,1)S(1)} async-done(((bf16[8,8,1792]{2,1,0:T(8,128)(2,1)}), bf16[8,8,1792]{2,1,0:T(8,128)(2,1)S(1)}, u32[]{:S(2)}, u32[]{:S(2)}) %all-to-all-start) | async-done | bytes 229408 | tf_op jit(solution)/shard_map/all_to_all | solution.py:45
  21.3 0.8 broadcast_in_dim.61
  22.1 4.2 %all-to-all-start.2 = ((bf16[8,8,3584]{2,1,0:T(8,128)(2,1)}), bf16[8,8,3584]{2,1,0:T(8,128)(2,1)S(1)}, u32[]{:S(2)}, u32[]{:S(2)}) async-start(bf16[8,8,3584]{2,1,0:T(8,128)(2,1)} %broadcast_in_dim.61), calls=%async_computation.2 | async-start | bytes 917504 | tf_op jit(solution)/shard_map/all_to_all | solution.py:45
  26.3 8.7 %shard_map.113.part = f32[32,2048]{1,0:T(8,128)S(1)} custom-call(s32[1]{0:T(128)} %bitcast.core, bf16[64,1792]{1,0:T(8,128)(2,1)S(1)} %bitcast.40, bf16[7168,1024]{1,0:T(8,128)(2,1)} %wg1.5, bf16[7168,1024]{1,0:T(8,128)(2,1)} %wg1.5, bf16[7168,1024]{1,0:T(8,128)(2,1)} %wu1.5, bf16[7168,1024]{1,0:T(8,128)(2,1)} %wu1.5), custom_call_target="tpu_custom_call" | custom-call | flops 939524096 | bytes 14680064 | tf_op jit(solution)/shard_map/pallas_call | solution.py:132
  35.0 1.4 %collective-permute-start.2 = (f32[32,2048]{1,0:T(8,128)S(1)}, f32[32,2048]{1,0:T(8,128)S(1)}, u32[]{:S(2)}, u32[]{:S(2)}) collective-permute-start(f32[32,2048]{1,0:T(8,128)S(1)} %shard_map.113.part), channel_id=1, source_target_pairs={{0,8},{8,0},{16,24},{24,16},{1,9},{9,1},{17,25},{25,17},{2,10},{10... | collective-permute-start | bytes 786440 | tf_op jit(solution)/shard_map/ppermute | solution.py:19
  36.5 0.0 all-to-all-done.2
  36.5 11.4 %shard_map.115.part = f32[32,3072]{1,0:T(8,128)S(1)} custom-call(s32[1]{0:T(128)} %bitcast.core, bf16[64,3584]{1,0:T(8,128)(2,1)S(1)} %bitcast.38, bf16[64,3584]{1,0:T(8,128)(2,1)S(1)} %bitcast.39, bf16[7168,1024]{1,0:T(8,128)(2,1)} %wg1.5, bf16[7168,1024]{1,0:T(8,128)(2,1)} %wg1.5, bf16[7168,1024]{1,0:T(8,128)(2,1)} %wu1.5, bf16[7168,1024]{1,0:T(8,128)(2,1)} %wu1.5, ...), custom_call_target="tpu_custom_call" | custom-call | flops 1409286144 | bytes 22020096 | tf_op jit(solution)/shard_map/pallas_call | solution.py:132
  47.9 0.0 copy-start
  47.9 0.0 copy-start.1
  47.9 0.0 copy-start.2
  47.9 0.0 copy-start.3
  47.9 4.0 %collective-permute-start.7 = (f32[32,3072]{1,0:T(8,128)S(1)}, f32[32,3072]{1,0:T(8,128)S(1)}, u32[]{:S(2)}, u32[]{:S(2)}) collective-permute-start(f32[32,3072]{1,0:T(8,128)S(1)} %shard_map.115.part), channel_id=1, source_target_pairs={{0,8},{8,0},{16,24},{24,16},{1,9},{9,1},{17,25},{25,17},{2,10},{10... | collective-permute-start | bytes 1179656 | tf_op jit(solution)/shard_map/ppermute | solution.py:19
  51.9 0.0 collective-permute-done.2.other
  51.9 7.3 %shard_map.114 = bf16[64,1792]{1,0:T(8,128)(2,1)} custom-call(s32[1]{0:T(128)} %bitcast.core, f32[32,2048]{1,0:T(8,128)S(1)} %shard_map.113.part, f32[32,2048]{1,0:T(8,128)S(1)} %collective-permute-done.2.other, bf16[1024,7168]{1,0:T(8,128)(2,1)} %wd1.3, bf16[1024,7168]{1,0:T(8,128)(2,1)} %wd1.3), custom_call_target="tpu_custom_call" | custom-call | flops 469762048 | bytes 7340032 | tf_op jit(solution)/shard_map/pallas_call | solution.py:132
  59.2 3.4 %all-to-all-start.1 = ((bf16[8,8,1792]{2,1,0:T(8,128)(2,1)}), bf16[8,8,1792]{2,1,0:T(8,128)(2,1)S(1)}, u32[]{:S(2)}, u32[]{:S(2)}) async-start(bf16[8,8,1792]{2,1,0:T(8,128)(2,1)} %bitcast.6), calls=%async_computation.1 | async-start | bytes 458752 | tf_op jit(solution)/shard_map/all_to_all | solution.py:252
  62.6 0.1 fusion.3
  62.7 4.1 %collective-permute-start.3 = (f32[2,4]{1,0:T(2,128)S(1)}, f32[2,4]{1,0:T(2,128)S(1)}, u32[]{:S(2)}, u32[]{:S(2)}) collective-permute-start(f32[2,4]{1,0:T(2,128)S(1)} %fusion.3), channel_id=1, source_target_pairs={{0,8},{8,16},{16,24},{1,9},{9,17},{17,25},{2,10},{10,18},{18,26},{... | collective-permute-start | bytes 104 | tf_op jit(solution)/shard_map/ppermute | solution.py:25
  66.9 0.1 fusion.4
  67.0 0.6 collective-permute-done.3
  67.6 0.0 collective-permute-start.4
  67.6 0.0 collective-permute-done.7.other
  67.6 10.4 %shard_map.116 = bf16[64,1792]{1,0:T(8,128)(2,1)} custom-call(s32[1]{0:T(128)} %bitcast.core, f32[32,3072]{1,0:T(8,128)S(1)} %shard_map.115.part, f32[32,3072]{1,0:T(8,128)S(1)} %collective-permute-done.7.other, bf16[7168,1024]{1,0:T(8,128)(2,1)} %wg1.5, bf16[7168,1024]{1,0:T(8,128)(2,1)} %wg1.5, bf16[7168,1024]{1,0:T(8,128)(2,1)} %wu1.5, bf16[7168,1024]{1,0:T(8,128)(2,1)} %wu1.5), custom_call_target="tpu_custom_call" | custom-call | flops 939524096 | bytes 14680064 | tf_op jit(solution)/shard_map/pallas_call | solution.py:132
  77.9 0.0 all-to-all-done.1
  77.9 5.7 %all-to-all-start.3 = ((bf16[8,8,1792]{2,1,0:T(8,128)(2,1)}), bf16[8,8,1792]{2,1,0:T(8,128)(2,1)S(1)}, u32[]{:S(2)}, u32[]{:S(2)}) async-start(bf16[8,8,1792]{2,1,0:T(8,128)(2,1)} %bitcast.26), calls=%async_computation.3 | async-start | bytes 458752 | tf_op jit(solution)/shard_map/all_to_all | solution.py:226
  83.6 0.0 collective-permute-done.4
  83.7 0.1 copy.19
  83.8 0.1 broadcast_in_dim.63
  83.9 0.1 copy.18
  84.0 0.1 broadcast_in_dim.60
  84.0 0.1 multiply_reduce_fusion.1
  84.2 6.6 %all-to-all-done.3 = bf16[8,8,1792]{2,1,0:T(8,128)(2,1)S(1)} async-done(((bf16[8,8,1792]{2,1,0:T(8,128)(2,1)}), bf16[8,8,1792]{2,1,0:T(8,128)(2,1)S(1)}, u32[]{:S(2)}, u32[]{:S(2)}) %all-to-all-start.3) | async-done | bytes 229408 | tf_op jit(solution)/shard_map/all_to_all | solution.py:226
  90.8 0.1 multiply_reduce_fusion
  91.0 2.3 %collective-permute-start.8 = (bf16[2,3584]{1,0:T(2,128)(2,1)S(1)}, bf16[2,3584]{1,0:T(2,128)(2,1)S(1)}, u32[]{:S(2)}, u32[]{:S(2)}) collective-permute-start(bf16[2,3584]{1,0:T(2,128)(2,1)S(1)} %bitcast.53), channel_id=1, source_target_pairs={{0,8},{8,0},{16,24},{24,16},{1,9},{9,1},{17,25},{25,17},{2,10},{10... | collective-permute-start | bytes 43016 | tf_op jit(solution)/shard_map/ppermute | solution.py:19
  93.3 0.1 collective-permute-start.5
  93.4 0.7 collective-permute-done.8
  94.1 2.3 %collective-permute-start.9 = (bf16[2,7168]{1,0:T(2,128)(2,1)S(1)}, bf16[2,7168]{1,0:T(2,128)(2,1)S(1)}, u32[]{:S(2)}, u32[]{:S(2)}) collective-permute-start(bf16[2,7168]{1,0:T(2,128)(2,1)S(1)} %broadcast_select_fusion), channel_id=1, source_target_pairs={{8,0},{16,8},{24,16},{9,1},{17,9},{25,17},{10,2},{18,10},{26,18},{... | collective-permute-start | bytes 86024 | tf_op jit(solution)/shard_map/ppermute | solution.py:25
  96.4 0.6 broadcast_select_fusion.2
  97.1 3.1 %collective-permute-done.9 = bf16[2,7168]{1,0:T(2,128)(2,1)S(1)} collective-permute-done((bf16[2,7168]{1,0:T(2,128)(2,1)S(1)}, bf16[2,7168]{1,0:T(2,128)(2,1)S(1)}, u32[]{:S(2)}, u32[]{:S(2)}) %collective-permute-start.9) | collective-permute-done | bytes 28704 | tf_op jit(solution)/shard_map/ppermute | solution.py:25
  100.2 0.6 copy.23
  (25 shorter events, 0.5 us)
Async XLA Ops:
  0.6 5.7 %collective-permute-start = (bf16[2,7168]{1,0:T(2,128)(2,1)}, bf16[2,7168]{1,0:T(2,128)(2,1)S(1)}, u32[]{:S(2)}, u32[]{:S(2)}) collective-permute-start(bf16[2,7168]{1,0:T(2,128)(2,1)} %bitcast.63), channel_id=1, source_target_pairs={{0,8},{8,16},{16,24},{1,9},{9,17},{17,25},{2,10},{10,18},{18,26},{... | collective-permute-start | bytes 86024 | tf_op jit(solution)/shard_map/ppermute | solution.py:25
  6.1 1.3 %collective-permute-start.6 = (bf16[4,3584]{1,0:T(4,128)(2,1)S(1)}, bf16[4,3584]{1,0:T(4,128)(2,1)S(1)}, u32[]{:S(2)}, u32[]{:S(2)}) collective-permute-start(bf16[4,3584]{1,0:T(4,128)(2,1)S(1)} %get-tuple-element.5), channel_id=1, source_target_pairs={{0,8},{8,0},{16,24},{24,16},{1,9},{9,1},{17,25},{25,17},{2,10},{10... | collective-permute-start | bytes 86024 | tf_op jit(solution)/shard_map/ppermute | solution.py:19
  6.4 1.2 %collective-permute-start.1 = (bf16[2,3584]{1,0:T(2,128)(2,1)S(1)}, bf16[2,3584]{1,0:T(2,128)(2,1)S(1)}, u32[]{:S(2)}, u32[]{:S(2)}) collective-permute-start(bf16[2,3584]{1,0:T(2,128)(2,1)S(1)} %get-tuple-element.11), channel_id=1, source_target_pairs={{0,8},{8,0},{16,24},{24,16},{1,9},{9,1},{17,25},{25,17},{2,10},{10... | collective-permute-start | bytes 43016 | tf_op jit(solution)/shard_map/ppermute | solution.py:19
  8.4 12.9 %all-to-all-start = ((bf16[8,8,1792]{2,1,0:T(8,128)(2,1)}), bf16[8,8,1792]{2,1,0:T(8,128)(2,1)S(1)}, u32[]{:S(2)}, u32[]{:S(2)}) async-start(bf16[8,8,1792]{2,1,0:T(8,128)(2,1)} %broadcast_in_dim.53), calls=%async_computation | async-start | bytes 458752 | tf_op jit(solution)/shard_map/all_to_all | solution.py:45
  22.1 14.4 %all-to-all-start.2 = ((bf16[8,8,3584]{2,1,0:T(8,128)(2,1)}), bf16[8,8,3584]{2,1,0:T(8,128)(2,1)S(1)}, u32[]{:S(2)}, u32[]{:S(2)}) async-start(bf16[8,8,3584]{2,1,0:T(8,128)(2,1)} %broadcast_in_dim.61), calls=%async_computation.2 | async-start | bytes 917504 | tf_op jit(solution)/shard_map/all_to_all | solution.py:45
  35.0 16.9 %collective-permute-start.2 = (f32[32,2048]{1,0:T(8,128)S(1)}, f32[32,2048]{1,0:T(8,128)S(1)}, u32[]{:S(2)}, u32[]{:S(2)}) collective-permute-start(f32[32,2048]{1,0:T(8,128)S(1)} %shard_map.113.part), channel_id=1, source_target_pairs={{0,8},{8,0},{16,24},{24,16},{1,9},{9,1},{17,25},{25,17},{2,10},{10... | collective-permute-start | bytes 786440 | tf_op jit(solution)/shard_map/ppermute | solution.py:19
  47.9 14.7 %copy-start = (f32[1,2,2]{2,1,0:T(2,128)S(1)}, f32[1,2,2]{2,1,0:T(2,128)}, u32[]{:S(2)}) copy-start(f32[1,2,2]{2,1,0:T(2,128)} %param.12) | copy-start | bytes 52
  47.9 14.7 %copy-start.1 = (s32[1,2,2]{2,1,0:T(2,128)S(1)}, s32[1,2,2]{2,1,0:T(2,128)}, u32[]{:S(2)}) copy-start(s32[1,2,2]{2,1,0:T(2,128)} %param.11) | copy-start | bytes 52
  47.9 19.0 %copy-start.2 = (f32[1,2,2]{2,1,0:T(2,128)S(1)}, f32[1,2,2]{2,1,0:T(2,128)}, u32[]{:S(2)}) copy-start(f32[1,2,2]{2,1,0:T(2,128)} %param.15) | copy-start | bytes 52
  47.9 19.0 %copy-start.3 = (s32[1,2,2]{2,1,0:T(2,128)S(1)}, s32[1,2,2]{2,1,0:T(2,128)}, u32[]{:S(2)}) copy-start(s32[1,2,2]{2,1,0:T(2,128)} %param.14) | copy-start | bytes 52
  47.9 19.6 %collective-permute-start.7 = (f32[32,3072]{1,0:T(8,128)S(1)}, f32[32,3072]{1,0:T(8,128)S(1)}, u32[]{:S(2)}, u32[]{:S(2)}) collective-permute-start(f32[32,3072]{1,0:T(8,128)S(1)} %shard_map.115.part), channel_id=1, source_target_pairs={{0,8},{8,0},{16,24},{24,16},{1,9},{9,1},{17,25},{25,17},{2,10},{10... | collective-permute-start | bytes 1179656 | tf_op jit(solution)/shard_map/ppermute | solution.py:19
  59.2 18.7 %all-to-all-start.1 = ((bf16[8,8,1792]{2,1,0:T(8,128)(2,1)}), bf16[8,8,1792]{2,1,0:T(8,128)(2,1)S(1)}, u32[]{:S(2)}, u32[]{:S(2)}) async-start(bf16[8,8,1792]{2,1,0:T(8,128)(2,1)} %bitcast.6), calls=%async_computation.1 | async-start | bytes 458752 | tf_op jit(solution)/shard_map/all_to_all | solution.py:252
  62.7 4.8 %collective-permute-start.3 = (f32[2,4]{1,0:T(2,128)S(1)}, f32[2,4]{1,0:T(2,128)S(1)}, u32[]{:S(2)}, u32[]{:S(2)}) collective-permute-start(f32[2,4]{1,0:T(2,128)S(1)} %fusion.3), channel_id=1, source_target_pairs={{0,8},{8,16},{16,24},{1,9},{9,17},{17,25},{2,10},{10,18},{18,26},{... | collective-permute-start | bytes 104 | tf_op jit(solution)/shard_map/ppermute | solution.py:25
  67.6 16.1 %collective-permute-start.4 = (f32[2,2,4]{2,1,0:T(2,128)S(1)}, f32[2,2,4]{2,1,0:T(2,128)S(1)}, u32[]{:S(2)}, u32[]{:S(2)}) collective-permute-start(f32[2,2,4]{2,1,0:T(2,128)S(1)} %get-tuple-element.15), channel_id=1, source_target_pairs={{0,8},{8,0},{16,24},{24,16},{1,9},{9,1},{17,25},{25,17},{2,10},{10... | collective-permute-start | bytes 200 | tf_op jit(solution)/shard_map/ppermute | solution.py:19
  77.9 12.9 %all-to-all-start.3 = ((bf16[8,8,1792]{2,1,0:T(8,128)(2,1)}), bf16[8,8,1792]{2,1,0:T(8,128)(2,1)S(1)}, u32[]{:S(2)}, u32[]{:S(2)}) async-start(bf16[8,8,1792]{2,1,0:T(8,128)(2,1)} %bitcast.26), calls=%async_computation.3 | async-start | bytes 458752 | tf_op jit(solution)/shard_map/all_to_all | solution.py:226
  91.0 3.1 %collective-permute-start.8 = (bf16[2,3584]{1,0:T(2,128)(2,1)S(1)}, bf16[2,3584]{1,0:T(2,128)(2,1)S(1)}, u32[]{:S(2)}, u32[]{:S(2)}) collective-permute-start(bf16[2,3584]{1,0:T(2,128)(2,1)S(1)} %bitcast.53), channel_id=1, source_target_pairs={{0,8},{8,0},{16,24},{24,16},{1,9},{9,1},{17,25},{25,17},{2,10},{10... | collective-permute-start | bytes 43016 | tf_op jit(solution)/shard_map/ppermute | solution.py:19
  93.3 3.1 %collective-permute-start.5 = (bf16[2,3584]{1,0:T(2,128)(2,1)S(1)}, bf16[2,3584]{1,0:T(2,128)(2,1)S(1)}, u32[]{:S(2)}, u32[]{:S(2)}) collective-permute-start(bf16[2,3584]{1,0:T(2,128)(2,1)S(1)} %bitcast.52), channel_id=1, source_target_pairs={{0,8},{8,0},{16,24},{24,16},{1,9},{9,1},{17,25},{25,17},{2,10},{10... | collective-permute-start | bytes 43016 | tf_op jit(solution)/shard_map/ppermute | solution.py:19
  94.1 6.0 %collective-permute-start.9 = (bf16[2,7168]{1,0:T(2,128)(2,1)S(1)}, bf16[2,7168]{1,0:T(2,128)(2,1)S(1)}, u32[]{:S(2)}, u32[]{:S(2)}) collective-permute-start(bf16[2,7168]{1,0:T(2,128)(2,1)S(1)} %broadcast_select_fusion), channel_id=1, source_target_pairs={{8,0},{16,8},{24,16},{9,1},{17,9},{25,17},{10,2},{18,10},{26,18},{... | collective-permute-start | bytes 86024 | tf_op jit(solution)/shard_map/ppermute | solution.py:25

commit v2 on v0

v2 whole, which is shorter than its diff:
```python
import functools

import jax
import jax.numpy as jnp
from jax import lax
from jax.experimental import pallas as pl
from jax.experimental.pallas import tpu as pltpu
from jax.sharding import PartitionSpec as P

GROUPS = 4
LANES = 128
PARTS = 4
F32 = jnp.float32
BF16 = jnp.bfloat16
NT = (((1,), (1,)), ((), ()))


def swap_cores(block):
    sections = range(lax.axis_size("section"))
    return lax.ppermute(block, "section", [(i, i ^ 1) for i in sections])


def swap_chips(block):
    odd = range(1, lax.axis_size("section") - 1, 2)
    return lax.ppermute(block, "section", [(i, i + 1) for i in odd] + [(i + 1, i) for i in odd])


def expert_weights(routes, probs):
    named = routes[:, :, None] == jnp.arange(GROUPS, dtype=jnp.int32)
    return jnp.sum(jnp.where(named, probs[:, :, None], 0.0), axis=1)


def as_lanes(weights, rows):
    high = lax.reduce_precision(weights, 8, 7)
    middle = lax.reduce_precision(weights - high, 8, 7)
    low = weights - high - middle
    terms = jnp.concatenate([high, middle, low], axis=1).astype(BF16)
    return jnp.pad(terms, ((0, rows - terms.shape[0]), (0, LANES - terms.shape[1])))


def from_lanes(block):
    terms = block[:2, : 3 * GROUPS].astype(F32)
    return terms[:, :GROUPS] + terms[:, GROUPS : 2 * GROUPS] + terms[:, 2 * GROUPS :]


def split_width(message, core):
    width = message.shape[1] - LANES
    half = width // 2
    first, second, lanes = message[:, :half], message[:, half:width], message[:, width:]
    keep = jnp.where(core == 0, first, second)
    send = jnp.where(core == 0, second, first)
    got = swap_cores(jnp.concatenate([send, lanes], axis=1))
    fwd = jnp.where(core == 0, keep, got[:, :half])[:2]
    bwd = jnp.where(core == 0, got[:, :half], keep)
    mine, theirs = from_lanes(lanes), from_lanes(got[:, half:])
    return (
        jnp.concatenate([fwd, bwd]),
        jnp.where(core == 0, mine, theirs),
        jnp.where(core == 0, theirs, mine),
    )


def to_all(block):
    rows, width = block.shape
    block = block.reshape(rows, PARTS, width // PARTS).transpose(1, 0, 2)
    block = block.reshape(1, rows * PARTS, width // PARTS)
    ranks = lax.axis_size("expert")
    spread = jnp.broadcast_to(block, (ranks,) + block.shape[1:])
    got = lax.all_to_all(spread, "expert", split_axis=0, concat_axis=0, tiled=True)
    return got.reshape(ranks * rows * PARTS, width // PARTS)


def dot(a, b):
    return jnp.dot(a, b, preferred_element_type=F32)


def dot_nt(a, b):
    return lax.dot_general(a, b, NT, preferred_element_type=F32)


def gathered_order(ranks):
    count = ranks * PARTS * 6
    out = lax.broadcasted_iota(jnp.int32, (count, count), 0)
    src = lax.broadcasted_iota(jnp.int32, (count, count), 1)
    part, rest = lax.div(out, 6 * ranks), lax.rem(out, 6 * ranks)
    kind, rest = lax.div(rest, 2 * ranks), lax.rem(rest, 2 * ranks)
    want = lax.div(rest, 2) * (6 * PARTS) + part * 6 + kind * 2 + lax.rem(rest, 2)
    return jnp.where(want == src, 1.0, 0.0).astype(BF16)


def returned_order(ranks):
    count = ranks * 8
    out = lax.broadcasted_iota(jnp.int32, (count, count), 0)
    src = lax.broadcasted_iota(jnp.int32, (count, count), 1)
    want = lax.div(lax.rem(out, 8), 2) * (2 * ranks) + lax.div(out, 8) * 2 + lax.rem(out, 2)
    return jnp.where(want == src, 1.0, 0.0).astype(BF16)


def fetch_kernel(core, wg, wu, wd, g, u, d, sems):
    half = g.shape[0]
    start = pl.multiple_of(core[0] * half, half)
    copies = [
        pltpu.make_async_copy(wg.at[pl.ds(start, half)], g, sems.at[0]),
        pltpu.make_async_copy(wu.at[pl.ds(start, half)], u, sems.at[1]),
        pltpu.make_async_copy(wd.at[:, pl.ds(start, half)], d, sems.at[2]),
    ]
    for copy in copies:
        copy.start()
    for copy in copies:
        copy.wait()


def fetch(core, w_gate, w_up, w_down):
    width, hid = w_gate.shape
    half = width // 2
    return pl.pallas_call(
        fetch_kernel,
        in_specs=[pl.BlockSpec(memory_space=pltpu.SMEM)]
        + [pl.BlockSpec(memory_space=pl.ANY)] * 3,
        out_specs=[pl.BlockSpec(memory_space=pltpu.VMEM)] * 3,
        out_shape=[
            pltpu.VMEM((half, hid), BF16),
            pltpu.VMEM((half, hid), BF16),
            pltpu.VMEM((hid, half), BF16),
        ],
        scratch_shapes=[pltpu.SemaphoreType.DMA((3,))],
        compiler_params=pltpu.CompilerParams(vmem_limit_bytes=32 * 2**20),
        cost_estimate=pl.CostEstimate(
            flops=0, bytes_accessed=6 * half * hid * 2, transcendentals=0
        ),
    )(core, w_gate, w_up, w_down)


def up_kernel(ranks, near, far, g, u, d, out):
    hid = g.shape[1]
    n = 2 * ranks
    piece = near.shape[1]
    order = gathered_order(ranks)
    near_rows = dot(order, near[...]).astype(BF16)
    far_rows = dot(order, far[...]).astype(BF16)
    a, b, dh = 0.0, 0.0, 0.0
    for part in range(PARTS):
        at = part * 3 * n
        cols = slice(part * piece, (part + 1) * piece)
        rows = jnp.concatenate(
            [
                near_rows[at : at + n],
                far_rows[at : at + n],
                near_rows[at + n : at + 2 * n],
                far_rows[at + n : at + 2 * n],
            ]
        )
        grads = jnp.concatenate(
            [near_rows[at + 2 * n : at + 3 * n], far_rows[at + 2 * n : at + 3 * n]]
        )
        a += dot(rows, g[cols, :])
        b += dot(rows, u[cols, :])
        dh += dot_nt(grads, d[:, cols])
    out[:, :hid] = a[: 2 * n]
    out[:, hid : 2 * hid] = b[: 2 * n]
    out[:, 2 * hid : 3 * hid] = a[2 * n :]
    out[:, 3 * hid : 4 * hid] = b[2 * n :]
    out[:, 4 * hid :] = dh


def down_kernel(ranks, mine, theirs, g, u, d, out):
    hid = g.shape[1]
    a = mine[:, :hid] + theirs[:, :hid]
    b = mine[:, hid : 2 * hid] + theirs[:, hid : 2 * hid]
    h = (a * jax.nn.sigmoid(a) * b).astype(BF16)
    a = mine[:, 2 * hid : 3 * hid] + theirs[:, 2 * hid : 3 * hid]
    b = mine[:, 3 * hid : 4 * hid] + theirs[:, 3 * hid : 4 * hid]
    dh = mine[:, 4 * hid :] + theirs[:, 4 * hid :]
    s = jax.nn.sigmoid(a)
    da = (dh * b * s * (1.0 + a * (1.0 - s))).astype(BF16)
    du = (dh * a * s).astype(BF16)
    order = returned_order(ranks)
    piece = out.shape[1] // PARTS
    for part in range(PARTS):
        cols = slice(part * piece, (part + 1) * piece)
        y = dot(h, d[:, cols])
        dx = dot_nt(da, g[cols, :]) + dot_nt(du, u[cols, :])
        rows = jnp.concatenate([y.astype(BF16), dx.astype(BF16)])
        out[:, cols] = dot(order, rows).astype(BF16)


def on_core(kernel, operands, shape, dtype, passes, weight):
    return pl.pallas_call(
        kernel,
        in_specs=[pl.BlockSpec(memory_space=pltpu.VMEM)] * len(operands),
        out_specs=pl.BlockSpec(memory_space=pltpu.VMEM),
        out_shape=jax.ShapeDtypeStruct(shape, dtype),
        compiler_params=pltpu.CompilerParams(vmem_limit_bytes=12 * 2**20),
        cost_estimate=pl.CostEstimate(
            flops=passes * 2 * weight.size * 256,
            bytes_accessed=passes * weight.size * 2,
            transcendentals=0,
        ),
    )(*operands)


def local(
    fwd_tokens,
    fwd_routes,
    fwd_probs,
    bwd_tokens,
    bwd_routes,
    bwd_probs,
    bwd_grads,
    w_gate,
    w_up,
    w_down,
):
    ranks = lax.axis_size("expert")
    shards = ranks // GROUPS
    width = fwd_tokens.shape[2]
    hid = w_gate.shape[1]
    core = lax.axis_index("section") % 2

    fwd = jnp.concatenate(
        [
            jnp.pad(fwd_tokens[0], ((0, 2), (0, 0))),
            as_lanes(expert_weights(fwd_routes[0], fwd_probs[0]), 4),
        ],
        axis=1,
    )
    bwd = jnp.concatenate(
        [
            jnp.concatenate([bwd_tokens[0], bwd_grads[0]]),
            as_lanes(expert_weights(bwd_routes[0], bwd_probs[0]), 4),
        ],
        axis=1,
    )
    near, near_fw, near_bw = split_width(jnp.where(core == 0, fwd, bwd), core)
    far, far_fw, far_bw = split_width(swap_chips(jnp.where(core == 0, bwd, fwd)), core)
    got_near = to_all(near)
    got_far = to_all(far)

    which, _ = lax.optimization_barrier((core.astype(jnp.int32).reshape(1), near))
    g, u, d = fetch(which, w_gate, w_up, w_down)
    part = on_core(
        functools.partial(up_kernel, ranks),
        (got_near, got_far, g, u, d),
        (4 * ranks, 5 * hid),
        F32,
        3,
        g,
    )
    out = on_core(
        functools.partial(down_kernel, ranks),
        (part, swap_cores(part), g, u, d),
        (8 * ranks, width // 2),
        BF16,
        3,
        g,
    )
    back = lax.all_to_all(
        out.reshape(ranks, 8, width // 2), "expert", split_axis=0, concat_axis=0, tiled=True
    )

    weights = jnp.concatenate([near_fw, far_fw, near_bw, far_bw]).T[:, None]
    weights = jnp.broadcast_to(weights, (GROUPS, shards, 8)).reshape(ranks, 8, 1)
    total = jnp.sum(back.astype(F32) * weights, axis=0).astype(BF16)
    first = jnp.concatenate([total[2:4], total[4:6]])
    second = jnp.concatenate([total[:2], total[6:]])
    own = jnp.where(core == 0, first, second)
    other = swap_cores(jnp.where(core == 0, second, first))
    whole = jnp.where(
        core == 0,
        jnp.concatenate([own, other], axis=1),
        jnp.concatenate([other, own], axis=1),
    )
    return (whole[None, :2], whole[None, 2:])


def solution(mesh):
    return jax.shard_map(
        local,
        mesh=mesh,
        in_specs=(
            P("section", "expert", None),
            P("section", "expert", None),
            P("section", "expert", None),
            P("section", "expert", None),
            P("section", "expert", None),
            P("section", "expert", None),
            P("section", "expert", None),
            P(None, "expert"),
            P(None, "expert"),
            P("expert", None),
        ),
        out_specs=(P("section", "expert", None), P("section", "expert", None)),
        check_vma=False,
    )
```

time: 118 us -> 94.9 us (0.80)
  matrix products: 60.8 us -> 0 us
  waiting for transfers between devices: 4.53 us -> 25 us
  Pallas kernels: 0 us -> 19.6 us
  starting transfers between devices: 39.2 us -> 24.8 us
  local copies, waits for them, and re-layouts: 7.85 us -> 20.5 us
    dot_general x11 -> x0, matrix products: 60.8 us -> none  [the longest x1 13.3 us: forward_rows(): jnp.dot(hidden, w_down, preferred_element_type=jnp.float32)]
    pallas_call x0 -> x3, Pallas kernels: none -> 19.6 us  [the longest x2 12.1 us: on_core(): pl.pallas_call(kernel, in_specs=[pl.BlockSpec(memory_space=pltpu.VMEM)] *...]
    all_to_all x5 -> x3, waiting for transfers between devices: 3.57 us -> 20.7 us  [the longest x1 12.2 us: local(): lax.all_to_all(out.reshape(ranks, 8, width // 2), 'expert', split_axis=0,...]
    unnamed x4 -> x12, local copies, waits for them, and re-layouts: 1.23 us -> 18.2 us
    all_to_all x5 -> x3, starting transfers between devices: 27.3 us -> 17.5 us  [the longest x2 11.7 us: to_all(): lax.all_to_all(spread, 'expert', split_axis=0, concat_axis=0, tiled=True)]
    ppermute x2 -> x5, starting transfers between devices: 11.9 us -> 7.34 us  [the longest x1 4.47 us: swap_chips(): lax.ppermute(block, 'section', [(i, i + 1) for i in odd] + [(i + 1, i) fo...]
    ppermute x2 -> x5, waiting for transfers between devices: 0.96 us -> 4.35 us  [the longest x4 2.58 us: swap_cores(): return lax.ppermute(block, 'section', [(i, i ^ 1) for i in sections])]
    reshape x9 -> x0, local copies, waits for them, and re-layouts: 2.2 us -> none  [the longest x1 0.79 us: local(): forward_rows(received.reshape(-1, width), w_gate, w_up, w_down)]
  transfers between devices with their start and end apart: 7 -> 8, of which waited for: 3 -> 5; matrix products, arithmetic and copies ran while one was open for 56% -> 1% of each run, Pallas kernels for 0% -> 8%
where the time goes in v2:
time: 94.9 us; the launch traced here: 94 us
  waiting for transfers between devices  25 us (26%)
  starting transfers between devices  24.8 us (26%)
  local copies, waits for them, and re-layouts  20.5 us (22%)
  Pallas kernels  19.6 us (21%)
  other arithmetic  3.24 us (3%)
    unnamed x12, local copies, waits for them, and re-layouts  18.2 us
    all_to_all x1, waiting for transfers between devices, local(): lax.all_to_all(out.reshape(ranks, 8, width // 2), 'expert', split_axis=0,...  12.2 us
    pallas_call x2, Pallas kernels, on_core(): pl.pallas_call(kernel, in_specs=[pl.BlockSpec(memory_space=pltpu.VMEM)] *...  12.1 us
    all_to_all x2, starting transfers between devices, to_all(): lax.all_to_all(spread, 'expert', split_axis=0, concat_axis=0, tiled=True)  11.7 us
    all_to_all x2, waiting for transfers between devices, to_all(): lax.all_to_all(spread, 'expert', split_axis=0, concat_axis=0, tiled=True)  8.52 us
    pallas_call x1, Pallas kernels, fetch(): pl.pallas_call(fetch_kernel, in_specs=[pl.BlockSpec(memory_space=pltpu.SM...  7.44 us
    all_to_all x1, starting transfers between devices, local(): lax.all_to_all(out.reshape(ranks, 8, width // 2), 'expert', split_axis=0,...  5.73 us
    ppermute x1, starting transfers between devices, swap_chips(): lax.ppermute(block, 'section', [(i, i + 1) for i in odd] + [(i + 1, i) fo...  4.47 us
  transfers between devices with their start and end apart: 8, of which 5 were waited for; matrix products, arithmetic and copies ran while one was open for 1% of the time, Pallas kernels for 8%

profile of v2, /device:TPU:1, one launch (start us, length us, event | category | flops | bytes accessed | tf_op | source)
XLA Modules:
  0.0 94.0 jit_solution(12181929769997711804)
XLA Ops:
  0.6 0.8 fusion.2
  1.4 0.8 fusion.3
  2.2 0.1 fusion.15
  2.3 0.9 broadcast_select_fusion
  3.3 0.1 collective-permute-start
  3.4 4.5 %collective-permute-start.1 = (bf16[4,7296]{1,0:T(4,128)(2,1)S(1)}, bf16[4,7296]{1,0:T(4,128)(2,1)S(1)}, u32[]{:S(2)}, u32[]{:S(2)}) collective-permute-start(bf16[4,7296]{1,0:T(4,128)(2,1)S(1)} %get-tuple-element.14), channel_id=1, source_target_pairs={{8,16},{16,8},{9,17},{17,9},{10,18},{18,10},{11,19},{19,11},{12,20... | collective-permute-start | bytes 175112 | tf_op jit(solution)/shard_map/ppermute | solution.py:25
  7.9 0.0 collective-permute-done
  7.9 1.8 %collective-permute-done.1 = bf16[4,7296]{1,0:T(4,128)(2,1)S(1)} collective-permute-done((bf16[4,7296]{1,0:T(4,128)(2,1)S(1)}, bf16[4,7296]{1,0:T(4,128)(2,1)S(1)}, u32[]{:S(2)}, u32[]{:S(2)}) %collective-permute-start.1) | collective-permute-done | bytes 58400 | tf_op jit(solution)/shard_map/ppermute | solution.py:25
  9.8 0.1 collective-permute-start.2
  9.9 0.8 broadcast_in_dim.56
  10.7 6.2 %all-to-all-start = ((bf16[8,24,896]{2,1,0:T(8,128)(2,1)}), bf16[8,24,896]{2,1,0:T(8,128)(2,1)S(1)}, u32[]{:S(2)}, u32[]{:S(2)}) async-start(bf16[8,24,896]{2,1,0:T(8,128)(2,1)} %broadcast_in_dim.56), calls=%async_computation | async-start | bytes 688128 | tf_op jit(solution)/shard_map/all_to_all | solution.py:69
  16.8 0.0 collective-permute-done.2
  17.0 8.5 %all-to-all-done = bf16[8,24,896]{2,1,0:T(8,128)(2,1)S(1)} async-done(((bf16[8,24,896]{2,1,0:T(8,128)(2,1)}), bf16[8,24,896]{2,1,0:T(8,128)(2,1)S(1)}, u32[]{:S(2)}, u32[]{:S(2)}) %all-to-all-start) | async-done | bytes 344096 | tf_op jit(solution)/shard_map/all_to_all | solution.py:69
  25.5 0.8 broadcast_in_dim.58
  26.3 5.6 %all-to-all-start.1 = ((bf16[8,24,896]{2,1,0:T(8,128)(2,1)}), bf16[8,24,896]{2,1,0:T(8,128)(2,1)S(1)}, u32[]{:S(2)}, u32[]{:S(2)}) async-start(bf16[8,24,896]{2,1,0:T(8,128)(2,1)} %broadcast_in_dim.58), calls=%async_computation.1 | async-start | bytes 688128 | tf_op jit(solution)/shard_map/all_to_all | solution.py:69
  31.8 7.4 %shard_map.113 = (bf16[3584,1024]{1,0:T(8,128)(2,1)S(1)}, bf16[3584,1024]{1,0:T(8,128)(2,1)S(1)}, bf16[1024,3584]{1,0:T(8,128)(2,1)S(1)}) custom-call(s32[1]{0:T(128)} %bitcast.13.core, bf16[7168,1024]{1,0:T(8,128)(2,1)} %wg.1, bf16[7168,1024]{1,0:T(8,128)(2,1)} %wu.1, bf16[1024,7168]{1,0:T(8,128)(2,1)} %wd.1), custom_call_target="tpu_custom_call" | custom-call | bytes 44040192 | tf_op jit(solution)/shard_map/pallas_call | solution.py:116
  39.3 0.0 copy-start
  39.3 2.9 %copy-done = bf16[3584,1024]{1,0:T(8,128)(2,1)} copy-done((bf16[3584,1024]{1,0:T(8,128)(2,1)}, bf16[3584,1024]{1,0:T(8,128)(2,1)S(1)}, u32[]{:S(2)}) %copy-start) | copy-done | bytes 7340056
  42.3 0.0 copy-start.2
  42.3 3.0 %copy-done.2 = bf16[3584,1024]{1,0:T(8,128)(2,1)} copy-done((bf16[3584,1024]{1,0:T(8,128)(2,1)}, bf16[3584,1024]{1,0:T(8,128)(2,1)S(1)}, u32[]{:S(2)}) %copy-start.2) | copy-done | bytes 7340056
  45.3 0.0 copy-start.4
  45.3 2.9 %copy-done.4 = bf16[1024,3584]{1,0:T(8,128)(2,1)} copy-done((bf16[1024,3584]{1,0:T(8,128)(2,1)}, bf16[1024,3584]{1,0:T(8,128)(2,1)S(1)}, u32[]{:S(2)}) %copy-start.4) | copy-done | bytes 7340056
  48.2 0.0 all-to-all-done.1
  48.2 0.0 copy-start.1
  48.2 3.1 %copy-done.1 = bf16[3584,1024]{1,0:T(8,128)(2,1)S(1)} copy-done((bf16[3584,1024]{1,0:T(8,128)(2,1)S(1)}, bf16[3584,1024]{1,0:T(8,128)(2,1)}, u32[]{:S(2)}) %copy-start.1) | copy-done | bytes 7340056
  51.3 0.0 copy-start.3
  51.3 3.1 %copy-done.3 = bf16[3584,1024]{1,0:T(8,128)(2,1)S(1)} copy-done((bf16[3584,1024]{1,0:T(8,128)(2,1)S(1)}, bf16[3584,1024]{1,0:T(8,128)(2,1)}, u32[]{:S(2)}) %copy-start.3) | copy-done | bytes 7340056
  54.4 0.0 copy-start.5
  54.4 3.1 %copy-done.5 = bf16[1024,3584]{1,0:T(8,128)(2,1)S(1)} copy-done((bf16[1024,3584]{1,0:T(8,128)(2,1)S(1)}, bf16[1024,3584]{1,0:T(8,128)(2,1)}, u32[]{:S(2)}) %copy-start.5) | copy-done | bytes 7340056
  57.5 5.1 %shard_map.114.mine = f32[32,5120]{1,0:T(8,128)S(1)} custom-call(bf16[192,896]{1,0:T(8,128)(2,1)S(1)} %bitcast.24, bf16[192,896]{1,0:T(8,128)(2,1)S(1)} %bitcast.25, bf16[3584,1024]{1,0:T(8,128)(2,1)S(1)} %copy-done.1, bf16[3584,1024]{1,0:T(8,128)(2,1)S(1)} %copy-done.3, bf16[1024,3584]{1,0:T(8,128)(2,1)S(1)} %copy-done.5), custom_call_target="tpu_custom_call" | custom-call | flops 5637144576 | bytes 22020096 | tf_op jit(solution)/shard_map/pallas_call | solution.py:188
  62.6 1.0 %collective-permute-start.3 = (f32[32,5120]{1,0:T(8,128)S(1)}, f32[32,5120]{1,0:T(8,128)S(1)}, u32[]{:S(2)}, u32[]{:S(2)}) collective-permute-start(f32[32,5120]{1,0:T(8,128)S(1)} %shard_map.114.mine), channel_id=1, source_target_pairs={{0,8},{8,0},{16,24},{24,16},{1,9},{9,1},{17,25},{25,17},{2,10},{10... | collective-permute-start | bytes 1966088 | tf_op jit(solution)/shard_map/ppermute | solution.py:20
  63.6 1.7 %collective-permute-done.3.theirs = f32[32,5120]{1,0:T(8,128)S(1)} collective-permute-done((f32[32,5120]{1,0:T(8,128)S(1)}, f32[32,5120]{1,0:T(8,128)S(1)}, u32[]{:S(2)}, u32[]{:S(2)}) %collective-permute-start.3) | collective-permute-done | bytes 655392 | tf_op jit(solution)/shard_map/ppermute | solution.py:20
  65.3 7.0 %shard_map.115 = bf16[64,3584]{1,0:T(8,128)(2,1)} custom-call(f32[32,5120]{1,0:T(8,128)S(1)} %shard_map.114.mine, f32[32,5120]{1,0:T(8,128)S(1)} %collective-permute-done.3.theirs, bf16[3584,1024]{1,0:T(8,128)(2,1)S(1)} %copy-done.1, bf16[3584,1024]{1,0:T(8,128)(2,1)S(1)} %copy-done.3, bf16[1024,3584]{1,0:T(8,128)(2,1)S(1)} %copy-done.5), custom_call_target="tpu_custom_call" | custom-call | flops 5637144576 | bytes 22020096 | tf_op jit(solution)/shard_map/pallas_call | solution.py:188
  72.3 5.7 %all-to-all-start.2 = ((bf16[8,8,3584]{2,1,0:T(8,128)(2,1)}), bf16[8,8,3584]{2,1,0:T(8,128)(2,1)S(1)}, u32[]{:S(2)}, u32[]{:S(2)}) async-start(bf16[8,8,3584]{2,1,0:T(8,128)(2,1)} %bitcast.14), calls=%async_computation.2 | async-start | bytes 917504 | tf_op jit(solution)/shard_map/all_to_all | solution.py:257
  78.1 0.1 broadcast_select_fusion.15
  78.1 0.1 broadcast_select_fusion.14
  78.2 0.1 copy.18
  78.3 12.2 %all-to-all-done.2 = bf16[8,8,3584]{2,1,0:T(8,128)(2,1)S(1)} async-done(((bf16[8,8,3584]{2,1,0:T(8,128)(2,1)}), bf16[8,8,3584]{2,1,0:T(8,128)(2,1)S(1)}, u32[]{:S(2)}, u32[]{:S(2)}) %all-to-all-start.2) | async-done | bytes 458784 | tf_op jit(solution)/shard_map/all_to_all | solution.py:257
  90.5 0.2 multiply_reduce_fusion
  90.7 0.1 broadcast_select_fusion.5
  90.7 1.7 %collective-permute-start.4 = (bf16[4,3584]{1,0:T(4,128)(2,1)S(1)}, bf16[4,3584]{1,0:T(4,128)(2,1)S(1)}, u32[]{:S(2)}, u32[]{:S(2)}) collective-permute-start(bf16[4,3584]{1,0:T(4,128)(2,1)S(1)} %get-tuple-element.17), channel_id=1, source_target_pairs={{0,8},{8,0},{16,24},{24,16},{1,9},{9,1},{17,25},{25,17},{2,10},{10... | collective-permute-start | bytes 86024 | tf_op jit(solution)/shard_map/ppermute | solution.py:20
  92.4 0.9 collective-permute-done.4
  93.3 0.7 slice_bitcast_fusion
  (24 shorter events, 0.4 us)
Async XLA Ops:
  3.3 4.6 %collective-permute-start = (bf16[4,3712]{1,0:T(4,128)(2,1)S(1)}, bf16[4,3712]{1,0:T(4,128)(2,1)S(1)}, u32[]{:S(2)}, u32[]{:S(2)}) collective-permute-start(bf16[4,3712]{1,0:T(4,128)(2,1)S(1)} %pad_maximum_fusion.3), channel_id=1, source_target_pairs={{0,8},{8,0},{16,24},{24,16},{1,9},{9,1},{17,25},{25,17},{2,10},{10... | collective-permute-start | bytes 89096 | tf_op jit(solution)/shard_map/ppermute | solution.py:20
  3.4 6.3 %collective-permute-start.1 = (bf16[4,7296]{1,0:T(4,128)(2,1)S(1)}, bf16[4,7296]{1,0:T(4,128)(2,1)S(1)}, u32[]{:S(2)}, u32[]{:S(2)}) collective-permute-start(bf16[4,7296]{1,0:T(4,128)(2,1)S(1)} %get-tuple-element.14), channel_id=1, source_target_pairs={{8,16},{16,8},{9,17},{17,9},{10,18},{18,10},{11,19},{19,11},{12,20... | collective-permute-start | bytes 175112 | tf_op jit(solution)/shard_map/ppermute | solution.py:25
  9.8 7.1 %collective-permute-start.2 = (bf16[4,3712]{1,0:T(4,128)(2,1)S(1)}, bf16[4,3712]{1,0:T(4,128)(2,1)S(1)}, u32[]{:S(2)}, u32[]{:S(2)}) collective-permute-start(bf16[4,3712]{1,0:T(4,128)(2,1)S(1)} %pad_maximum_fusion.4), channel_id=1, source_target_pairs={{0,8},{8,0},{16,24},{24,16},{1,9},{9,1},{17,25},{25,17},{2,10},{10... | collective-permute-start | bytes 89096 | tf_op jit(solution)/shard_map/ppermute | solution.py:20
  10.7 14.8 %all-to-all-start = ((bf16[8,24,896]{2,1,0:T(8,128)(2,1)}), bf16[8,24,896]{2,1,0:T(8,128)(2,1)S(1)}, u32[]{:S(2)}, u32[]{:S(2)}) async-start(bf16[8,24,896]{2,1,0:T(8,128)(2,1)} %broadcast_in_dim.56), calls=%async_computation | async-start | bytes 688128 | tf_op jit(solution)/shard_map/all_to_all | solution.py:69
  26.3 21.9 %all-to-all-start.1 = ((bf16[8,24,896]{2,1,0:T(8,128)(2,1)}), bf16[8,24,896]{2,1,0:T(8,128)(2,1)S(1)}, u32[]{:S(2)}, u32[]{:S(2)}) async-start(bf16[8,24,896]{2,1,0:T(8,128)(2,1)} %broadcast_in_dim.58), calls=%async_computation.1 | async-start | bytes 688128 | tf_op jit(solution)/shard_map/all_to_all | solution.py:69
  39.3 3.0 %copy-start = (bf16[3584,1024]{1,0:T(8,128)(2,1)}, bf16[3584,1024]{1,0:T(8,128)(2,1)S(1)}, u32[]{:S(2)}) copy-start(bf16[3584,1024]{1,0:T(8,128)(2,1)S(1)} %get-tuple-element.7.g) | copy-start | bytes 22020100
  42.3 3.0 %copy-start.2 = (bf16[3584,1024]{1,0:T(8,128)(2,1)}, bf16[3584,1024]{1,0:T(8,128)(2,1)S(1)}, u32[]{:S(2)}) copy-start(bf16[3584,1024]{1,0:T(8,128)(2,1)S(1)} %get-tuple-element.8.u) | copy-start | bytes 22020100
  45.3 2.9 %copy-start.4 = (bf16[1024,3584]{1,0:T(8,128)(2,1)}, bf16[1024,3584]{1,0:T(8,128)(2,1)S(1)}, u32[]{:S(2)}) copy-start(bf16[1024,3584]{1,0:T(8,128)(2,1)S(1)} %get-tuple-element.9.d) | copy-start | bytes 22020100
  48.2 3.1 %copy-start.1 = (bf16[3584,1024]{1,0:T(8,128)(2,1)S(1)}, bf16[3584,1024]{1,0:T(8,128)(2,1)}, u32[]{:S(2)}) copy-start(bf16[3584,1024]{1,0:T(8,128)(2,1)} %copy-done) | copy-start | bytes 22020100
  51.3 3.1 %copy-start.3 = (bf16[3584,1024]{1,0:T(8,128)(2,1)S(1)}, bf16[3584,1024]{1,0:T(8,128)(2,1)}, u32[]{:S(2)}) copy-start(bf16[3584,1024]{1,0:T(8,128)(2,1)} %copy-done.2) | copy-start | bytes 22020100
  54.4 3.1 %copy-start.5 = (bf16[1024,3584]{1,0:T(8,128)(2,1)S(1)}, bf16[1024,3584]{1,0:T(8,128)(2,1)}, u32[]{:S(2)}) copy-start(bf16[1024,3584]{1,0:T(8,128)(2,1)} %copy-done.4) | copy-start | bytes 22020100
  62.6 2.7 %collective-permute-start.3 = (f32[32,5120]{1,0:T(8,128)S(1)}, f32[32,5120]{1,0:T(8,128)S(1)}, u32[]{:S(2)}, u32[]{:S(2)}) collective-permute-start(f32[32,5120]{1,0:T(8,128)S(1)} %shard_map.114.mine), channel_id=1, source_target_pairs={{0,8},{8,0},{16,24},{24,16},{1,9},{9,1},{17,25},{25,17},{2,10},{10... | collective-permute-start | bytes 1966088 | tf_op jit(solution)/shard_map/ppermute | solution.py:20
  72.3 18.2 %all-to-all-start.2 = ((bf16[8,8,3584]{2,1,0:T(8,128)(2,1)}), bf16[8,8,3584]{2,1,0:T(8,128)(2,1)S(1)}, u32[]{:S(2)}, u32[]{:S(2)}) async-start(bf16[8,8,3584]{2,1,0:T(8,128)(2,1)} %bitcast.14), calls=%async_computation.2 | async-start | bytes 917504 | tf_op jit(solution)/shard_map/all_to_all | solution.py:257
  90.7 2.5 %collective-permute-start.4 = (bf16[4,3584]{1,0:T(4,128)(2,1)S(1)}, bf16[4,3584]{1,0:T(4,128)(2,1)S(1)}, u32[]{:S(2)}, u32[]{:S(2)}) collective-permute-start(bf16[4,3584]{1,0:T(4,128)(2,1)S(1)} %get-tuple-element.17), channel_id=1, source_target_pairs={{0,8},{8,0},{16,24},{24,16},{1,9},{9,1},{17,25},{25,17},{2,10},{10... | collective-permute-start | bytes 86024 | tf_op jit(solution)/shard_map/ppermute | solution.py:20

commit v3 on v2

v3 whole, which is shorter than its diff:
```python
import functools

import jax
import jax.numpy as jnp
from jax import lax
from jax.experimental import pallas as pl
from jax.experimental.pallas import tpu as pltpu
from jax.sharding import PartitionSpec as P

GROUPS = 4
PARTS = 4
BATCH = 8
F32 = jnp.float32
BF16 = jnp.bfloat16


def swap_cores(block):
    sections = range(lax.axis_size("section"))
    return lax.ppermute(block, "section", [(i, i ^ 1) for i in sections])


def expert_weights(routes, probs):
    named = routes[:, :, None] == jnp.arange(GROUPS, dtype=jnp.int32)
    return jnp.sum(jnp.where(named, probs[:, :, None], 0.0), axis=1)


def by_section(mine, theirs, core):
    return jnp.where(core == 0, mine, theirs), jnp.where(core == 0, theirs, mine)


def swap_ranks(block, bit):
    ranks = range(lax.axis_size("expert"))
    return lax.ppermute(block, "expert", [(i, i ^ bit) for i in ranks])


def to_next_chips(fwd, bwd, bit):
    sections, ranks = lax.axis_size("section"), lax.axis_size("expert")

    def move(block, pairs):
        route = [(a * ranks + e, b * ranks + (e ^ bit)) for a, b in pairs for e in range(ranks)]
        return lax.ppermute(block, ("section", "expert"), route)

    up = [(i, i + 2) for i in range(sections - 2)]
    down = [(b, a) for a, b in up]
    if sections != 4:
        return jnp.concatenate([move(fwd, up), move(bwd, down)])
    first = lax.axis_index("section") < 2
    rows = bwd.shape[0]
    padded = jnp.pad(fwd, ((0, rows - fwd.shape[0]), (0, 0)))
    got = move(jnp.where(first, padded, bwd), up + down)
    none = jnp.zeros_like(got)
    return jnp.concatenate(
        [jnp.where(first, none, got)[: fwd.shape[0]], jnp.where(first, got, none)]
    )


def folded(block):
    rows, width = block.shape
    block = block.reshape(rows, PARTS, width // PARTS).transpose(1, 0, 2)
    return block.reshape(rows * PARTS, width // PARTS)


def dot(a, b):
    return jnp.dot(a, b, preferred_element_type=F32)


def one_hot(want, src):
    return jnp.where(want == src, 1.0, 0.0).astype(BF16)


def gathered_order():
    count = 2 * BATCH * PARTS * 6
    out = lax.broadcasted_iota(jnp.int32, (count, count), 0)
    src = lax.broadcasted_iota(jnp.int32, (count, count), 1)
    part, rest = lax.div(out, 12 * BATCH), lax.rem(out, 12 * BATCH)
    kind, rest = lax.div(rest, 4 * BATCH), lax.rem(rest, 4 * BATCH)
    row = jnp.where(kind == 0, part * 2, part * 4 + kind * 2 + 2 * PARTS - 2)
    want = lax.div(rest, 2) * (6 * PARTS) + row + lax.rem(rest, 2)
    return one_hot(want, src)


def returned_order(ranks, me):
    count = ranks * 8
    out = lax.broadcasted_iota(jnp.int32, (count, count), 0)
    src = lax.broadcasted_iota(jnp.int32, (count, count), 1)
    apart = lax.bitwise_xor(lax.div(out, 8), jnp.full((count, count), me, jnp.int32))
    place = jnp.zeros_like(out)
    for _ in range(ranks.bit_length() - 1):
        place = place * 2 + lax.rem(apart, 2)
        apart = lax.div(apart, 2)
    kind = lax.div(lax.rem(out, 8), 4)
    want = kind * (4 * ranks) + place * 4 + lax.rem(out, 4)
    return one_hot(want, src)


def fetch_kernel(steps, axis, place, weight, earlier, held, turned, zero, sems):
    size = held.shape[axis] // steps
    base = place[0] * held.shape[axis]

    def at(start):
        rows = pl.ds(pl.multiple_of(start, 128), size)
        return rows if axis == 0 else (slice(None), rows)

    copies = [
        pltpu.make_async_copy(
            weight.at[at(base + i * size)], held.at[at(i * size)], sems.at[i]
        )
        for i in range(steps)
    ]
    for copy in copies:
        copy.start()
    for i, copy in enumerate(copies):
        copy.wait()
        here = slice(i * size, (i + 1) * size)
        if axis == 0:
            turned[:, here] = held[here, :].T
        else:
            turned[here, :] = held[:, here].T
    zero[...] = jnp.zeros_like(zero)


def fetch(place, weight, axis, earlier, like):
    steps = 4
    shape = list(weight.shape)
    shape[axis] //= 2
    return pl.pallas_call(
        functools.partial(fetch_kernel, steps, axis),
        in_specs=[
            pl.BlockSpec(memory_space=pltpu.SMEM),
            pl.BlockSpec(memory_space=pltpu.HBM),
            pl.BlockSpec(memory_space=pl.ANY),
        ],
        out_specs=[pl.BlockSpec(memory_space=pltpu.VMEM)] * 3,
        out_shape=[
            pltpu.VMEM(tuple(shape), BF16),
            pltpu.VMEM(tuple(shape[::-1]), BF16),
            jax.ShapeDtypeStruct(like, BF16),
        ],
        scratch_shapes=[pltpu.SemaphoreType.DMA((steps,))],
        compiler_params=pltpu.CompilerParams(vmem_limit_bytes=2**20),
        cost_estimate=pl.CostEstimate(
            flops=0, bytes_accessed=weight.size * 4, transcendentals=0
        ),
    )(place, pltpu.with_memory_space_constraint(weight, pltpu.HBM), earlier)


def up_kernel(ranks, first, second, third, fourth, g, u, d_t, out):
    hid = g.shape[1]
    n = 4 * BATCH
    piece = first.shape[1]
    blocks = jnp.concatenate([first[...], second[...], third[...], fourth[...]])
    order = gathered_order()
    count = order.shape[0]
    batches = ranks // BATCH
    sorted_rows = [
        dot(order, blocks[i * count : (i + 1) * count]).astype(BF16) for i in range(batches)
    ]
    a, b, dh = 0.0, 0.0, 0.0
    for part in range(PARTS):
        at = part * 3 * n
        cols = slice(part * piece, (part + 1) * piece)
        kinds = [
            jnp.concatenate([rows[at + k * n : at + (k + 1) * n] for rows in sorted_rows])
            for k in range(3)
        ]
        rows = jnp.concatenate(kinds[:2])
        a += dot(rows, g[cols, :])
        b += dot(rows, u[cols, :])
        dh += dot(kinds[2], d_t[cols, :])
    n = n * batches
    out[:, :hid] = a[:n]
    out[:, hid : 2 * hid] = b[:n]
    out[:, 2 * hid : 3 * hid] = a[n:]
    out[:, 3 * hid : 4 * hid] = b[n:]
    out[:, 4 * hid :] = dh


def down_kernel(ranks, place, mine, theirs, g_t, u_t, d, out):
    hid = d.shape[0]
    a = mine[:, :hid] + theirs[:, :hid]
    b = mine[:, hid : 2 * hid] + theirs[:, hid : 2 * hid]
    h = (a * jax.nn.sigmoid(a) * b).astype(BF16)
    a = mine[:, 2 * hid : 3 * hid] + theirs[:, 2 * hid : 3 * hid]
    b = mine[:, 3 * hid : 4 * hid] + theirs[:, 3 * hid : 4 * hid]
    dh = mine[:, 4 * hid :] + theirs[:, 4 * hid :]
    s = jax.nn.sigmoid(a)
    da = (dh * b * s * (1.0 + a * (1.0 - s))).astype(BF16)
    du = (dh * a * s).astype(BF16)
    order = returned_order(ranks, place[1])
    piece = out.shape[1] // PARTS
    for part in range(PARTS):
        cols = slice(part * piece, (part + 1) * piece)
        y = dot(h, d[:, cols])
        dx = dot(da, g_t[:, cols]) + dot(du, u_t[:, cols])
        rows = jnp.concatenate([y.astype(BF16), dx.astype(BF16)])
        out[:, cols] = dot(order, rows).astype(BF16)


def on_core(kernel, ranks, scalars, operands, results, weight):
    return pl.pallas_call(
        kernel,
        in_specs=[pl.BlockSpec(memory_space=pltpu.SMEM)] * len(scalars)
        + [pl.BlockSpec(memory_space=pltpu.VMEM)] * len(operands),
        out_specs=[pl.BlockSpec(memory_space=pltpu.VMEM)] * len(results),
        out_shape=[jax.ShapeDtypeStruct(*result) for result in results],
        compiler_params=pltpu.CompilerParams(vmem_limit_bytes=ranks * 2**18),
        cost_estimate=pl.CostEstimate(
            flops=6 * weight.size * 256, bytes_accessed=6 * weight.size, transcendentals=0
        ),
    )(*scalars, *[pltpu.with_memory_space_constraint(x, pltpu.VMEM) for x in operands])


def after(value, other):
    return lax.optimization_barrier((value, other))[0]


def local(
    fwd_tokens,
    fwd_routes,
    fwd_probs,
    bwd_tokens,
    bwd_routes,
    bwd_probs,
    bwd_grads,
    w_gate,
    w_up,
    w_down,
):
    ranks = lax.axis_size("expert")
    shards = ranks // GROUPS
    width = fwd_tokens.shape[2]
    half = width // 2
    hid = w_gate.shape[1]
    core = lax.axis_index("section") % 2
    place = jnp.stack([core, lax.axis_index("expert")]).astype(jnp.int32)

    rows = jnp.concatenate([fwd_tokens[0], bwd_tokens[0], bwd_grads[0]])
    first, second = rows[:, :half], rows[:, half:]
    keep, send = by_section(first, second, core)
    even, odd = by_section(keep, swap_cores(send), core)

    near = jnp.concatenate([folded(even[:2]), folded(odd[2:])])
    far_fwd, far_bwd = folded(odd[:2]), folded(even[2:])
    top = ranks // 2
    far = to_next_chips(far_fwd, far_bwd, 0)
    far_top = to_next_chips(far_fwd, far_bwd, top)
    blocks = jnp.concatenate([near, far, swap_ranks(near, top), far_top])
    g, g_t, zero = fetch(place, w_gate, 0, near, blocks.shape)
    blocks = blocks + zero
    bit = top // 2
    while bit > 2:
        blocks = jnp.concatenate([blocks, swap_ranks(blocks, bit)])
        bit //= 2
    second = swap_ranks(blocks, 2)
    third = swap_ranks(blocks, 1)
    u, u_t, zero = fetch(place, w_up, 0, blocks, second.shape)
    second = second + zero
    fourth = swap_ranks(second, 1)
    d, d_t, _ = fetch(place, w_down, 1, second, (16, 128))

    (mine,) = on_core(
        functools.partial(up_kernel, ranks),
        ranks,
        (),
        (blocks, second, third, fourth, g, u, d_t),
        [((4 * ranks, 5 * hid), F32)],
        g,
    )
    (out,) = on_core(
        functools.partial(down_kernel, ranks),
        ranks,
        (place,),
        (mine, swap_cores(mine), g_t, u_t, d),
        [((8 * ranks, half), BF16)],
        g,
    )
    back = lax.all_to_all(
        out.reshape(ranks, 8, half), "expert", split_axis=0, concat_axis=0, tiled=True
    )

    weights = jnp.concatenate(
        [
            expert_weights(after(fwd_routes[0], out), fwd_probs[0]),
            expert_weights(after(bwd_routes[0], out), bwd_probs[0]),
        ]
    )
    even, odd = by_section(weights, swap_cores(weights), core)
    far = to_next_chips(odd[:2], even[2:], 0)
    weights = jnp.concatenate([even[:2], far[:2], odd[2:], far[2:]]).T[:, None]
    weights = jnp.broadcast_to(weights, (GROUPS, shards, 8)).reshape(ranks, 8, 1)

    total = jnp.sum(back.astype(F32) * weights, axis=0).astype(BF16)
    first = jnp.concatenate([total[2:4], total[4:6]])
    second = jnp.concatenate([total[:2], total[6:]])
    own = jnp.where(core == 0, first, second)
    other = swap_cores(jnp.where(core == 0, second, first))
    whole = jnp.where(
        core == 0,
        jnp.concatenate([own, other], axis=1),
        jnp.concatenate([other, own], axis=1),
    )
    return (whole[None, :2], whole[None, 2:])


def solution(mesh):
    return jax.shard_map(
        local,
        mesh=mesh,
        in_specs=(
            P("section", "expert", None),
            P("section", "expert", None),
            P("section", "expert", None),
            P("section", "expert", None),
            P("section", "expert", None),
            P("section", "expert", None),
            P("section", "expert", None),
            P(None, "expert"),
            P(None, "expert"),
            P("expert", None),
        ),
        out_specs=(P("section", "expert", None), P("section", "expert", None)),
        check_vma=False,
    )
```

time: 94.9 us -> 58 us (0.61)
  local copies, waits for them, and re-layouts: 20.5 us -> 0.94 us
  waiting for transfers between devices: 25 us -> 13.9 us
  starting transfers between devices: 24.8 us -> 18.2 us
  Pallas kernels: 19.6 us -> 22 us
  other arithmetic: 3.24 us -> 1.53 us
    unnamed x12 -> x10, local copies, waits for them, and re-layouts: 18.2 us -> 0.03 us
    all_to_all x3 -> x1, starting transfers between devices: 17.5 us -> 4.26 us  [local(): lax.all_to_all(out.reshape(ranks, 8, half), 'expert', split_axis=0, conca...]
    all_to_all x3 -> x1, waiting for transfers between devices: 20.7 us -> 7.84 us  [local(): lax.all_to_all(out.reshape(ranks, 8, half), 'expert', split_axis=0, conca...]
    ppermute x1 -> x7, starting transfers between devices: 4.47 us -> 9.06 us  [the longest x3 5.99 us: move(): return lax.ppermute(block, ('section', 'expert'), route)]
    pallas_call x3 -> x5, Pallas kernels: 19.6 us -> 22 us  [the longest x3 13.4 us: fetch(): pl.pallas_call(functools.partial(fetch_kernel, steps, axis), in_specs=[pl...]
    ppermute x4, starting transfers between devices: 2.88 us -> 4.85 us  [swap_cores(): return lax.ppermute(block, 'section', [(i, i ^ 1) for i in sections])]
    ppermute x4, waiting for transfers between devices: 2.58 us -> 4.51 us  [swap_cores(): return lax.ppermute(block, 'section', [(i, i ^ 1) for i in sections])]
    broadcast_in_dim x4 -> x0, local copies, waits for them, and re-layouts: 1.57 us -> none  [to_all(): spread = jnp.broadcast_to(block, (ranks,) + block.shape[1:])]
  transfers between devices with their start and end apart: 8 -> 12, of which waited for: 5 -> 6; matrix products, arithmetic and copies ran while one was open for 1% -> 1% of each run, Pallas kernels for 8% -> 23%
where the time goes in v3:
time: 58 us; the launch traced here: 57.4 us
  Pallas kernels  22 us (38%)
  starting transfers between devices  18.2 us (31%)
  waiting for transfers between devices  13.9 us (24%)
  other arithmetic  1.53 us (3%)
  local copies, waits for them, and re-layouts  0.94 us (2%)
  between operations  0.89 us (2%)
    pallas_call x3, Pallas kernels, fetch(): pl.pallas_call(functools.partial(fetch_kernel, steps, axis), in_specs=[pl...  13.4 us
    pallas_call x2, Pallas kernels, on_core(): pl.pallas_call(kernel, in_specs=[pl.BlockSpec(memory_space=pltpu.SMEM)] *...  8.68 us
    all_to_all x1, waiting for transfers between devices, local(): lax.all_to_all(out.reshape(ranks, 8, half), 'expert', split_axis=0, conca...  7.84 us
    ppermute x3, starting transfers between devices, move(): return lax.ppermute(block, ('section', 'expert'), route)  5.99 us
    ppermute x4, starting transfers between devices, swap_cores(): return lax.ppermute(block, 'section', [(i, i ^ 1) for i in sections])  4.85 us
    ppermute x4, waiting for transfers between devices, swap_cores(): return lax.ppermute(block, 'section', [(i, i ^ 1) for i in sections])  4.51 us
    all_to_all x1, starting transfers between devices, local(): lax.all_to_all(out.reshape(ranks, 8, half), 'expert', split_axis=0, conca...  4.26 us
    ppermute x4, starting transfers between devices, swap_ranks(): return lax.ppermute(block, 'expert', [(i, i ^ bit) for i in ranks])  3.06 us
  transfers between devices with their start and end apart: 12, of which 6 were waited for; matrix products, arithmetic and copies ran while one was open for 1% of the time, Pallas kernels for 23%

profile of v3, /device:TPU:1, one launch (start us, length us, event | category | flops | bytes accessed | tf_op | source)
XLA Modules:
  0.0 57.4 jit_solution(17100535890586320307)
XLA Ops:
  0.6 0.9 %pad_maximum_fusion = bf16[6,7168]{1,0:T(8,128)(2,1)S(1)} fusion(bf16[2,7168]{1,0:T(2,128)(2,1)} %bitcast.33, bf16[2,7168]{1,0:T(2,128)(2,1)} %bitcast.34, bf16[2,7168]{1,0:T(2,128)(2,1)} %bitcast.35), kind=kLoop, calls=%fused_computation.1 | loop fusion | flops 258048 | bytes 172032 | tf_op jit(solution)/shard_map/concatenate | solution.py:237
  1.5 0.1 collective-permute-start
  1.7 0.1 pad_add_fusion.place
  1.7 1.1 %collective-permute-done = bf16[6,3584]{1,0:T(8,128)(2,1)S(1)} collective-permute-done((bf16[6,3584]{1,0:T(8,128)(2,1)S(1)}, bf16[6,3584]{1,0:T(8,128)(2,1)S(1)}, u32[]{:S(2)}, u32[]{:S(2)}) %collective-permute-start) | collective-permute-done | bytes 43040 | tf_op jit(solution)/shard_map/ppermute | solution.py:19
  3.0 4.5 %collective-permute-start.3 = (bf16[16,896]{1,0:T(8,128)(2,1)S(1)}, bf16[16,896]{1,0:T(8,128)(2,1)S(1)}, u32[]{:S(2)}, u32[]{:S(2)}) collective-permute-start(bf16[16,896]{1,0:T(8,128)(2,1)S(1)} %pad_select_fusion), channel_id=1, source_target_pairs={{0,20},{1,21},{2,22},{3,23},{4,16},{5,17},{6,18},{7,19},{8,28},{9,... | collective-permute-start | bytes 86024 | tf_op jit(solution)/shard_map/ppermute | solution.py:41
  7.5 0.3 collective-permute-start.1
  7.8 0.2 collective-permute-start.2
  8.0 4.3 %shard_map.113 = (bf16[3584,1024]{1,0:T(8,128)(2,1)S(1)}, bf16[1024,3584]{1,0:T(8,128)(2,1)S(1)}, bf16[96,896]{1,0:T(8,128)(2,1)S(1)}) custom-call(s32[2]{0:T(128)S(1)} %pad_add_fusion.place, bf16[7168,1024]{1,0:T(8,128)(2,1)} %weight.3, bf16[24,896]{1,0:T(8,128)(2,1)S(1)} %get-tuple-element.30.earlier), custom_call_target="tpu_custom_call" | custom-call | bytes 29360128 | tf_op jit(solution)/shard_map/pallas_call | solution.py:126
  12.2 0.0 collective-permute-done.1
  12.3 0.0 collective-permute-done.2
  12.3 0.0 collective-permute-done.3
  12.4 1.4 %collective-permute-start.4 = (bf16[96,896]{1,0:T(8,128)(2,1)S(1)}, bf16[96,896]{1,0:T(8,128)(2,1)S(1)}, u32[]{:S(2)}, u32[]{:S(2)}) collective-permute-start(bf16[96,896]{1,0:T(8,128)(2,1)S(1)} %add.13.earlier.first), channel_id=1, source_target_pairs={{0,2},{1,3},{2,0},{3,1},{4,6},{5,7},{6,4},{7,5},{8,10},{9,11},{10,... | collective-permute-start | bytes 516104 | tf_op jit(solution)/shard_map/ppermute | solution.py:33
  13.8 1.2 %collective-permute-start.5 = (bf16[96,896]{1,0:T(8,128)(2,1)S(1)}, bf16[96,896]{1,0:T(8,128)(2,1)S(1)}, u32[]{:S(2)}, u32[]{:S(2)}) collective-permute-start(bf16[96,896]{1,0:T(8,128)(2,1)S(1)} %add.13.earlier.first), channel_id=1, source_target_pairs={{0,1},{1,0},{2,3},{3,2},{4,5},{5,4},{6,7},{7,6},{8,9},{9,8},{10,11... | collective-permute-start | bytes 516104 | tf_op jit(solution)/shard_map/ppermute | solution.py:33
  15.0 4.3 %shard_map.114 = (bf16[3584,1024]{1,0:T(8,128)(2,1)S(1)}, bf16[1024,3584]{1,0:T(8,128)(2,1)S(1)}, bf16[96,896]{1,0:T(8,128)(2,1)S(1)}) custom-call(s32[2]{0:T(128)S(1)} %pad_add_fusion.place, bf16[7168,1024]{1,0:T(8,128)(2,1)} %weight.4, bf16[96,896]{1,0:T(8,128)(2,1)S(1)} %add.13.earlier.first), custom_call_target="tpu_custom_call" | custom-call | bytes 29360128 | tf_op jit(solution)/shard_map/pallas_call | solution.py:126
  19.3 0.0 collective-permute-done.4
  19.3 0.3 collective-permute-start.6
  19.6 4.8 %shard_map.115 = (bf16[1024,3584]{1,0:T(8,128)(2,1)S(1)}, bf16[3584,1024]{1,0:T(8,128)(2,1)S(1)}, bf16[16,128]{1,0:T(8,128)(2,1)}) custom-call(s32[2]{0:T(128)S(1)} %pad_add_fusion.place, bf16[1024,7168]{1,0:T(8,128)(2,1)} %weight.5, bf16[96,896]{1,0:T(8,128)(2,1)S(1)} %add.14.earlier.second), custom_call_target="tpu_custom_call" | custom-call | bytes 29360128 | tf_op jit(solution)/shard_map/pallas_call | solution.py:126
  24.5 0.0 collective-permute-done.5.third
  24.5 0.0 collective-permute-done.6.fourth
  24.5 3.6 %shard_map.116.mine = f32[32,5120]{1,0:T(8,128)S(1)} custom-call(bf16[96,896]{1,0:T(8,128)(2,1)S(1)} %add.13.earlier.first, bf16[96,896]{1,0:T(8,128)(2,1)S(1)} %add.14.earlier.second, bf16[96,896]{1,0:T(8,128)(2,1)S(1)} %collective-permute-done.5.third, bf16[96,896]{1,0:T(8,128)(2,1)S(1)} %collective-permute-done.6.fourth, ...), custom_call_target="tpu_custom_call" | custom-call | flops 5637144576 | bytes 22020096 | tf_op jit(solution)/shard_map/pallas_call | solution.py:200
  28.1 2.3 %collective-permute-start.7 = (f32[32,5120]{1,0:T(8,128)S(1)}, f32[32,5120]{1,0:T(8,128)S(1)}, u32[]{:S(2)}, u32[]{:S(2)}) collective-permute-start(f32[32,5120]{1,0:T(8,128)S(1)} %shard_map.116.mine), channel_id=1, source_target_pairs={{0,8},{8,0},{16,24},{24,16},{1,9},{9,1},{17,25},{25,17},{2,10},{10... | collective-permute-start | bytes 1966088 | tf_op jit(solution)/shard_map/ppermute | solution.py:19
  30.4 1.7 %collective-permute-done.7.theirs = f32[32,5120]{1,0:T(8,128)S(1)} collective-permute-done((f32[32,5120]{1,0:T(8,128)S(1)}, f32[32,5120]{1,0:T(8,128)S(1)}, u32[]{:S(2)}, u32[]{:S(2)}) %collective-permute-start.7) | collective-permute-done | bytes 655392 | tf_op jit(solution)/shard_map/ppermute | solution.py:19
  32.1 0.0 copy-start
  32.2 0.0 copy-start.1
  32.2 0.0 copy-start.2
  32.2 0.0 copy-start.3
  32.2 5.1 %shard_map.117 = bf16[64,3584]{1,0:T(8,128)(2,1)} custom-call(s32[2]{0:T(128)S(1)} %pad_add_fusion.place, f32[32,5120]{1,0:T(8,128)S(1)} %shard_map.116.mine, f32[32,5120]{1,0:T(8,128)S(1)} %collective-permute-done.7.theirs, bf16[1024,3584]{1,0:T(8,128)(2,1)S(1)} %get-tuple-element.17.g_t, bf16[1024,3584]{1,0:T(8,128)(2,1)S(1)} %get-tuple-element.18.u_t, ...), custom_call_target="tpu_custom_call" | custom-call | flops 5637144576 | bytes 22020096 | tf_op jit(solution)/shard_map/pallas_call | solution.py:200
  37.2 4.3 %all-to-all-start = ((bf16[8,8,3584]{2,1,0:T(8,128)(2,1)}), bf16[8,8,3584]{2,1,0:T(8,128)(2,1)S(1)}, u32[]{:S(2)}, u32[]{:S(2)}) async-start(bf16[8,8,3584]{2,1,0:T(8,128)(2,1)} %bitcast.13), calls=%async_computation | async-start | bytes 917504 | tf_op jit(solution)/shard_map/all_to_all | solution.py:277
  41.5 0.0 copy-done
  41.5 0.0 copy-done.1
  41.5 0.0 copy-done.2
  41.5 0.0 copy-done.3
  41.5 0.1 fusion
  41.6 0.7 %collective-permute-start.8 = (f32[4,4]{1,0:T(4,128)S(1)}, f32[4,4]{1,0:T(4,128)S(1)}, u32[]{:S(2)}, u32[]{:S(2)}) collective-permute-start(f32[4,4]{1,0:T(4,128)S(1)} %pad_maximum_fusion.2), channel_id=1, source_target_pairs={{0,8},{8,0},{16,24},{24,16},{1,9},{9,1},{17,25},{25,17},{2,10},{10... | collective-permute-start | bytes 200 | tf_op jit(solution)/shard_map/ppermute | solution.py:19
  42.4 0.8 %collective-permute-done.8 = f32[4,4]{1,0:T(4,128)S(1)} collective-permute-done((f32[4,4]{1,0:T(4,128)S(1)}, f32[4,4]{1,0:T(4,128)S(1)}, u32[]{:S(2)}, u32[]{:S(2)}) %collective-permute-start.8) | collective-permute-done | bytes 96 | tf_op jit(solution)/shard_map/ppermute | solution.py:19
  43.2 1.3 %collective-permute-start.9 = (f32[2,4]{1,0:T(2,128)S(1)}, f32[2,4]{1,0:T(2,128)S(1)}, u32[]{:S(2)}, u32[]{:S(2)}) collective-permute-start(f32[2,4]{1,0:T(2,128)S(1)} %get-tuple-element.37), channel_id=1, source_target_pairs={{0,16},{1,17},{2,18},{3,19},{4,20},{5,21},{6,22},{7,23},{8,24},{9,... | collective-permute-start | bytes 104 | tf_op jit(solution)/shard_map/ppermute | solution.py:41
  44.5 1.5 %collective-permute-done.9 = f32[2,4]{1,0:T(2,128)S(1)} collective-permute-done((f32[2,4]{1,0:T(2,128)S(1)}, f32[2,4]{1,0:T(2,128)S(1)}, u32[]{:S(2)}, u32[]{:S(2)}) %collective-permute-start.9) | collective-permute-done | bytes 64 | tf_op jit(solution)/shard_map/ppermute | solution.py:41
  46.0 0.1 copy.20
  46.1 7.8 %all-to-all-done = bf16[8,8,3584]{2,1,0:T(8,128)(2,1)S(1)} async-done(((bf16[8,8,3584]{2,1,0:T(8,128)(2,1)}), bf16[8,8,3584]{2,1,0:T(8,128)(2,1)S(1)}, u32[]{:S(2)}, u32[]{:S(2)}) %all-to-all-start) | async-done | bytes 458784 | tf_op jit(solution)/shard_map/all_to_all | solution.py:277
  53.9 0.2 multiply_reduce_fusion
  54.1 0.1 broadcast_select_fusion.5
  54.2 1.7 %collective-permute-start.10 = (bf16[4,3584]{1,0:T(4,128)(2,1)S(1)}, bf16[4,3584]{1,0:T(4,128)(2,1)S(1)}, u32[]{:S(2)}, u32[]{:S(2)}) collective-permute-start(bf16[4,3584]{1,0:T(4,128)(2,1)S(1)} %get-tuple-element.25), channel_id=1, source_target_pairs={{0,8},{8,0},{16,24},{24,16},{1,9},{9,1},{17,25},{25,17},{2,10},{10... | collective-permute-start | bytes 86024 | tf_op jit(solution)/shard_map/ppermute | solution.py:19
  55.9 0.9 %collective-permute-done.10 = bf16[4,3584]{1,0:T(4,128)(2,1)S(1)} collective-permute-done((bf16[4,3584]{1,0:T(4,128)(2,1)S(1)}, bf16[4,3584]{1,0:T(4,128)(2,1)S(1)}, u32[]{:S(2)}, u32[]{:S(2)}) %collective-permute-start.10) | collective-permute-done | bytes 28704 | tf_op jit(solution)/shard_map/ppermute | solution.py:19
  56.8 0.7 %slice_bitcast_fusion = (bf16[1,2,7168]{2,1,0:T(2,128)(2,1)}, bf16[1,2,7168]{2,1,0:T(2,128)(2,1)}) fusion(bf16[4,7168]{1,0:T(4,128)(2,1)S(1)} %maximum_select_fusion), kind=kLoop, calls=%fused_computation.7 | loop fusion | bytes 114688 | tf_op jit(solution)/shard_map/broadcast_in_dim | solution.py:302
  (28 shorter events, 0.4 us)
Async XLA Ops:
  1.5 1.3 %collective-permute-start = (bf16[6,3584]{1,0:T(8,128)(2,1)S(1)}, bf16[6,3584]{1,0:T(8,128)(2,1)S(1)}, u32[]{:S(2)}, u32[]{:S(2)}) collective-permute-start(bf16[6,3584]{1,0:T(8,128)(2,1)S(1)} %broadcast_select_fusion.2), channel_id=1, source_target_pairs={{0,8},{8,0},{16,24},{24,16},{1,9},{9,1},{17,25},{25,17},{2,10},{10... | collective-permute-start | bytes 129032 | tf_op jit(solution)/shard_map/ppermute | solution.py:19
  3.0 9.3 %collective-permute-start.3 = (bf16[16,896]{1,0:T(8,128)(2,1)S(1)}, bf16[16,896]{1,0:T(8,128)(2,1)S(1)}, u32[]{:S(2)}, u32[]{:S(2)}) collective-permute-start(bf16[16,896]{1,0:T(8,128)(2,1)S(1)} %pad_select_fusion), channel_id=1, source_target_pairs={{0,20},{1,21},{2,22},{3,23},{4,16},{5,17},{6,18},{7,19},{8,28},{9,... | collective-permute-start | bytes 86024 | tf_op jit(solution)/shard_map/ppermute | solution.py:41
  7.5 4.8 %collective-permute-start.1 = (bf16[16,896]{1,0:T(8,128)(2,1)S(1)}, bf16[16,896]{1,0:T(8,128)(2,1)S(1)}, u32[]{:S(2)}, u32[]{:S(2)}) collective-permute-start(bf16[16,896]{1,0:T(8,128)(2,1)S(1)} %pad_select_fusion), channel_id=1, source_target_pairs={{0,16},{1,17},{2,18},{3,19},{4,20},{5,21},{6,22},{7,23},{8,24},{9,... | collective-permute-start | bytes 86024 | tf_op jit(solution)/shard_map/ppermute | solution.py:41
  7.8 4.5 %collective-permute-start.2 = (bf16[24,896]{1,0:T(8,128)(2,1)S(1)}, bf16[24,896]{1,0:T(8,128)(2,1)S(1)}, u32[]{:S(2)}, u32[]{:S(2)}) collective-permute-start(bf16[24,896]{1,0:T(8,128)(2,1)S(1)} %get-tuple-element.30.earlier), channel_id=1, source_target_pairs={{0,4},{1,5},{2,6},{3,7},{4,0},{5,1},{6,2},{7,3},{8,12},{9,13},{10,... | collective-permute-start | bytes 129032 | tf_op jit(solution)/shard_map/ppermute | solution.py:33
  12.4 6.9 %collective-permute-start.4 = (bf16[96,896]{1,0:T(8,128)(2,1)S(1)}, bf16[96,896]{1,0:T(8,128)(2,1)S(1)}, u32[]{:S(2)}, u32[]{:S(2)}) collective-permute-start(bf16[96,896]{1,0:T(8,128)(2,1)S(1)} %add.13.earlier.first), channel_id=1, source_target_pairs={{0,2},{1,3},{2,0},{3,1},{4,6},{5,7},{6,4},{7,5},{8,10},{9,11},{10,... | collective-permute-start | bytes 516104 | tf_op jit(solution)/shard_map/ppermute | solution.py:33
  13.8 10.7 %collective-permute-start.5 = (bf16[96,896]{1,0:T(8,128)(2,1)S(1)}, bf16[96,896]{1,0:T(8,128)(2,1)S(1)}, u32[]{:S(2)}, u32[]{:S(2)}) collective-permute-start(bf16[96,896]{1,0:T(8,128)(2,1)S(1)} %add.13.earlier.first), channel_id=1, source_target_pairs={{0,1},{1,0},{2,3},{3,2},{4,5},{5,4},{6,7},{7,6},{8,9},{9,8},{10,11... | collective-permute-start | bytes 516104 | tf_op jit(solution)/shard_map/ppermute | solution.py:33
  19.3 5.1 %collective-permute-start.6 = (bf16[96,896]{1,0:T(8,128)(2,1)S(1)}, bf16[96,896]{1,0:T(8,128)(2,1)S(1)}, u32[]{:S(2)}, u32[]{:S(2)}) collective-permute-start(bf16[96,896]{1,0:T(8,128)(2,1)S(1)} %add.14.earlier.second), channel_id=1, source_target_pairs={{0,1},{1,0},{2,3},{3,2},{4,5},{5,4},{6,7},{7,6},{8,9},{9,8},{10,11... | collective-permute-start | bytes 516104 | tf_op jit(solution)/shard_map/ppermute | solution.py:33
  28.1 4.0 %collective-permute-start.7 = (f32[32,5120]{1,0:T(8,128)S(1)}, f32[32,5120]{1,0:T(8,128)S(1)}, u32[]{:S(2)}, u32[]{:S(2)}) collective-permute-start(f32[32,5120]{1,0:T(8,128)S(1)} %shard_map.116.mine), channel_id=1, source_target_pairs={{0,8},{8,0},{16,24},{24,16},{1,9},{9,1},{17,25},{25,17},{2,10},{10... | collective-permute-start | bytes 1966088 | tf_op jit(solution)/shard_map/ppermute | solution.py:19
  32.1 9.4 %copy-start = (f32[1,2,2]{2,1,0:T(2,128)S(1)}, f32[1,2,2]{2,1,0:T(2,128)}, u32[]{:S(2)}) copy-start(f32[1,2,2]{2,1,0:T(2,128)} %param.12) | copy-start | bytes 52
  32.2 9.4 %copy-start.1 = (s32[1,2,2]{2,1,0:T(2,128)S(1)}, s32[1,2,2]{2,1,0:T(2,128)}, u32[]{:S(2)}) copy-start(s32[1,2,2]{2,1,0:T(2,128)} %param.11) | copy-start | bytes 52
  32.2 9.4 %copy-start.2 = (f32[1,2,2]{2,1,0:T(2,128)S(1)}, f32[1,2,2]{2,1,0:T(2,128)}, u32[]{:S(2)}) copy-start(f32[1,2,2]{2,1,0:T(2,128)} %param.15) | copy-start | bytes 52
  32.2 9.4 %copy-start.3 = (s32[1,2,2]{2,1,0:T(2,128)S(1)}, s32[1,2,2]{2,1,0:T(2,128)}, u32[]{:S(2)}) copy-start(s32[1,2,2]{2,1,0:T(2,128)} %param.14) | copy-start | bytes 52
  37.2 16.7 %all-to-all-start = ((bf16[8,8,3584]{2,1,0:T(8,128)(2,1)}), bf16[8,8,3584]{2,1,0:T(8,128)(2,1)S(1)}, u32[]{:S(2)}, u32[]{:S(2)}) async-start(bf16[8,8,3584]{2,1,0:T(8,128)(2,1)} %bitcast.13), calls=%async_computation | async-start | bytes 917504 | tf_op jit(solution)/shard_map/all_to_all | solution.py:277
  41.6 1.5 %collective-permute-start.8 = (f32[4,4]{1,0:T(4,128)S(1)}, f32[4,4]{1,0:T(4,128)S(1)}, u32[]{:S(2)}, u32[]{:S(2)}) collective-permute-start(f32[4,4]{1,0:T(4,128)S(1)} %pad_maximum_fusion.2), channel_id=1, source_target_pairs={{0,8},{8,0},{16,24},{24,16},{1,9},{9,1},{17,25},{25,17},{2,10},{10... | collective-permute-start | bytes 200 | tf_op jit(solution)/shard_map/ppermute | solution.py:19
  43.2 2.8 %collective-permute-start.9 = (f32[2,4]{1,0:T(2,128)S(1)}, f32[2,4]{1,0:T(2,128)S(1)}, u32[]{:S(2)}, u32[]{:S(2)}) collective-permute-start(f32[2,4]{1,0:T(2,128)S(1)} %get-tuple-element.37), channel_id=1, source_target_pairs={{0,16},{1,17},{2,18},{3,19},{4,20},{5,21},{6,22},{7,23},{8,24},{9,... | collective-permute-start | bytes 104 | tf_op jit(solution)/shard_map/ppermute | solution.py:41
  54.2 2.5 %collective-permute-start.10 = (bf16[4,3584]{1,0:T(4,128)(2,1)S(1)}, bf16[4,3584]{1,0:T(4,128)(2,1)S(1)}, u32[]{:S(2)}, u32[]{:S(2)}) collective-permute-start(bf16[4,3584]{1,0:T(4,128)(2,1)S(1)} %get-tuple-element.25), channel_id=1, source_target_pairs={{0,8},{8,0},{16,24},{24,16},{1,9},{9,1},{17,25},{25,17},{2,10},{10... | collective-permute-start | bytes 86024 | tf_op jit(solution)/shard_map/ppermute | solution.py:19

commit v4 on v3

v4 whole, which is shorter than its diff:
```python
import functools
import typing

import jax
import jax.numpy as jnp
from jax import lax
from jax.experimental import pallas as pl
from jax.experimental.pallas import tpu as pltpu
from jax.sharding import PartitionSpec as P

GROUPS = 4
PARTS = 4
BATCH = 8
F32 = jnp.float32
BF16 = jnp.bfloat16


def swap_cores(block):
    sections = range(lax.axis_size("section"))
    return lax.ppermute(block, "section", [(i, i ^ 1) for i in sections])


def expert_weights(routes, probs):
    named = routes[:, :, None] == jnp.arange(GROUPS, dtype=jnp.int32)
    return jnp.sum(jnp.where(named, probs[:, :, None], 0.0), axis=1)


def by_section(mine, theirs, core):
    return jnp.where(core == 0, mine, theirs), jnp.where(core == 0, theirs, mine)


def swap_ranks(block, bit):
    ranks = range(lax.axis_size("expert"))
    return lax.ppermute(block, "expert", [(i, i ^ bit) for i in ranks])


def to_next_chips(fwd, bwd, bit):
    sections, ranks = lax.axis_size("section"), lax.axis_size("expert")

    def move(block, pairs):
        route = [(a * ranks + e, b * ranks + (e ^ bit)) for a, b in pairs for e in range(ranks)]
        return lax.ppermute(block, ("section", "expert"), route)

    up = [(i, i + 2) for i in range(sections - 2)]
    down = [(b, a) for a, b in up]
    if sections != 4:
        return [move(fwd, up), move(bwd, down)]
    return [move(jnp.where(lax.axis_index("section") < 2, fwd, bwd), up + down)]


def folded(block):
    rows, width = block.shape
    block = block.reshape(rows, PARTS, width // PARTS).transpose(1, 0, 2)
    return block.reshape(rows * PARTS, width // PARTS)


def unfolded(block):
    rows, width = block.shape
    block = block.reshape(PARTS, rows // PARTS, width).transpose(1, 0, 2)
    return block.reshape(rows // PARTS, width * PARTS)


class Plan(typing.NamedTuple):
    fwd: int
    both: int
    bwd: int
    rows: int
    places: tuple
    other: tuple


def plan_of(sections):
    if sections == 4:
        places = ((0, 2, 0), (24, 4, 0), (8, 4, 0), (24, 4, 2), (8, 4, 2))
        other = (None, (24, 2, 0), None, (32, 2, 0), None)
        return Plan(1, 1, 1, 40, places, other)
    places = ((0, 2, 0), (24, 2, 0), (8, 4, 0), (32, 4, 0), (8, 4, 2), (32, 4, 2))
    return Plan(2, 0, 2, 48, places, (None,) * 6)


def dot(a, b):
    return jnp.dot(a, b, preferred_element_type=F32)


def one_hot(rows, want):
    out = lax.broadcasted_iota(jnp.int32, (rows, rows), 0)
    src = lax.broadcasted_iota(jnp.int32, (rows, rows), 1)
    return jnp.where(want(out) == src, 1.0, 0.0).astype(BF16)


def gathered_order(plan, forward):
    kinds = len(plan.places)

    def want(out):
        part, rest = lax.div(out, kinds * 2 * BATCH), lax.rem(out, kinds * 2 * BATCH)
        kind, rest = lax.div(rest, 2 * BATCH), lax.rem(rest, 2 * BATCH)
        row = jnp.zeros_like(out)
        for i, (here, there) in enumerate(zip(plan.places, plan.other, strict=True)):
            base, size, offset = here
            if there is not None:
                base, size, offset = (
                    jnp.where(forward == 1, t, h) for h, t in zip(here, there, strict=True)
                )
            row = jnp.where(kind == i, base + offset + part * size, row)
        return lax.div(rest, 2) * plan.rows + row + lax.rem(rest, 2)

    return one_hot(BATCH * plan.rows, want)


def returned_order(groups):
    size = PARTS * groups * 2

    def want(out):
        block, rest = lax.div(out, size), lax.rem(out, size)
        return lax.div(rest, 2) * (2 * BATCH) + block * 2 + lax.rem(rest, 2)

    return one_hot(BATCH * size, want)


def fetch_kernel(steps, axis, order, place, weight, earlier, held, turned, zero, *rest):
    sems = rest[-1]
    size = held.shape[axis] // steps
    base = place[0] * held.shape[axis]

    def at(start):
        rows = pl.ds(pl.multiple_of(start, 128), size)
        return rows if axis == 0 else (slice(None), rows)

    copies = [
        pltpu.make_async_copy(
            weight.at[at(base + i * size)], held.at[at(i * size)], sems.at[i]
        )
        for i in range(steps)
    ]
    for copy in copies:
        copy.start()
    if order is not None:
        rest[0][...] = order(place)
    for i, copy in enumerate(copies):
        copy.wait()
        here = slice(i * size, (i + 1) * size)
        if axis == 0:
            turned[:, here] = held[here, :].T
        else:
            turned[here, :] = held[:, here].T
    zero[...] = jnp.zeros_like(zero)


def fetch(place, weight, axis, earlier, like, order=None, count=0):
    steps = 4
    shape = list(weight.shape)
    shape[axis] //= 2
    return pl.pallas_call(
        functools.partial(fetch_kernel, steps, axis, order),
        in_specs=[
            pl.BlockSpec(memory_space=pltpu.SMEM),
            pl.BlockSpec(memory_space=pltpu.HBM),
            pl.BlockSpec(memory_space=pl.ANY),
        ],
        out_specs=[pl.BlockSpec(memory_space=pltpu.VMEM)] * (3 + (count > 0)),
        out_shape=[
            pltpu.VMEM(tuple(shape), BF16),
            pltpu.VMEM(tuple(shape[::-1]), BF16),
            jax.ShapeDtypeStruct(like, BF16),
            pltpu.VMEM((count, count), BF16),
        ][: 3 + (count > 0)],
        scratch_shapes=[pltpu.SemaphoreType.DMA((steps,))],
        compiler_params=pltpu.CompilerParams(vmem_limit_bytes=2**21),
        cost_estimate=pl.CostEstimate(
            flops=0, bytes_accessed=weight.size * 4, transcendentals=0
        ),
    )(place, pltpu.with_memory_space_constraint(weight, pltpu.HBM), earlier)


def up_kernel(plan, ranks, order, first, second, third, fourth, g, u, d_t, out):
    hid = g.shape[1]
    n = 2 * BATCH
    kinds = len(plan.places)
    groups = plan.fwd + plan.both + plan.bwd
    piece = first.shape[1]
    blocks = jnp.concatenate([first[...], second[...], third[...], fourth[...]])
    order = order[...]
    count = order.shape[0]
    batches = ranks // BATCH
    sorted_rows = [
        dot(order, blocks[i * count : (i + 1) * count]).astype(BF16) for i in range(batches)
    ]
    a, b, dh = 0.0, 0.0, 0.0
    for part in range(PARTS):
        cols = slice(part * piece, (part + 1) * piece)
        at = [(part * kinds + kind) * n for kind in range(kinds)]
        taken = [jnp.concatenate([rows[i : i + n] for rows in sorted_rows]) for i in at]
        rows = jnp.concatenate(taken[:groups])
        a += dot(rows, g[cols, :])
        b += dot(rows, u[cols, :])
        dh += dot(jnp.concatenate(taken[groups:]), d_t[cols, :])
    n = n * batches
    for i in range(groups):
        out[:, i * hid : (i + 1) * hid] = a[i * n : (i + 1) * n]
        out[:, (groups + i) * hid : (groups + i + 1) * hid] = b[i * n : (i + 1) * n]
    for i in range(kinds - groups):
        at = (2 * groups + i) * hid
        out[:, at : at + hid] = dh[i * n : (i + 1) * n]


def down_kernel(plan, ranks, place, order, mine, theirs, g_t, u_t, d, kept, sent):
    hid = d.shape[0]
    groups = plan.fwd + plan.both + plan.bwd
    n = 2 * ranks
    split = plan.fwd * n

    def summed(i):
        return mine[:, i * hid : (i + 1) * hid] + theirs[:, i * hid : (i + 1) * hid]

    h, da, du = [], [], []
    forward = jnp.where(place[2] == 1, 1.0, 0.0)
    for i in range(groups):
        a, b = summed(i), summed(groups + i)
        s = jax.nn.sigmoid(a)
        if i < plan.fwd + plan.both:
            hidden = (a * s * b).astype(BF16)
            h.append(hidden if i < plan.fwd else hidden * forward.astype(BF16))
        if i >= plan.fwd:
            dh = summed(2 * groups + i - plan.fwd)
            da.append((dh * b * s * (1.0 + a * (1.0 - s))).astype(BF16))
            du.append((dh * a * s).astype(BF16))
    h, da, du = jnp.concatenate(h), jnp.concatenate(da), jnp.concatenate(du)
    piece = kept.shape[1]
    results = []
    for part in range(PARTS):
        cols = slice(part * piece, (part + 1) * piece)
        y = dot(h, d[:, cols])
        dx = dot(da, g_t[:, cols]) + dot(du, u_t[:, cols])
        shared = plan.both * n
        rows = [y[:split], y[split:] + dx[:shared], dx[shared:]] if shared else [y, dx]
        results.append(jnp.concatenate(rows).astype(BF16))
    order = order[...]
    size = 2 * BATCH
    rows = [
        jnp.concatenate(
            [
                result[i * n + batch * size : i * n + (batch + 1) * size]
                for result in results
                for i in range(groups)
            ]
        )
        for batch in range(ranks // BATCH)
    ]
    rows = jnp.concatenate([dot(order, batch).astype(BF16) for batch in rows])
    kept[...] = rows[: kept.shape[0]]
    sent[...] = rows[kept.shape[0] :]


def pair_kernel(kept, got, weights, *pairs):
    size = pairs[0].shape[0]
    for i, pair in enumerate(pairs):
        rows = slice(i * size, (i + 1) * size)
        pair[...] = (kept[rows].astype(F32) + got[rows].astype(F32)).astype(BF16)


def finish_kernel(plan, offsets, shards, ranks, place, weights, *refs):
    *back, own, other = refs
    total = 0.0
    for offset, block in zip(offsets, back, strict=True):
        expert = lax.div(lax.bitwise_xor(place[1], jnp.int32(offset)), jnp.int32(shards))
        named = lax.broadcasted_iota(jnp.int32, weights.shape, 1) == expert
        weight = jnp.sum(jnp.where(named, weights[...], 0.0), axis=1, keepdims=True)
        total += block[...].astype(F32) * weight
    forward = jnp.where(place[2] == 1, 1.0, 0.0)
    size = 2 * (plan.fwd + plan.both + plan.bwd)
    even, odd = [], []
    for part in range(PARTS):
        rows = [total[i : i + 2] for i in range(part * size, (part + 1) * size, 2)]
        if plan.both:
            fwd, far, bwd = rows
            even += [far * forward, bwd]
            odd += [fwd, far * (1.0 - forward)]
        else:
            fwd, far_fwd, bwd, far_bwd = rows
            even += [far_fwd, bwd]
            odd += [fwd, far_bwd]
    even, odd = jnp.concatenate(even), jnp.concatenate(odd)
    own[...] = jnp.where(place[0] == 0, even, odd).astype(BF16)
    other[...] = jnp.where(place[0] == 0, odd, even).astype(BF16)


def on_core(kernel, place, operands, results, cost):
    specs = [pl.BlockSpec(memory_space=pltpu.VMEM)] * len(operands)
    operands = [pltpu.with_memory_space_constraint(x, pltpu.VMEM) for x in operands]
    if place is not None:
        specs = [pl.BlockSpec(memory_space=pltpu.SMEM)] + specs
        operands = [place] + operands
    ranks = lax.axis_size("expert")
    return pl.pallas_call(
        kernel,
        in_specs=specs,
        out_specs=[pl.BlockSpec(memory_space=pltpu.VMEM)] * len(results),
        out_shape=[jax.ShapeDtypeStruct(*result) for result in results],
        compiler_params=pltpu.CompilerParams(vmem_limit_bytes=ranks * 3 * 2**17),
        cost_estimate=pl.CostEstimate(
            flops=cost * 512, bytes_accessed=cost * 2, transcendentals=0
        ),
    )(*operands)


def after(value, other):
    return lax.optimization_barrier((value, other))[0]


def local(
    fwd_tokens,
    fwd_routes,
    fwd_probs,
    bwd_tokens,
    bwd_routes,
    bwd_probs,
    bwd_grads,
    w_gate,
    w_up,
    w_down,
):
    ranks, sections = lax.axis_size("expert"), lax.axis_size("section")
    shards = ranks // GROUPS
    plan = plan_of(sections)
    groups = plan.fwd + plan.both + plan.bwd
    width = fwd_tokens.shape[2]
    half = width // 2
    hid = w_gate.shape[1]
    section = lax.axis_index("section")
    core = section % 2
    place = jnp.stack([core, lax.axis_index("expert"), section >= 2]).astype(jnp.int32)

    rows = jnp.concatenate([fwd_tokens[0], bwd_tokens[0], bwd_grads[0]])
    keep, send = by_section(rows[:, :half], rows[:, half:], core)
    even, odd = by_section(keep, swap_cores(send), core)

    near = jnp.concatenate([folded(even[:2]), folded(odd[2:])])
    far_fwd, far_bwd = folded(odd[:2]), folded(even[2:])
    if plan.both:
        far_fwd = jnp.pad(far_fwd, ((0, far_bwd.shape[0] - far_fwd.shape[0]), (0, 0)))
    top = ranks // 2
    far = to_next_chips(far_fwd, far_bwd, 0)
    far_top = to_next_chips(far_fwd, far_bwd, top)
    blocks = jnp.concatenate([near, *far, swap_ranks(near, top), *far_top])
    offsets = [0, top]
    g, g_t, zero = fetch(place, w_gate, 0, near, blocks.shape)
    blocks = blocks + zero
    bit = top // 2
    while bit > 2:
        blocks = jnp.concatenate([blocks, swap_ranks(blocks, bit)])
        offsets += [o ^ bit for o in offsets]
        bit //= 2
    offsets += [o ^ 2 for o in offsets]
    second = swap_ranks(blocks, 2)
    third = swap_ranks(blocks, 1)
    u, u_t, zero, back_order = fetch(
        place,
        w_up,
        0,
        blocks,
        second.shape,
        lambda _: returned_order(groups),
        BATCH * PARTS * groups * 2,
    )
    second = second + zero
    fourth = swap_ranks(second, 1)
    d, d_t, _, got_order = fetch(
        place,
        w_down,
        1,
        second,
        (16, 128),
        lambda place: gathered_order(plan, place[2]),
        BATCH * plan.rows,
    )

    (mine,) = on_core(
        functools.partial(up_kernel, plan, ranks),
        None,
        (got_order, blocks, second, third, fourth, g, u, d_t),
        [((2 * ranks, (groups + len(plan.places)) * hid), F32)],
        3 * hid * half,
    )
    kept, sent = on_core(
        functools.partial(down_kernel, plan, ranks),
        place,
        (back_order, mine, swap_cores(mine), g_t, u_t, d),
        [((ranks // 2 * PARTS * groups * 2, half // PARTS), BF16)] * 2,
        3 * hid * half,
    )
    weights = jnp.concatenate(
        [
            expert_weights(after(fwd_routes[0], sent), fwd_probs[0]),
            expert_weights(after(bwd_routes[0], sent), bwd_probs[0]),
        ]
    )
    even, odd = by_section(weights, swap_cores(weights), core)
    far = to_next_chips(odd[:2], even[2:], 0)
    weights = jnp.concatenate([even[:2], far[0], odd[2:], *far[1:]])
    weights = jnp.concatenate([weights] * PARTS)
    block = ((PARTS * groups * 2, half // PARTS), BF16)
    pairs = on_core(
        pair_kernel, None, (kept, swap_ranks(sent, 1), weights), [block] * (ranks // 2), half
    )
    back = [swap_ranks(pair, o) if o else pair for pair, o in zip(pairs, offsets, strict=True)]
    own, other = on_core(
        functools.partial(finish_kernel, plan, offsets, shards, ranks),
        place,
        (weights, *back),
        [((4 * PARTS, half // PARTS), BF16)] * 2,
        half,
    )
    own, other = unfolded(own), unfolded(swap_cores(other))
    whole = jnp.where(
        core == 0,
        jnp.concatenate([own, other], axis=1),
        jnp.concatenate([other, own], axis=1),
    )
    return (whole[None, :2], whole[None, 2:])


def solution(mesh):
    return jax.shard_map(
        local,
        mesh=mesh,
        in_specs=(
            P("section", "expert", None),
            P("section", "expert", None),
            P("section", "expert", None),
            P("section", "expert", None),
            P("section", "expert", None),
            P("section", "expert", None),
            P("section", "expert", None),
            P(None, "expert"),
            P(None, "expert"),
            P("expert", None),
        ),
        out_specs=(P("section", "expert", None), P("section", "expert", None)),
        check_vma=False,
    )
```

time: 58 us -> 55.8 us (0.962)
  waiting for transfers between devices: 13.9 us -> 10.3 us
  starting transfers between devices: 18.2 us -> 19.2 us
  Pallas kernels: 22 us -> 22.8 us
    all_to_all x1 -> x0, waiting for transfers between devices: 7.84 us -> none  [local(): lax.all_to_all(out.reshape(ranks, 8, half), 'expert', split_axis=0, conca...]
    ppermute x4 -> x8, waiting for transfers between devices: 0.01 us -> 5.3 us  [swap_ranks(): return lax.ppermute(block, 'expert', [(i, i ^ bit) for i in ranks])]
    ppermute x4 -> x8, starting transfers between devices: 3.06 us -> 7.92 us  [swap_ranks(): return lax.ppermute(block, 'expert', [(i, i ^ bit) for i in ranks])]
    all_to_all x1 -> x0, starting transfers between devices: 4.26 us -> none  [local(): lax.all_to_all(out.reshape(ranks, 8, half), 'expert', split_axis=0, conca...]
    ppermute x4, waiting for transfers between devices: 4.51 us -> 3.49 us  [swap_cores(): return lax.ppermute(block, 'section', [(i, i ^ 1) for i in sections])]
    pallas_call x5 -> x7, Pallas kernels: 22 us -> 22.8 us  [the longest x3 13.4 us: fetch(): pl.pallas_call(functools.partial(fetch_kernel, steps, axis, order), in_sp...]
  transfers between devices with their start and end apart: 12 -> 15, of which waited for: 6 -> 8; matrix products, arithmetic and copies ran while one was open for 1% -> 0% of each run, Pallas kernels for 23% -> 24%
where the time goes in v4:
time: 55.8 us; the launch traced here: 55.4 us
  Pallas kernels  22.8 us (41%)
  starting transfers between devices  19.2 us (34%)
  waiting for transfers between devices  10.3 us (18%)
  other arithmetic  1.22 us (2%)
  local copies, waits for them, and re-layouts  0.94 us (2%)
  between operations  0.91 us (2%)
    pallas_call x3, Pallas kernels, fetch(): pl.pallas_call(functools.partial(fetch_kernel, steps, axis, order), in_sp...  13.4 us
    pallas_call x4, Pallas kernels, on_core(): pl.pallas_call(kernel, in_specs=specs, out_specs=[pl.BlockSpec(memory_spa...  9.4 us
    ppermute x8, starting transfers between devices, swap_ranks(): return lax.ppermute(block, 'expert', [(i, i ^ bit) for i in ranks])  7.92 us
    ppermute x3, starting transfers between devices, move(): return lax.ppermute(block, ('section', 'expert'), route)  5.98 us
    ppermute x4, starting transfers between devices, swap_cores(): return lax.ppermute(block, 'section', [(i, i ^ 1) for i in sections])  5.33 us
    ppermute x8, waiting for transfers between devices, swap_ranks(): return lax.ppermute(block, 'expert', [(i, i ^ bit) for i in ranks])  5.3 us
    ppermute x4, waiting for transfers between devices, swap_cores(): return lax.ppermute(block, 'section', [(i, i ^ 1) for i in sections])  3.49 us
    ppermute x3, waiting for transfers between devices, move(): return lax.ppermute(block, ('section', 'expert'), route)  1.51 us
  transfers between devices with their start and end apart: 15, of which 8 were waited for; matrix products, arithmetic and copies ran while one was open for 0% of the time, Pallas kernels for 24%

profile of v4, /device:TPU:1, one launch (start us, length us, event | category | flops | bytes accessed | tf_op | source)
XLA Modules:
  0.0 55.4 jit_solution(3543014673770043411)
XLA Ops:
  0.6 0.9 %pad_maximum_fusion = bf16[6,7168]{1,0:T(8,128)(2,1)S(1)} fusion(bf16[2,7168]{1,0:T(2,128)(2,1)} %bitcast.38, bf16[2,7168]{1,0:T(2,128)(2,1)} %bitcast.39, bf16[2,7168]{1,0:T(2,128)(2,1)} %bitcast.40), kind=kLoop, calls=%fused_computation | loop fusion | flops 258048 | bytes 172032 | tf_op jit(solution)/shard_map/concatenate | solution.py:333
  1.5 0.1 collective-permute-start
  1.7 0.1 pad_add_fusion.place
  1.7 1.1 %collective-permute-done = bf16[6,3584]{1,0:T(8,128)(2,1)S(1)} collective-permute-done((bf16[6,3584]{1,0:T(8,128)(2,1)S(1)}, bf16[6,3584]{1,0:T(8,128)(2,1)S(1)}, u32[]{:S(2)}, u32[]{:S(2)}) %collective-permute-start) | collective-permute-done | bytes 43040 | tf_op jit(solution)/shard_map/ppermute | solution.py:20
  3.0 4.5 %collective-permute-start.3 = (bf16[16,896]{1,0:T(8,128)(2,1)S(1)}, bf16[16,896]{1,0:T(8,128)(2,1)S(1)}, u32[]{:S(2)}, u32[]{:S(2)}) collective-permute-start(bf16[16,896]{1,0:T(8,128)(2,1)S(1)} %pad_select_fusion), channel_id=1, source_target_pairs={{0,20},{1,21},{2,22},{3,23},{4,16},{5,17},{6,18},{7,19},{8,28},{9,... | collective-permute-start | bytes 86024 | tf_op jit(solution)/shard_map/ppermute | solution.py:42
  7.5 0.3 collective-permute-start.1
  7.8 0.2 collective-permute-start.2
  8.0 4.3 %shard_map.113 = (bf16[3584,1024]{1,0:T(8,128)(2,1)S(1)}, bf16[1024,3584]{1,0:T(8,128)(2,1)S(1)}, bf16[80,896]{1,0:T(8,128)(2,1)S(1)}) custom-call(s32[3]{0:T(128)S(1)} %pad_add_fusion.place, bf16[7168,1024]{1,0:T(8,128)(2,1)} %weight.3, bf16[24,896]{1,0:T(8,128)(2,1)S(1)} %get-tuple-element.46.earlier), custom_call_target="tpu_custom_call" | custom-call | bytes 29360128 | tf_op jit(solution)/shard_map/pallas_call | solution.py:153
  12.2 0.0 collective-permute-done.1
  12.3 0.0 collective-permute-done.2
  12.3 0.0 collective-permute-done.3
  12.4 1.4 %collective-permute-start.4 = (bf16[80,896]{1,0:T(8,128)(2,1)S(1)}, bf16[80,896]{1,0:T(8,128)(2,1)S(1)}, u32[]{:S(2)}, u32[]{:S(2)}) collective-permute-start(bf16[80,896]{1,0:T(8,128)(2,1)S(1)} %add.13.earlier.first), channel_id=1, source_target_pairs={{0,2},{1,3},{2,0},{3,1},{4,6},{5,7},{6,4},{7,5},{8,10},{9,11},{10,... | collective-permute-start | bytes 430088 | tf_op jit(solution)/shard_map/ppermute | solution.py:34
  13.7 1.2 %collective-permute-start.5 = (bf16[80,896]{1,0:T(8,128)(2,1)S(1)}, bf16[80,896]{1,0:T(8,128)(2,1)S(1)}, u32[]{:S(2)}, u32[]{:S(2)}) collective-permute-start(bf16[80,896]{1,0:T(8,128)(2,1)S(1)} %add.13.earlier.first), channel_id=1, source_target_pairs={{0,1},{1,0},{2,3},{3,2},{4,5},{5,4},{6,7},{7,6},{8,9},{9,8},{10,11... | collective-permute-start | bytes 430088 | tf_op jit(solution)/shard_map/ppermute | solution.py:34
  15.0 4.3 %shard_map.114 = (bf16[3584,1024]{1,0:T(8,128)(2,1)S(1)}, bf16[1024,3584]{1,0:T(8,128)(2,1)S(1)}, bf16[80,896]{1,0:T(8,128)(2,1)S(1)}, bf16[192,192]{1,0:T(8,128)(2,1)S(1)}) custom-call(s32[3]{0:T(128)S(1)} %pad_add_fusion.place, bf16[7168,1024]{1,0:T(8,128)(2,1)} %weight.4, bf16[80,896]{1,0:T(8,128)(2,1)S(1)} %add.13.earlier.first), custom_call_target="tpu_custom_call" | custom-call | bytes 29360128 | tf_op jit(solution)/shard_map/pallas_call | solution.py:153
  19.2 0.0 collective-permute-done.4
  19.3 0.3 collective-permute-start.6
  19.6 4.8 %shard_map.115 = (bf16[1024,3584]{1,0:T(8,128)(2,1)S(1)}, bf16[3584,1024]{1,0:T(8,128)(2,1)S(1)}, bf16[16,128]{1,0:T(8,128)(2,1)}, bf16[320,320]{1,0:T(8,128)(2,1)S(1)}) custom-call(s32[3]{0:T(128)S(1)} %pad_add_fusion.place, bf16[1024,7168]{1,0:T(8,128)(2,1)} %weight.5, bf16[80,896]{1,0:T(8,128)(2,1)S(1)} %add.14.earlier.second), custom_call_target="tpu_custom_call" | custom-call | bytes 29360128 | tf_op jit(solution)/shard_map/pallas_call | solution.py:153
  24.4 0.0 collective-permute-done.5.third
  24.4 0.0 collective-permute-done.6.fourth
  24.4 4.3 %shard_map.116.mine = f32[16,8192]{1,0:T(8,128)S(1)} custom-call(bf16[320,320]{1,0:T(8,128)(2,1)S(1)} %get-tuple-element.25.order, bf16[80,896]{1,0:T(8,128)(2,1)S(1)} %add.13.earlier.first, bf16[80,896]{1,0:T(8,128)(2,1)S(1)} %add.14.earlier.second, bf16[80,896]{1,0:T(8,128)(2,1)S(1)} %collective-permute-done.5.third, ...), custom_call_target="tpu_custom_call" | custom-call | flops 5637144576 | bytes 22020096 | tf_op jit(solution)/shard_map/pallas_call | solution.py:294
  28.7 2.3 %collective-permute-start.7 = (f32[16,8192]{1,0:T(8,128)S(1)}, f32[16,8192]{1,0:T(8,128)S(1)}, u32[]{:S(2)}, u32[]{:S(2)}) collective-permute-start(f32[16,8192]{1,0:T(8,128)S(1)} %shard_map.116.mine), channel_id=1, source_target_pairs={{0,8},{8,0},{16,24},{24,16},{1,9},{9,1},{17,25},{25,17},{2,10},{10... | collective-permute-start | bytes 1572872 | tf_op jit(solution)/shard_map/ppermute | solution.py:20
  31.0 1.5 %collective-permute-done.7.theirs = f32[16,8192]{1,0:T(8,128)S(1)} collective-permute-done((f32[16,8192]{1,0:T(8,128)S(1)}, f32[16,8192]{1,0:T(8,128)S(1)}, u32[]{:S(2)}, u32[]{:S(2)}) %collective-permute-start.7) | collective-permute-done | bytes 524320 | tf_op jit(solution)/shard_map/ppermute | solution.py:20
  32.5 0.0 copy-start
  32.5 0.0 copy-start.1
  32.5 0.0 copy-start.2
  32.5 4.4 %shard_map.117 = (bf16[96,896]{1,0:T(8,128)(2,1)S(1)}, bf16[96,896]{1,0:T(8,128)(2,1)S(1)}) custom-call(s32[3]{0:T(128)S(1)} %pad_add_fusion.place, bf16[192,192]{1,0:T(8,128)(2,1)S(1)} %get-tuple-element.23.order, f32[16,8192]{1,0:T(8,128)S(1)} %shard_map.116.mine, f32[16,8192]{1,0:T(8,128)S(1)} %collective-permute-done.7.theirs, ...), custom_call_target="tpu_custom_call" | custom-call | flops 5637144576 | bytes 22020096 | tf_op jit(solution)/shard_map/pallas_call | solution.py:294
  36.9 0.0 copy-done
  36.9 0.0 copy-done.1
  37.0 0.0 copy-done.2
  37.0 0.0 copy-done.3
  37.0 0.1 fusion
  37.1 0.4 collective-permute-start.8
  37.5 1.2 %collective-permute-start.10 = (bf16[96,896]{1,0:T(8,128)(2,1)S(1)}, bf16[96,896]{1,0:T(8,128)(2,1)S(1)}, u32[]{:S(2)}, u32[]{:S(2)}) collective-permute-start(bf16[96,896]{1,0:T(8,128)(2,1)S(1)} %get-tuple-element.32), channel_id=1, source_target_pairs={{0,1},{1,0},{2,3},{3,2},{4,5},{5,4},{6,7},{7,6},{8,9},{9,8},{10,11... | collective-permute-start | bytes 516104 | tf_op jit(solution)/shard_map/ppermute | solution.py:34
  38.8 0.0 collective-permute-done.8
  38.8 1.3 %collective-permute-start.9 = (f32[2,4]{1,0:T(2,128)S(1)}, f32[2,4]{1,0:T(2,128)S(1)}, u32[]{:S(2)}, u32[]{:S(2)}) collective-permute-start(f32[2,4]{1,0:T(2,128)S(1)} %get-tuple-element.53), channel_id=1, source_target_pairs={{0,16},{1,17},{2,18},{3,19},{4,20},{5,21},{6,22},{7,23},{8,24},{9,... | collective-permute-start | bytes 104 | tf_op jit(solution)/shard_map/ppermute | solution.py:42
  40.1 1.5 %collective-permute-done.9 = f32[2,4]{1,0:T(2,128)S(1)} collective-permute-done((f32[2,4]{1,0:T(2,128)S(1)}, f32[2,4]{1,0:T(2,128)S(1)}, u32[]{:S(2)}, u32[]{:S(2)}) %collective-permute-start.9) | collective-permute-done | bytes 64 | tf_op jit(solution)/shard_map/ppermute | solution.py:42
  41.6 0.1 concatenate.28.weights
  41.6 1.7 %collective-permute-done.10.got = bf16[96,896]{1,0:T(8,128)(2,1)S(1)} collective-permute-done((bf16[96,896]{1,0:T(8,128)(2,1)S(1)}, bf16[96,896]{1,0:T(8,128)(2,1)S(1)}, u32[]{:S(2)}, u32[]{:S(2)}) %collective-permute-start.10) | collective-permute-done | bytes 172064 | tf_op jit(solution)/shard_map/ppermute | solution.py:34
  43.4 2.1 %collective-permute-start.11 = (bf16[24,896]{1,0:T(8,128)(2,1)S(1)}, bf16[24,896]{1,0:T(8,128)(2,1)S(1)}, u32[]{:S(2)}, u32[]{:S(2)}) collective-permute-start(bf16[24,896]{1,0:T(8,128)(2,1)S(1)} %get-tuple-element.37), channel_id=1, source_target_pairs={{0,4},{1,5},{2,6},{3,7},{4,0},{5,1},{6,2},{7,3},{8,12},{9,13},{10,... | collective-permute-start | bytes 129032 | tf_op jit(solution)/shard_map/ppermute | solution.py:34
  45.5 0.2 collective-permute-start.12
  45.7 1.3 %collective-permute-start.13 = (bf16[24,896]{1,0:T(8,128)(2,1)S(1)}, bf16[24,896]{1,0:T(8,128)(2,1)S(1)}, u32[]{:S(2)}, u32[]{:S(2)}) collective-permute-start(bf16[24,896]{1,0:T(8,128)(2,1)S(1)} %get-tuple-element.39), channel_id=1, source_target_pairs={{0,6},{1,7},{2,4},{3,5},{4,2},{5,3},{6,0},{7,1},{8,14},{9,15},{10,... | collective-permute-start | bytes 129032 | tf_op jit(solution)/shard_map/ppermute | solution.py:34
  47.0 0.7 %collective-permute-done.11.refs_1_ = bf16[24,896]{1,0:T(8,128)(2,1)S(1)} collective-permute-done((bf16[24,896]{1,0:T(8,128)(2,1)S(1)}, bf16[24,896]{1,0:T(8,128)(2,1)S(1)}, u32[]{:S(2)}, u32[]{:S(2)}) %collective-permute-start.11) | collective-permute-done | bytes 43040 | tf_op jit(solution)/shard_map/ppermute | solution.py:34
  47.7 1.2 %collective-permute-done.12.refs_2_ = bf16[24,896]{1,0:T(8,128)(2,1)S(1)} collective-permute-done((bf16[24,896]{1,0:T(8,128)(2,1)S(1)}, bf16[24,896]{1,0:T(8,128)(2,1)S(1)}, u32[]{:S(2)}, u32[]{:S(2)}) %collective-permute-start.12) | collective-permute-done | bytes 43040 | tf_op jit(solution)/shard_map/ppermute | solution.py:34
  48.9 1.7 %collective-permute-done.13.refs_3_ = bf16[24,896]{1,0:T(8,128)(2,1)S(1)} collective-permute-done((bf16[24,896]{1,0:T(8,128)(2,1)S(1)}, bf16[24,896]{1,0:T(8,128)(2,1)S(1)}, u32[]{:S(2)}, u32[]{:S(2)}) %collective-permute-start.13) | collective-permute-done | bytes 43040 | tf_op jit(solution)/shard_map/ppermute | solution.py:34
  50.6 0.7 %shard_map.119 = (bf16[16,896]{1,0:T(8,128)(2,1)S(1)}, bf16[16,896]{1,0:T(8,128)(2,1)S(1)}) custom-call(s32[3]{0:T(128)S(1)} %pad_add_fusion.place, f32[24,4]{1,0:T(8,128)S(1)} %concatenate.28.weights, bf16[24,896]{1,0:T(8,128)(2,1)S(1)} %get-tuple-element.36.refs_0_, bf16[24,896]{1,0:T(8,128)(2,1)S(1)} %collective-permute-done.11.refs_1_, ...), custom_call_target="tpu_custom_call" | custom-call | flops 1835008 | bytes 7168 | tf_op jit(solution)/shard_map/pallas_call | solution.py:294
  51.3 2.5 %collective-permute-start.14 = (bf16[16,896]{1,0:T(8,128)(2,1)S(1)}, bf16[16,896]{1,0:T(8,128)(2,1)S(1)}, u32[]{:S(2)}, u32[]{:S(2)}) collective-permute-start(bf16[16,896]{1,0:T(8,128)(2,1)S(1)} %get-tuple-element.41), channel_id=1, source_target_pairs={{0,8},{8,0},{16,24},{24,16},{1,9},{9,1},{17,25},{25,17},{2,10},{10... | collective-permute-start | bytes 86024 | tf_op jit(solution)/shard_map/ppermute | solution.py:20
  53.8 0.8 %collective-permute-done.14 = bf16[16,896]{1,0:T(8,128)(2,1)S(1)} collective-permute-done((bf16[16,896]{1,0:T(8,128)(2,1)S(1)}, bf16[16,896]{1,0:T(8,128)(2,1)S(1)}, u32[]{:S(2)}, u32[]{:S(2)}) %collective-permute-start.14) | collective-permute-done | bytes 28704 | tf_op jit(solution)/shard_map/ppermute | solution.py:20
  54.7 0.7 %slice_bitcast_fusion = (bf16[1,2,7168]{2,1,0:T(2,128)(2,1)}, bf16[1,2,7168]{2,1,0:T(2,128)(2,1)}) fusion(bf16[4,7168]{1,0:T(4,128)(2,1)S(1)} %maximum_select_fusion), kind=kLoop, calls=%fused_computation.6 | loop fusion | bytes 114688 | tf_op jit(solution)/shard_map/broadcast_in_dim | solution.py:419
  (26 shorter events, 0.4 us)
Async XLA Ops:
  1.5 1.3 %collective-permute-start = (bf16[6,3584]{1,0:T(8,128)(2,1)S(1)}, bf16[6,3584]{1,0:T(8,128)(2,1)S(1)}, u32[]{:S(2)}, u32[]{:S(2)}) collective-permute-start(bf16[6,3584]{1,0:T(8,128)(2,1)S(1)} %broadcast_select_fusion.2), channel_id=1, source_target_pairs={{0,8},{8,0},{16,24},{24,16},{1,9},{9,1},{17,25},{25,17},{2,10},{10... | collective-permute-start | bytes 129032 | tf_op jit(solution)/shard_map/ppermute | solution.py:20
  3.0 9.3 %collective-permute-start.3 = (bf16[16,896]{1,0:T(8,128)(2,1)S(1)}, bf16[16,896]{1,0:T(8,128)(2,1)S(1)}, u32[]{:S(2)}, u32[]{:S(2)}) collective-permute-start(bf16[16,896]{1,0:T(8,128)(2,1)S(1)} %pad_select_fusion), channel_id=1, source_target_pairs={{0,20},{1,21},{2,22},{3,23},{4,16},{5,17},{6,18},{7,19},{8,28},{9,... | collective-permute-start | bytes 86024 | tf_op jit(solution)/shard_map/ppermute | solution.py:42
  7.5 4.8 %collective-permute-start.1 = (bf16[16,896]{1,0:T(8,128)(2,1)S(1)}, bf16[16,896]{1,0:T(8,128)(2,1)S(1)}, u32[]{:S(2)}, u32[]{:S(2)}) collective-permute-start(bf16[16,896]{1,0:T(8,128)(2,1)S(1)} %pad_select_fusion), channel_id=1, source_target_pairs={{0,16},{1,17},{2,18},{3,19},{4,20},{5,21},{6,22},{7,23},{8,24},{9,... | collective-permute-start | bytes 86024 | tf_op jit(solution)/shard_map/ppermute | solution.py:42
  7.8 4.5 %collective-permute-start.2 = (bf16[24,896]{1,0:T(8,128)(2,1)S(1)}, bf16[24,896]{1,0:T(8,128)(2,1)S(1)}, u32[]{:S(2)}, u32[]{:S(2)}) collective-permute-start(bf16[24,896]{1,0:T(8,128)(2,1)S(1)} %get-tuple-element.46.earlier), channel_id=1, source_target_pairs={{0,4},{1,5},{2,6},{3,7},{4,0},{5,1},{6,2},{7,3},{8,12},{9,13},{10,... | collective-permute-start | bytes 129032 | tf_op jit(solution)/shard_map/ppermute | solution.py:34
  12.4 6.9 %collective-permute-start.4 = (bf16[80,896]{1,0:T(8,128)(2,1)S(1)}, bf16[80,896]{1,0:T(8,128)(2,1)S(1)}, u32[]{:S(2)}, u32[]{:S(2)}) collective-permute-start(bf16[80,896]{1,0:T(8,128)(2,1)S(1)} %add.13.earlier.first), channel_id=1, source_target_pairs={{0,2},{1,3},{2,0},{3,1},{4,6},{5,7},{6,4},{7,5},{8,10},{9,11},{10,... | collective-permute-start | bytes 430088 | tf_op jit(solution)/shard_map/ppermute | solution.py:34
  13.7 10.7 %collective-permute-start.5 = (bf16[80,896]{1,0:T(8,128)(2,1)S(1)}, bf16[80,896]{1,0:T(8,128)(2,1)S(1)}, u32[]{:S(2)}, u32[]{:S(2)}) collective-permute-start(bf16[80,896]{1,0:T(8,128)(2,1)S(1)} %add.13.earlier.first), channel_id=1, source_target_pairs={{0,1},{1,0},{2,3},{3,2},{4,5},{5,4},{6,7},{7,6},{8,9},{9,8},{10,11... | collective-permute-start | bytes 430088 | tf_op jit(solution)/shard_map/ppermute | solution.py:34
  19.3 5.1 %collective-permute-start.6 = (bf16[80,896]{1,0:T(8,128)(2,1)S(1)}, bf16[80,896]{1,0:T(8,128)(2,1)S(1)}, u32[]{:S(2)}, u32[]{:S(2)}) collective-permute-start(bf16[80,896]{1,0:T(8,128)(2,1)S(1)} %add.14.earlier.second), channel_id=1, source_target_pairs={{0,1},{1,0},{2,3},{3,2},{4,5},{5,4},{6,7},{7,6},{8,9},{9,8},{10,11... | collective-permute-start | bytes 430088 | tf_op jit(solution)/shard_map/ppermute | solution.py:34
  28.7 3.8 %collective-permute-start.7 = (f32[16,8192]{1,0:T(8,128)S(1)}, f32[16,8192]{1,0:T(8,128)S(1)}, u32[]{:S(2)}, u32[]{:S(2)}) collective-permute-start(f32[16,8192]{1,0:T(8,128)S(1)} %shard_map.116.mine), channel_id=1, source_target_pairs={{0,8},{8,0},{16,24},{24,16},{1,9},{9,1},{17,25},{25,17},{2,10},{10... | collective-permute-start | bytes 1572872 | tf_op jit(solution)/shard_map/ppermute | solution.py:20
  32.5 4.4 %copy-start = (f32[1,2,2]{2,1,0:T(2,128)S(1)}, f32[1,2,2]{2,1,0:T(2,128)}, u32[]{:S(2)}) copy-start(f32[1,2,2]{2,1,0:T(2,128)} %param.12) | copy-start | bytes 52
  32.5 4.4 %copy-start.1 = (s32[1,2,2]{2,1,0:T(2,128)S(1)}, s32[1,2,2]{2,1,0:T(2,128)}, u32[]{:S(2)}) copy-start(s32[1,2,2]{2,1,0:T(2,128)} %param.11) | copy-start | bytes 52
  32.5 4.4 %copy-start.2 = (f32[1,2,2]{2,1,0:T(2,128)S(1)}, f32[1,2,2]{2,1,0:T(2,128)}, u32[]{:S(2)}) copy-start(f32[1,2,2]{2,1,0:T(2,128)} %param.15) | copy-start | bytes 52
  32.5 4.4 %copy-start.3 = (s32[1,2,2]{2,1,0:T(2,128)S(1)}, s32[1,2,2]{2,1,0:T(2,128)}, u32[]{:S(2)}) copy-start(s32[1,2,2]{2,1,0:T(2,128)} %param.14) | copy-start | bytes 52
  37.1 1.7 %collective-permute-start.8 = (f32[4,4]{1,0:T(4,128)S(1)}, f32[4,4]{1,0:T(4,128)S(1)}, u32[]{:S(2)}, u32[]{:S(2)}) collective-permute-start(f32[4,4]{1,0:T(4,128)S(1)} %pad_maximum_fusion.1), channel_id=1, source_target_pairs={{0,8},{8,0},{16,24},{24,16},{1,9},{9,1},{17,25},{25,17},{2,10},{10... | collective-permute-start | bytes 200 | tf_op jit(solution)/shard_map/ppermute | solution.py:20
  37.5 5.8 %collective-permute-start.10 = (bf16[96,896]{1,0:T(8,128)(2,1)S(1)}, bf16[96,896]{1,0:T(8,128)(2,1)S(1)}, u32[]{:S(2)}, u32[]{:S(2)}) collective-permute-start(bf16[96,896]{1,0:T(8,128)(2,1)S(1)} %get-tuple-element.32), channel_id=1, source_target_pairs={{0,1},{1,0},{2,3},{3,2},{4,5},{5,4},{6,7},{7,6},{8,9},{9,8},{10,11... | collective-permute-start | bytes 516104 | tf_op jit(solution)/shard_map/ppermute | solution.py:34
  38.8 2.8 %collective-permute-start.9 = (f32[2,4]{1,0:T(2,128)S(1)}, f32[2,4]{1,0:T(2,128)S(1)}, u32[]{:S(2)}, u32[]{:S(2)}) collective-permute-start(f32[2,4]{1,0:T(2,128)S(1)} %get-tuple-element.53), channel_id=1, source_target_pairs={{0,16},{1,17},{2,18},{3,19},{4,20},{5,21},{6,22},{7,23},{8,24},{9,... | collective-permute-start | bytes 104 | tf_op jit(solution)/shard_map/ppermute | solution.py:42
  43.4 4.3 %collective-permute-start.11 = (bf16[24,896]{1,0:T(8,128)(2,1)S(1)}, bf16[24,896]{1,0:T(8,128)(2,1)S(1)}, u32[]{:S(2)}, u32[]{:S(2)}) collective-permute-start(bf16[24,896]{1,0:T(8,128)(2,1)S(1)} %get-tuple-element.37), channel_id=1, source_target_pairs={{0,4},{1,5},{2,6},{3,7},{4,0},{5,1},{6,2},{7,3},{8,12},{9,13},{10,... | collective-permute-start | bytes 129032 | tf_op jit(solution)/shard_map/ppermute | solution.py:34
  45.5 3.4 %collective-permute-start.12 = (bf16[24,896]{1,0:T(8,128)(2,1)S(1)}, bf16[24,896]{1,0:T(8,128)(2,1)S(1)}, u32[]{:S(2)}, u32[]{:S(2)}) collective-permute-start(bf16[24,896]{1,0:T(8,128)(2,1)S(1)} %get-tuple-element.38), channel_id=1, source_target_pairs={{0,2},{1,3},{2,0},{3,1},{4,6},{5,7},{6,4},{7,5},{8,10},{9,11},{10,... | collective-permute-start | bytes 129032 | tf_op jit(solution)/shard_map/ppermute | solution.py:34
  45.7 4.9 %collective-permute-start.13 = (bf16[24,896]{1,0:T(8,128)(2,1)S(1)}, bf16[24,896]{1,0:T(8,128)(2,1)S(1)}, u32[]{:S(2)}, u32[]{:S(2)}) collective-permute-start(bf16[24,896]{1,0:T(8,128)(2,1)S(1)} %get-tuple-element.39), channel_id=1, source_target_pairs={{0,6},{1,7},{2,4},{3,5},{4,2},{5,3},{6,0},{7,1},{8,14},{9,15},{10,... | collective-permute-start | bytes 129032 | tf_op jit(solution)/shard_map/ppermute | solution.py:34
  51.3 3.4 %collective-permute-start.14 = (bf16[16,896]{1,0:T(8,128)(2,1)S(1)}, bf16[16,896]{1,0:T(8,128)(2,1)S(1)}, u32[]{:S(2)}, u32[]{:S(2)}) collective-permute-start(bf16[16,896]{1,0:T(8,128)(2,1)S(1)} %get-tuple-element.41), channel_id=1, source_target_pairs={{0,8},{8,0},{16,24},{24,16},{1,9},{9,1},{17,25},{25,17},{2,10},{10... | collective-permute-start | bytes 86024 | tf_op jit(solution)/shard_map/ppermute | solution.py:20

commit v5 on v4

--- a/solution.py
+++ b/solution.py
@@ -117,62 +117,75 @@
     return one_hot(BATCH * size, want)
 
 
-def fetch_kernel(steps, axis, order, place, weight, earlier, held, turned, zero, *rest):
-    sems = rest[-1]
-    size = held.shape[axis] // steps
-    base = place[0] * held.shape[axis]
-
-    def at(start):
-        rows = pl.ds(pl.multiple_of(start, 128), size)
-        return rows if axis == 0 else (slice(None), rows)
-
-    copies = [
-        pltpu.make_async_copy(
-            weight.at[at(base + i * size)], held.at[at(i * size)], sems.at[i]
-        )
-        for i in range(steps)
-    ]
+class Piece(typing.NamedTuple):
+    weight: int
+    axis: int
+    start: int
+    size: int
+    steps: int
+
+
+def fetch_kernel(pieces, order, place, *refs):
+    count = 1 + max(piece.weight for piece in pieces)
+    weights, refs = refs[:count], refs[count + 1 :]
+    *outs, zero, made, sems = refs
+    copies = []
+    for i, piece in enumerate(pieces):
+        weight, held = weights[piece.weight], outs[2 * i]
+        half = weight.shape[piece.axis] // 2
+        size = piece.size // piece.steps
+        for step in range(piece.steps):
+            start = place[0] * half + piece.start + step * size
+            there = pl.ds(pl.multiple_of(start, 128), size)
+            here = pl.ds(step * size, size)
+            if piece.axis == 1:
+                there, here = (slice(None), there), (slice(None), here)
+            sem = sems.at[len(copies)]
+            copies.append(pltpu.make_async_copy(weight.at[there], held.at[here], sem))
     for copy in copies:
         copy.start()
-    if order is not None:
-        rest[0][...] = order(place)
-    for i, copy in enumerate(copies):
-        copy.wait()
-        here = slice(i * size, (i + 1) * size)
-        if axis == 0:
-            turned[:, here] = held[here, :].T
-        else:
-            turned[here, :] = held[:, here].T
     zero[...] = jnp.zeros_like(zero)
-
-
-def fetch(place, weight, axis, earlier, like, order=None, count=0):
-    steps = 4
-    shape = list(weight.shape)
-    shape[axis] //= 2
+    made[...] = order(place)
+    copies = iter(copies)
+    for i, piece in enumerate(pieces):
+        held, turned = outs[2 * i : 2 * i + 2]
+        size = piece.size // piece.steps
+        for step in range(piece.steps):
+            next(copies).wait()
+            here = slice(step * size, (step + 1) * size)
+            if piece.axis == 0:
+                turned[:, here] = held[here, :].T
+            else:
+                turned[here, :] = held[:, here].T
+
+
+def fetch(place, weights, pieces, earlier, like, order, count):
+    shapes = []
+    for piece in pieces:
+        shape = list(weights[piece.weight].shape)
+        shape[piece.axis] = piece.size
+        shapes += [tuple(shape), tuple(shape[::-1])]
+    nbytes = sum(piece.size for piece in pieces) * weights[0].shape[1] * 4
+    steps = sum(piece.steps for piece in pieces)
     return pl.pallas_call(
-        functools.partial(fetch_kernel, steps, axis, order),
-        in_specs=[
-            pl.BlockSpec(memory_space=pltpu.SMEM),
-            pl.BlockSpec(memory_space=pltpu.HBM),
-            pl.BlockSpec(memory_space=pl.ANY),
-        ],
-        out_specs=[pl.BlockSpec(memory_space=pltpu.VMEM)] * (3 + (count > 0)),
-        out_shape=[
-            pltpu.VMEM(tuple(shape), BF16),
-            pltpu.VMEM(tuple(shape[::-1]), BF16),
-            jax.ShapeDtypeStruct(like, BF16),
-            pltpu.VMEM((count, count), BF16),
-        ][: 3 + (count > 0)],
+        functools.partial(fetch_kernel, pieces, order),
+        in_specs=[pl.BlockSpec(memory_space=pltpu.SMEM)]
+        + [pl.BlockSpec(memory_space=pltpu.HBM)] * len(weights)
+        + [pl.BlockSpec(memory_space=pl.ANY)],
+        out_specs=[pl.BlockSpec(memory_space=pltpu.VMEM)] * (len(shapes) + 2),
+        out_shape=[pltpu.VMEM(shape, BF16) for shape in shapes]
+        + [jax.ShapeDtypeStruct(like, BF16), pltpu.VMEM((count, count), BF16)],
         scratch_shapes=[pltpu.SemaphoreType.DMA((steps,))],
         compiler_params=pltpu.CompilerParams(vmem_limit_bytes=2**21),
-        cost_estimate=pl.CostEstimate(
-            flops=0, bytes_accessed=weight.size * 4, transcendentals=0
-        ),
-    )(place, pltpu.with_memory_space_constraint(weight, pltpu.HBM), earlier)
-
-
-def up_kernel(plan, ranks, order, first, second, third, fourth, g, u, d_t, out):
+        cost_estimate=pl.CostEstimate(flops=0, bytes_accessed=nbytes, transcendentals=0),
+    )(
+        place,
+        *[pltpu.with_memory_space_constraint(weight, pltpu.HBM) for weight in weights],
+        earlier,
+    )
+
+
+def up_kernel(plan, ranks, order, first, second, third, fourth, g, u_low, u_high, d_t, out):
     hid = g.shape[1]
     n = 2 * BATCH
     kinds = len(plan.places)
@@ -192,7 +205,8 @@
         taken = [jnp.concatenate([rows[i : i + n] for rows in sorted_rows]) for i in at]
         rows = jnp.concatenate(taken[:groups])
         a += dot(rows, g[cols, :])
-        b += dot(rows, u[cols, :])
+        u = u_high[(part - 1) * piece : part * piece, :] if part else u_low[...]
+        b += dot(rows, u)
         dh += dot(jnp.concatenate(taken[groups:]), d_t[cols, :])
     n = n * batches
     for i in range(groups):
@@ -203,7 +217,7 @@
         out[:, at : at + hid] = dh[i * n : (i + 1) * n]
 
 
-def down_kernel(plan, ranks, place, order, mine, theirs, g_t, u_t, d, kept, sent):
+def down_kernel(plan, ranks, place, order, mine, theirs, g_t, u_t_low, u_t_high, d, kept, sent):
     hid = d.shape[0]
     groups = plan.fwd + plan.both + plan.bwd
     n = 2 * ranks
@@ -230,7 +244,8 @@
     for part in range(PARTS):
         cols = slice(part * piece, (part + 1) * piece)
         y = dot(h, d[:, cols])
-        dx = dot(da, g_t[:, cols]) + dot(du, u_t[:, cols])
+        u_t = u_t_high[:, (part - 1) * piece : part * piece] if part else u_t_low[...]
+        dx = dot(da, g_t[:, cols]) + dot(du, u_t)
         shared = plan.both * n
         rows = [y[:split], y[split:] + dx[:shared], dx[shared:]] if shared else [y, dx]
         results.append(jnp.concatenate(rows).astype(BF16))
@@ -343,7 +358,16 @@
     far_top = to_next_chips(far_fwd, far_bwd, top)
     blocks = jnp.concatenate([near, *far, swap_ranks(near, top), *far_top])
     offsets = [0, top]
-    g, g_t, zero = fetch(place, w_gate, 0, near, blocks.shape)
+    piece = half // PARTS
+    g, g_t, u_low, u_t_low, zero, back_order = fetch(
+        place,
+        (w_gate, w_up),
+        (Piece(0, 0, 0, half, 4), Piece(1, 0, 0, piece, 1)),
+        near,
+        blocks.shape,
+        lambda _: returned_order(groups),
+        BATCH * PARTS * groups * 2,
+    )
     blocks = blocks + zero
     bit = top // 2
     while bit > 2:
@@ -351,24 +375,14 @@
         offsets += [o ^ bit for o in offsets]
         bit //= 2
     offsets += [o ^ 2 for o in offsets]
+    fourth = swap_ranks(blocks, 3)
     second = swap_ranks(blocks, 2)
     third = swap_ranks(blocks, 1)
-    u, u_t, zero, back_order = fetch(
+    u_high, u_t_high, d, d_t, _, got_order = fetch(
         place,
-        w_up,
-        0,
+        (w_up, w_down),
+        (Piece(0, 0, piece, half - piece, 3), Piece(1, 1, 0, half, 4)),
         blocks,
-        second.shape,
-        lambda _: returned_order(groups),
-        BATCH * PARTS * groups * 2,
-    )
-    second = second + zero
-    fourth = swap_ranks(second, 1)
-    d, d_t, _, got_order = fetch(
-        place,
-        w_down,
-        1,
-        second,
         (16, 128),
         lambda place: gathered_order(plan, place[2]),
         BATCH * plan.rows,
@@ -377,14 +391,14 @@
     (mine,) = on_core(
         functools.partial(up_kernel, plan, ranks),
         None,
-        (got_order, blocks, second, third, fourth, g, u, d_t),
+        (got_order, blocks, second, third, fourth, g, u_low, u_high, d_t),
         [((2 * ranks, (groups + len(plan.places)) * hid), F32)],
         3 * hid * half,
     )
     kept, sent = on_core(
         functools.partial(down_kernel, plan, ranks),
         place,
-        (back_order, mine, swap_cores(mine), g_t, u_t, d),
+        (back_order, mine, swap_cores(mine), g_t, u_t_low, u_t_high, d),
         [((ranks // 2 * PARTS * groups * 2, half // PARTS), BF16)] * 2,
         3 * hid * half,
     )
@@ -402,7 +416,9 @@
     pairs = on_core(
         pair_kernel, None, (kept, swap_ranks(sent, 1), weights), [block] * (ranks // 2), half
     )
-    back = [swap_ranks(pair, o) if o else pair for pair, o in zip(pairs, offsets, strict=True)]
+    pairs = dict(zip(offsets, pairs, strict=True))
+    offsets = [0] + sorted(offsets[1:], reverse=True)
+    back = [swap_ranks(pairs[o], o) if o else pairs[o] for o in offsets]
     own, other = on_core(
         functools.partial(finish_kernel, plan, offsets, shards, ranks),
         place,

time: 55.8 us -> 52.7 us (0.944)
  Pallas kernels: 22.8 us -> 20.2 us
  starting transfers between devices: 19.2 us -> 18.4 us
    pallas_call x3 -> x2, Pallas kernels: 13.4 us -> 10.9 us  [fetch(): pl.pallas_call(functools.partial(fetch_kernel, pieces, order), in_specs=[...]
    ppermute x4, starting transfers between devices: 5.33 us -> 4.18 us  [swap_cores(): return lax.ppermute(block, 'section', [(i, i ^ 1) for i in sections])]
  transfers between devices with their start and end apart: 15 -> 15, of which waited for: 8 -> 8; matrix products, arithmetic and copies ran while one was open for 0% -> 0% of each run, Pallas kernels for 24% -> 21%
where the time goes in v5:
time: 52.7 us; the launch traced here: 52.2 us
  Pallas kernels  20.2 us (38%)
  starting transfers between devices  18.4 us (35%)
  waiting for transfers between devices  10.7 us (20%)
  other arithmetic  1.18 us (2%)
  local copies, waits for them, and re-layouts  0.94 us (2%)
  between operations  0.88 us (2%)
    pallas_call x2, Pallas kernels, fetch(): pl.pallas_call(functools.partial(fetch_kernel, pieces, order), in_specs=[...  10.9 us
    pallas_call x4, Pallas kernels, on_core(): pl.pallas_call(kernel, in_specs=specs, out_specs=[pl.BlockSpec(memory_spa...  9.36 us
    ppermute x8, starting transfers between devices, swap_ranks(): return lax.ppermute(block, 'expert', [(i, i ^ bit) for i in ranks])  8.21 us
    ppermute x3, starting transfers between devices, move(): return lax.ppermute(block, ('section', 'expert'), route)  5.98 us
    ppermute x8, waiting for transfers between devices, swap_ranks(): return lax.ppermute(block, 'expert', [(i, i ^ bit) for i in ranks])  5.66 us
    ppermute x4, starting transfers between devices, swap_cores(): return lax.ppermute(block, 'section', [(i, i ^ 1) for i in sections])  4.18 us
    ppermute x4, waiting for transfers between devices, swap_cores(): return lax.ppermute(block, 'section', [(i, i ^ 1) for i in sections])  3.49 us
    ppermute x3, waiting for transfers between devices, move(): return lax.ppermute(block, ('section', 'expert'), route)  1.51 us
  transfers between devices with their start and end apart: 15, of which 8 were waited for; matrix products, arithmetic and copies ran while one was open for 0% of the time, Pallas kernels for 21%

profile of v5, /device:TPU:1, one launch (start us, length us, event | category | flops | bytes accessed | tf_op | source)
XLA Modules:
  0.0 52.2 jit_solution(5373239230351433557)
XLA Ops:
  0.6 0.9 %pad_maximum_fusion = bf16[6,7168]{1,0:T(8,128)(2,1)S(1)} fusion(bf16[2,7168]{1,0:T(2,128)(2,1)} %bitcast.38, bf16[2,7168]{1,0:T(2,128)(2,1)} %bitcast.39, bf16[2,7168]{1,0:T(2,128)(2,1)} %bitcast.40), kind=kLoop, calls=%fused_computation | loop fusion | flops 258048 | bytes 172032 | tf_op jit(solution)/shard_map/concatenate | solution.py:348
  1.5 0.1 collective-permute-start
  1.7 0.1 pad_add_fusion.place
  1.7 1.1 %collective-permute-done = bf16[6,3584]{1,0:T(8,128)(2,1)S(1)} collective-permute-done((bf16[6,3584]{1,0:T(8,128)(2,1)S(1)}, bf16[6,3584]{1,0:T(8,128)(2,1)S(1)}, u32[]{:S(2)}, u32[]{:S(2)}) %collective-permute-start) | collective-permute-done | bytes 43040 | tf_op jit(solution)/shard_map/ppermute | solution.py:20
  3.0 4.5 %collective-permute-start.3 = (bf16[16,896]{1,0:T(8,128)(2,1)S(1)}, bf16[16,896]{1,0:T(8,128)(2,1)S(1)}, u32[]{:S(2)}, u32[]{:S(2)}) collective-permute-start(bf16[16,896]{1,0:T(8,128)(2,1)S(1)} %pad_select_fusion), channel_id=1, source_target_pairs={{0,20},{1,21},{2,22},{3,23},{4,16},{5,17},{6,18},{7,19},{8,28},{9,... | collective-permute-start | bytes 86024 | tf_op jit(solution)/shard_map/ppermute | solution.py:42
  7.5 0.3 collective-permute-start.1
  7.8 0.2 collective-permute-start.2
  8.0 4.8 %shard_map.113 = (bf16[3584,1024]{1,0:T(8,128)(2,1)S(1)}, bf16[1024,3584]{1,0:T(8,128)(2,1)S(1)}, bf16[896,1024]{1,0:T(8,128)(2,1)S(1)}, bf16[1024,896]{1,0:T(8,...) custom-call(s32[3]{0:T(128)S(1)} %pad_add_fusion.place, bf16[7168,1024]{1,0:T(8,128)(2,1)} %refs_0_.2, ...), custom_call_target="tpu_custom_call" | custom-call | bytes 18350080 | tf_op jit(solution)/shard_map/pallas_call | solution.py:170
  12.8 0.0 collective-permute-done.1
  12.8 0.0 collective-permute-done.2
  12.8 0.0 collective-permute-done.3
  12.9 2.3 %collective-permute-start.6 = (bf16[80,896]{1,0:T(8,128)(2,1)S(1)}, bf16[80,896]{1,0:T(8,128)(2,1)S(1)}, u32[]{:S(2)}, u32[]{:S(2)}) collective-permute-start(bf16[80,896]{1,0:T(8,128)(2,1)S(1)} %add.10.refs_2_.first), channel_id=1, source_target_pairs={{0,3},{1,2},{2,1},{3,0},{4,7},{5,6},{6,5},{7,4},{8,11},{9,10},{10,... | collective-permute-start | bytes 430088 | tf_op jit(solution)/shard_map/ppermute | solution.py:34
  15.2 0.2 collective-permute-start.5
  15.4 0.2 collective-permute-start.4
  15.6 6.1 %shard_map.114 = (bf16[2688,1024]{1,0:T(8,128)(2,1)S(1)}, bf16[1024,2688]{1,0:T(8,128)(2,1)S(1)}, bf16[1024,3584]{1,0:T(8,128)(2,1)S(1)}, bf16[3584,1024]{1,0:T(...) custom-call(s32[3]{0:T(128)S(1)} %pad_add_fusion.place, bf16[7168,1024]{1,0:T(8,128)(2,1)} %refs_0_.3, ...), custom_call_target="tpu_custom_call" | custom-call | bytes 25690112 | tf_op jit(solution)/shard_map/pallas_call | solution.py:170
  21.7 0.0 collective-permute-done.6.fourth
  21.7 0.7 %collective-permute-done.5.third = bf16[80,896]{1,0:T(8,128)(2,1)S(1)} collective-permute-done((bf16[80,896]{1,0:T(8,128)(2,1)S(1)}, bf16[80,896]{1,0:T(8,128)(2,1)S(1)}, u32[]{:S(2)}, u32[]{:S(2)}) %collective-permute-start.5) | collective-permute-done | bytes 143392 | tf_op jit(solution)/shard_map/ppermute | solution.py:34
  22.4 0.0 collective-permute-done.4.second
  22.4 4.3 %shard_map.115.mine = f32[16,8192]{1,0:T(8,128)S(1)} custom-call(bf16[320,320]{1,0:T(8,128)(2,1)S(1)} %get-tuple-element.25.order, bf16[80,896]{1,0:T(8,128)(2,1)S(1)} %add.10.refs_2_.first, bf16[80,896]{1,0:T(8,128)(2,1)S(1)} %collective-permute-done.4.second, bf16[80,896]{1,0:T(8,128)(2,1)S(1)} %collective-permute-done.5.third, ...), custom_call_target="tpu_custom_call" | custom-call | flops 5637144576 | bytes 22020096 | tf_op jit(solution)/shard_map/pallas_call | solution.py:309
  26.7 1.2 %collective-permute-start.7 = (f32[16,8192]{1,0:T(8,128)S(1)}, f32[16,8192]{1,0:T(8,128)S(1)}, u32[]{:S(2)}, u32[]{:S(2)}) collective-permute-start(f32[16,8192]{1,0:T(8,128)S(1)} %shard_map.115.mine), channel_id=1, source_target_pairs={{0,8},{8,0},{16,24},{24,16},{1,9},{9,1},{17,25},{25,17},{2,10},{10... | collective-permute-start | bytes 1572872 | tf_op jit(solution)/shard_map/ppermute | solution.py:20
  27.8 1.5 %collective-permute-done.7.theirs = f32[16,8192]{1,0:T(8,128)S(1)} collective-permute-done((f32[16,8192]{1,0:T(8,128)S(1)}, f32[16,8192]{1,0:T(8,128)S(1)}, u32[]{:S(2)}, u32[]{:S(2)}) %collective-permute-start.7) | collective-permute-done | bytes 524320 | tf_op jit(solution)/shard_map/ppermute | solution.py:20
  29.4 0.0 copy-start
  29.4 0.0 copy-start.1
  29.4 0.0 copy-start.2
  29.4 0.0 copy-start.3
  29.4 4.3 %shard_map.116 = (bf16[96,896]{1,0:T(8,128)(2,1)S(1)}, bf16[96,896]{1,0:T(8,128)(2,1)S(1)}) custom-call(s32[3]{0:T(128)S(1)} %pad_add_fusion.place, bf16[192,192]{1,0:T(8,128)(2,1)S(1)} %get-tuple-element.23.order, f32[16,8192]{1,0:T(8,128)S(1)} %shard_map.115.mine, f32[16,8192]{1,0:T(8,128)S(1)} %collective-permute-done.7.theirs, ...), custom_call_target="tpu_custom_call" | custom-call | flops 5637144576 | bytes 22020096 | tf_op jit(solution)/shard_map/pallas_call | solution.py:309
  33.7 0.0 copy-done
  33.7 0.0 copy-done.1
  33.7 0.0 copy-done.2
  33.8 0.0 copy-done.3
  33.8 0.1 fusion
  33.9 0.4 collective-permute-start.8
  34.3 1.4 %collective-permute-start.10 = (bf16[96,896]{1,0:T(8,128)(2,1)S(1)}, bf16[96,896]{1,0:T(8,128)(2,1)S(1)}, u32[]{:S(2)}, u32[]{:S(2)}) collective-permute-start(bf16[96,896]{1,0:T(8,128)(2,1)S(1)} %get-tuple-element.34), channel_id=1, source_target_pairs={{0,1},{1,0},{2,3},{3,2},{4,5},{5,4},{6,7},{7,6},{8,9},{9,8},{10,11... | collective-permute-start | bytes 516104 | tf_op jit(solution)/shard_map/ppermute | solution.py:34
  35.7 0.0 collective-permute-done.8
  35.7 1.3 %collective-permute-start.9 = (f32[2,4]{1,0:T(2,128)S(1)}, f32[2,4]{1,0:T(2,128)S(1)}, u32[]{:S(2)}, u32[]{:S(2)}) collective-permute-start(f32[2,4]{1,0:T(2,128)S(1)} %get-tuple-element.55), channel_id=1, source_target_pairs={{0,16},{1,17},{2,18},{3,19},{4,20},{5,21},{6,22},{7,23},{8,24},{9,... | collective-permute-start | bytes 104 | tf_op jit(solution)/shard_map/ppermute | solution.py:42
  37.0 1.5 %collective-permute-done.9 = f32[2,4]{1,0:T(2,128)S(1)} collective-permute-done((f32[2,4]{1,0:T(2,128)S(1)}, f32[2,4]{1,0:T(2,128)S(1)}, u32[]{:S(2)}, u32[]{:S(2)}) %collective-permute-start.9) | collective-permute-done | bytes 64 | tf_op jit(solution)/shard_map/ppermute | solution.py:42
  38.5 0.1 concatenate.28.weights
  38.6 1.6 %collective-permute-done.10.got = bf16[96,896]{1,0:T(8,128)(2,1)S(1)} collective-permute-done((bf16[96,896]{1,0:T(8,128)(2,1)S(1)}, bf16[96,896]{1,0:T(8,128)(2,1)S(1)}, u32[]{:S(2)}, u32[]{:S(2)}) %collective-permute-start.10) | collective-permute-done | bytes 172064 | tf_op jit(solution)/shard_map/ppermute | solution.py:34
  40.2 3.6 %collective-permute-start.11 = (bf16[24,896]{1,0:T(8,128)(2,1)S(1)}, bf16[24,896]{1,0:T(8,128)(2,1)S(1)}, u32[]{:S(2)}, u32[]{:S(2)}) collective-permute-start(bf16[24,896]{1,0:T(8,128)(2,1)S(1)} %get-tuple-element.39), channel_id=1, source_target_pairs={{0,6},{1,7},{2,4},{3,5},{4,2},{5,3},{6,0},{7,1},{8,14},{9,15},{10,... | collective-permute-start | bytes 129032 | tf_op jit(solution)/shard_map/ppermute | solution.py:34
  43.8 0.0 collective-permute-start.12
  43.8 0.4 collective-permute-start.13
  44.1 1.1 %collective-permute-done.11.refs_1_ = bf16[24,896]{1,0:T(8,128)(2,1)S(1)} collective-permute-done((bf16[24,896]{1,0:T(8,128)(2,1)S(1)}, bf16[24,896]{1,0:T(8,128)(2,1)S(1)}, u32[]{:S(2)}, u32[]{:S(2)}) %collective-permute-start.11) | collective-permute-done | bytes 43040 | tf_op jit(solution)/shard_map/ppermute | solution.py:34
  45.2 2.4 %collective-permute-done.12.refs_2_ = bf16[24,896]{1,0:T(8,128)(2,1)S(1)} collective-permute-done((bf16[24,896]{1,0:T(8,128)(2,1)S(1)}, bf16[24,896]{1,0:T(8,128)(2,1)S(1)}, u32[]{:S(2)}, u32[]{:S(2)}) %collective-permute-start.12) | collective-permute-done | bytes 43040 | tf_op jit(solution)/shard_map/ppermute | solution.py:34
  47.5 0.0 collective-permute-done.13.refs_3_
  47.5 0.7 %shard_map.118 = (bf16[16,896]{1,0:T(8,128)(2,1)S(1)}, bf16[16,896]{1,0:T(8,128)(2,1)S(1)}) custom-call(s32[3]{0:T(128)S(1)} %pad_add_fusion.place, f32[24,4]{1,0:T(8,128)S(1)} %concatenate.28.weights, bf16[24,896]{1,0:T(8,128)(2,1)S(1)} %get-tuple-element.38.refs_0_, bf16[24,896]{1,0:T(8,128)(2,1)S(1)} %collective-permute-done.11.refs_1_, ...), custom_call_target="tpu_custom_call" | custom-call | flops 1835008 | bytes 7168 | tf_op jit(solution)/shard_map/pallas_call | solution.py:309
  48.2 2.4 %collective-permute-start.14 = (bf16[16,896]{1,0:T(8,128)(2,1)S(1)}, bf16[16,896]{1,0:T(8,128)(2,1)S(1)}, u32[]{:S(2)}, u32[]{:S(2)}) collective-permute-start(bf16[16,896]{1,0:T(8,128)(2,1)S(1)} %get-tuple-element.43), channel_id=1, source_target_pairs={{0,8},{8,0},{16,24},{24,16},{1,9},{9,1},{17,25},{25,17},{2,10},{10... | collective-permute-start | bytes 86024 | tf_op jit(solution)/shard_map/ppermute | solution.py:20
  50.7 0.8 %collective-permute-done.14 = bf16[16,896]{1,0:T(8,128)(2,1)S(1)} collective-permute-done((bf16[16,896]{1,0:T(8,128)(2,1)S(1)}, bf16[16,896]{1,0:T(8,128)(2,1)S(1)}, u32[]{:S(2)}, u32[]{:S(2)}) %collective-permute-start.14) | collective-permute-done | bytes 28704 | tf_op jit(solution)/shard_map/ppermute | solution.py:20
  51.6 0.7 %slice_bitcast_fusion = (bf16[1,2,7168]{2,1,0:T(2,128)(2,1)}, bf16[1,2,7168]{2,1,0:T(2,128)(2,1)}) fusion(bf16[4,7168]{1,0:T(4,128)(2,1)S(1)} %maximum_select_fusion), kind=kLoop, calls=%fused_computation.6 | loop fusion | bytes 114688 | tf_op jit(solution)/shard_map/broadcast_in_dim | solution.py:435
  (24 shorter events, 0.4 us)
Async XLA Ops:
  1.5 1.3 %collective-permute-start = (bf16[6,3584]{1,0:T(8,128)(2,1)S(1)}, bf16[6,3584]{1,0:T(8,128)(2,1)S(1)}, u32[]{:S(2)}, u32[]{:S(2)}) collective-permute-start(bf16[6,3584]{1,0:T(8,128)(2,1)S(1)} %broadcast_select_fusion.2), channel_id=1, source_target_pairs={{0,8},{8,0},{16,24},{24,16},{1,9},{9,1},{17,25},{25,17},{2,10},{10... | collective-permute-start | bytes 129032 | tf_op jit(solution)/shard_map/ppermute | solution.py:20
  3.0 9.8 %collective-permute-start.3 = (bf16[16,896]{1,0:T(8,128)(2,1)S(1)}, bf16[16,896]{1,0:T(8,128)(2,1)S(1)}, u32[]{:S(2)}, u32[]{:S(2)}) collective-permute-start(bf16[16,896]{1,0:T(8,128)(2,1)S(1)} %pad_select_fusion), channel_id=1, source_target_pairs={{0,20},{1,21},{2,22},{3,23},{4,16},{5,17},{6,18},{7,19},{8,28},{9,... | collective-permute-start | bytes 86024 | tf_op jit(solution)/shard_map/ppermute | solution.py:42
  7.5 5.3 %collective-permute-start.1 = (bf16[16,896]{1,0:T(8,128)(2,1)S(1)}, bf16[16,896]{1,0:T(8,128)(2,1)S(1)}, u32[]{:S(2)}, u32[]{:S(2)}) collective-permute-start(bf16[16,896]{1,0:T(8,128)(2,1)S(1)} %pad_select_fusion), channel_id=1, source_target_pairs={{0,16},{1,17},{2,18},{3,19},{4,20},{5,21},{6,22},{7,23},{8,24},{9,... | collective-permute-start | bytes 86024 | tf_op jit(solution)/shard_map/ppermute | solution.py:42
  7.8 5.0 %collective-permute-start.2 = (bf16[24,896]{1,0:T(8,128)(2,1)S(1)}, bf16[24,896]{1,0:T(8,128)(2,1)S(1)}, u32[]{:S(2)}, u32[]{:S(2)}) collective-permute-start(bf16[24,896]{1,0:T(8,128)(2,1)S(1)} %get-tuple-element.49.refs_2_), channel_id=1, source_target_pairs={{0,4},{1,5},{2,6},{3,7},{4,0},{5,1},{6,2},{7,3},{8,12},{9,13},{10,... | collective-permute-start | bytes 129032 | tf_op jit(solution)/shard_map/ppermute | solution.py:34
  12.9 8.8 %collective-permute-start.6 = (bf16[80,896]{1,0:T(8,128)(2,1)S(1)}, bf16[80,896]{1,0:T(8,128)(2,1)S(1)}, u32[]{:S(2)}, u32[]{:S(2)}) collective-permute-start(bf16[80,896]{1,0:T(8,128)(2,1)S(1)} %add.10.refs_2_.first), channel_id=1, source_target_pairs={{0,3},{1,2},{2,1},{3,0},{4,7},{5,6},{6,5},{7,4},{8,11},{9,10},{10,... | collective-permute-start | bytes 430088 | tf_op jit(solution)/shard_map/ppermute | solution.py:34
  15.2 7.2 %collective-permute-start.5 = (bf16[80,896]{1,0:T(8,128)(2,1)S(1)}, bf16[80,896]{1,0:T(8,128)(2,1)S(1)}, u32[]{:S(2)}, u32[]{:S(2)}) collective-permute-start(bf16[80,896]{1,0:T(8,128)(2,1)S(1)} %add.10.refs_2_.first), channel_id=1, source_target_pairs={{0,1},{1,0},{2,3},{3,2},{4,5},{5,4},{6,7},{7,6},{8,9},{9,8},{10,11... | collective-permute-start | bytes 430088 | tf_op jit(solution)/shard_map/ppermute | solution.py:34
  15.4 6.9 %collective-permute-start.4 = (bf16[80,896]{1,0:T(8,128)(2,1)S(1)}, bf16[80,896]{1,0:T(8,128)(2,1)S(1)}, u32[]{:S(2)}, u32[]{:S(2)}) collective-permute-start(bf16[80,896]{1,0:T(8,128)(2,1)S(1)} %add.10.refs_2_.first), channel_id=1, source_target_pairs={{0,2},{1,3},{2,0},{3,1},{4,6},{5,7},{6,4},{7,5},{8,10},{9,11},{10,... | collective-permute-start | bytes 430088 | tf_op jit(solution)/shard_map/ppermute | solution.py:34
  26.7 2.7 %collective-permute-start.7 = (f32[16,8192]{1,0:T(8,128)S(1)}, f32[16,8192]{1,0:T(8,128)S(1)}, u32[]{:S(2)}, u32[]{:S(2)}) collective-permute-start(f32[16,8192]{1,0:T(8,128)S(1)} %shard_map.115.mine), channel_id=1, source_target_pairs={{0,8},{8,0},{16,24},{24,16},{1,9},{9,1},{17,25},{25,17},{2,10},{10... | collective-permute-start | bytes 1572872 | tf_op jit(solution)/shard_map/ppermute | solution.py:20
  29.4 4.4 %copy-start = (f32[1,2,2]{2,1,0:T(2,128)S(1)}, f32[1,2,2]{2,1,0:T(2,128)}, u32[]{:S(2)}) copy-start(f32[1,2,2]{2,1,0:T(2,128)} %param.12) | copy-start | bytes 52
  29.4 4.4 %copy-start.1 = (s32[1,2,2]{2,1,0:T(2,128)S(1)}, s32[1,2,2]{2,1,0:T(2,128)}, u32[]{:S(2)}) copy-start(s32[1,2,2]{2,1,0:T(2,128)} %param.11) | copy-start | bytes 52
  29.4 4.4 %copy-start.2 = (f32[1,2,2]{2,1,0:T(2,128)S(1)}, f32[1,2,2]{2,1,0:T(2,128)}, u32[]{:S(2)}) copy-start(f32[1,2,2]{2,1,0:T(2,128)} %param.15) | copy-start | bytes 52
  29.4 4.4 %copy-start.3 = (s32[1,2,2]{2,1,0:T(2,128)S(1)}, s32[1,2,2]{2,1,0:T(2,128)}, u32[]{:S(2)}) copy-start(s32[1,2,2]{2,1,0:T(2,128)} %param.14) | copy-start | bytes 52
  33.9 1.9 %collective-permute-start.8 = (f32[4,4]{1,0:T(4,128)S(1)}, f32[4,4]{1,0:T(4,128)S(1)}, u32[]{:S(2)}, u32[]{:S(2)}) collective-permute-start(f32[4,4]{1,0:T(4,128)S(1)} %pad_maximum_fusion.1), channel_id=1, source_target_pairs={{0,8},{8,0},{16,24},{24,16},{1,9},{9,1},{17,25},{25,17},{2,10},{10... | collective-permute-start | bytes 200 | tf_op jit(solution)/shard_map/ppermute | solution.py:20
  34.3 5.8 %collective-permute-start.10 = (bf16[96,896]{1,0:T(8,128)(2,1)S(1)}, bf16[96,896]{1,0:T(8,128)(2,1)S(1)}, u32[]{:S(2)}, u32[]{:S(2)}) collective-permute-start(bf16[96,896]{1,0:T(8,128)(2,1)S(1)} %get-tuple-element.34), channel_id=1, source_target_pairs={{0,1},{1,0},{2,3},{3,2},{4,5},{5,4},{6,7},{7,6},{8,9},{9,8},{10,11... | collective-permute-start | bytes 516104 | tf_op jit(solution)/shard_map/ppermute | solution.py:34
  35.7 2.8 %collective-permute-start.9 = (f32[2,4]{1,0:T(2,128)S(1)}, f32[2,4]{1,0:T(2,128)S(1)}, u32[]{:S(2)}, u32[]{:S(2)}) collective-permute-start(f32[2,4]{1,0:T(2,128)S(1)} %get-tuple-element.55), channel_id=1, source_target_pairs={{0,16},{1,17},{2,18},{3,19},{4,20},{5,21},{6,22},{7,23},{8,24},{9,... | collective-permute-start | bytes 104 | tf_op jit(solution)/shard_map/ppermute | solution.py:42
  40.2 5.0 %collective-permute-start.11 = (bf16[24,896]{1,0:T(8,128)(2,1)S(1)}, bf16[24,896]{1,0:T(8,128)(2,1)S(1)}, u32[]{:S(2)}, u32[]{:S(2)}) collective-permute-start(bf16[24,896]{1,0:T(8,128)(2,1)S(1)} %get-tuple-element.39), channel_id=1, source_target_pairs={{0,6},{1,7},{2,4},{3,5},{4,2},{5,3},{6,0},{7,1},{8,14},{9,15},{10,... | collective-permute-start | bytes 129032 | tf_op jit(solution)/shard_map/ppermute | solution.py:34
  43.8 3.8 %collective-permute-start.12 = (bf16[24,896]{1,0:T(8,128)(2,1)S(1)}, bf16[24,896]{1,0:T(8,128)(2,1)S(1)}, u32[]{:S(2)}, u32[]{:S(2)}) collective-permute-start(bf16[24,896]{1,0:T(8,128)(2,1)S(1)} %get-tuple-element.40), channel_id=1, source_target_pairs={{0,4},{1,5},{2,6},{3,7},{4,0},{5,1},{6,2},{7,3},{8,12},{9,13},{10,... | collective-permute-start | bytes 129032 | tf_op jit(solution)/shard_map/ppermute | solution.py:34
  43.8 3.8 %collective-permute-start.13 = (bf16[24,896]{1,0:T(8,128)(2,1)S(1)}, bf16[24,896]{1,0:T(8,128)(2,1)S(1)}, u32[]{:S(2)}, u32[]{:S(2)}) collective-permute-start(bf16[24,896]{1,0:T(8,128)(2,1)S(1)} %get-tuple-element.41), channel_id=1, source_target_pairs={{0,2},{1,3},{2,0},{3,1},{4,6},{5,7},{6,4},{7,5},{8,10},{9,11},{10,... | collective-permute-start | bytes 129032 | tf_op jit(solution)/shard_map/ppermute | solution.py:34
  48.2 3.3 %collective-permute-start.14 = (bf16[16,896]{1,0:T(8,128)(2,1)S(1)}, bf16[16,896]{1,0:T(8,128)(2,1)S(1)}, u32[]{:S(2)}, u32[]{:S(2)}) collective-permute-start(bf16[16,896]{1,0:T(8,128)(2,1)S(1)} %get-tuple-element.43), channel_id=1, source_target_pairs={{0,8},{8,0},{16,24},{24,16},{1,9},{9,1},{17,25},{25,17},{2,10},{10... | collective-permute-start | bytes 86024 | tf_op jit(solution)/shard_map/ppermute | solution.py:20

commit v6 on v5

--- a/solution.py
+++ b/solution.py
@@ -273,30 +273,39 @@
         pair[...] = (kept[rows].astype(F32) + got[rows].astype(F32)).astype(BF16)
 
 
-def finish_kernel(plan, offsets, shards, ranks, place, weights, *refs):
-    *back, own, other = refs
-    total = 0.0
-    for offset, block in zip(offsets, back, strict=True):
+def select_kernel(plan, offsets, shards, place, weights, columns, chosen):
+    size = weights.shape[0]
+    for i, offset in enumerate(offsets):
         expert = lax.div(lax.bitwise_xor(place[1], jnp.int32(offset)), jnp.int32(shards))
         named = lax.broadcasted_iota(jnp.int32, weights.shape, 1) == expert
         weight = jnp.sum(jnp.where(named, weights[...], 0.0), axis=1, keepdims=True)
-        total += block[...].astype(F32) * weight
-    forward = jnp.where(place[2] == 1, 1.0, 0.0)
-    size = 2 * (plan.fwd + plan.both + plan.bwd)
-    even, odd = [], []
-    for part in range(PARTS):
-        rows = [total[i : i + 2] for i in range(part * size, (part + 1) * size, 2)]
-        if plan.both:
-            fwd, far, bwd = rows
-            even += [far * forward, bwd]
-            odd += [fwd, far * (1.0 - forward)]
-        else:
-            fwd, far_fwd, bwd, far_bwd = rows
-            even += [far_fwd, bwd]
-            odd += [fwd, far_bwd]
-    even, odd = jnp.concatenate(even), jnp.concatenate(odd)
-    own[...] = jnp.where(place[0] == 0, even, odd).astype(BF16)
-    other[...] = jnp.where(place[0] == 0, odd, even).astype(BF16)
+        columns[i * size : (i + 1) * size, :] = jnp.broadcast_to(weight, (size, 128))
+    out = lax.broadcasted_iota(jnp.int32, chosen.shape, 0)
+    src = lax.broadcasted_iota(jnp.int32, chosen.shape, 1)
+    odd = jnp.where(out < 4 * PARTS, place[0], 1 - place[0])
+    part, row = lax.rem(lax.div(out, 4), PARTS), lax.rem(out, 4)
+    bwd = lax.div(row, 2)
+    if plan.both:
+        far = jnp.where(place[2] == 1, 0, 1)
+        group = jnp.where(bwd == odd, 1, 2 * bwd)
+        present = (bwd != odd) | (bwd == far)
+    else:
+        group = 2 * bwd + jnp.where(bwd == odd, 1, 0)
+        present = out >= 0
+    groups = plan.fwd + plan.both + plan.bwd
+    want = part * (2 * groups) + group * 2 + lax.rem(row, 2)
+    chosen[...] = jnp.where((want == src) & present, 1.0, 0.0).astype(BF16)
+
+
+def finish_kernel(columns, chosen, *refs):
+    *back, own, other = refs
+    size = back[0].shape[0]
+    total = 0.0
+    for i, block in enumerate(back):
+        total += block[...].astype(F32) * columns[i * size : (i + 1) * size, :1]
+    rows = dot(chosen[...], total.astype(BF16)).astype(BF16)
+    own[...] = rows[: own.shape[0]]
+    other[...] = rows[own.shape[0] :]
 
 
 def on_core(kernel, place, operands, results, cost):
@@ -345,9 +354,13 @@
     core = section % 2
     place = jnp.stack([core, lax.axis_index("expert"), section >= 2]).astype(jnp.int32)
 
-    rows = jnp.concatenate([fwd_tokens[0], bwd_tokens[0], bwd_grads[0]])
-    keep, send = by_section(rows[:, :half], rows[:, half:], core)
-    even, odd = by_section(keep, swap_cores(send), core)
+    inputs = [fwd_tokens[0], bwd_tokens[0], bwd_grads[0]]
+    theirs = jnp.concatenate([swap_cores(block) for block in inputs])
+    mine = jnp.concatenate(inputs)
+    mine, theirs = (
+        jnp.where(core == 0, rows[:, :half], rows[:, half:]) for rows in (mine, theirs)
+    )
+    even, odd = by_section(mine, theirs, core)
 
     near = jnp.concatenate([folded(even[:2]), folded(odd[2:])])
     far_fwd, far_bwd = folded(odd[:2]), folded(even[2:])
@@ -419,10 +432,17 @@
     pairs = dict(zip(offsets, pairs, strict=True))
     offsets = [0] + sorted(offsets[1:], reverse=True)
     back = [swap_ranks(pairs[o], o) if o else pairs[o] for o in offsets]
+    columns, chosen = on_core(
+        functools.partial(select_kernel, plan, offsets, shards),
+        place,
+        (weights,),
+        [((len(offsets) * weights.shape[0], 128), F32), ((8 * PARTS, weights.shape[0]), BF16)],
+        half,
+    )
     own, other = on_core(
-        functools.partial(finish_kernel, plan, offsets, shards, ranks),
-        place,
-        (weights, *back),
+        finish_kernel,
+        None,
+        (columns, chosen, *back),
         [((4 * PARTS, half // PARTS), BF16)] * 2,
         half,
     )

time: 52.7 us -> 52.1 us (0.989)
  waiting for transfers between devices: 10.7 us -> 9.29 us
    ppermute x4 -> x6, waiting for transfers between devices: 3.49 us -> 2.74 us  [swap_cores(): return lax.ppermute(block, 'section', [(i, i ^ 1) for i in sections])]
    ppermute x8, waiting for transfers between devices: 5.66 us -> 5.04 us  [swap_ranks(): return lax.ppermute(block, 'expert', [(i, i ^ bit) for i in ranks])]
    ppermute x4 -> x6, starting transfers between devices: 4.18 us -> 4.7 us  [swap_cores(): return lax.ppermute(block, 'section', [(i, i ^ 1) for i in sections])]
    pallas_call x4 -> x5, Pallas kernels: 9.36 us -> 9.54 us  [on_core(): pl.pallas_call(kernel, in_specs=specs, out_specs=[pl.BlockSpec(memory_spa...]
  transfers between devices with their start and end apart: 15 -> 17, of which waited for: 8 -> 8; matrix products, arithmetic and copies ran while one was open for 0% -> 2% of each run, Pallas kernels for 21% -> 22%
where the time goes in v6:
time: 52.1 us; the launch traced here: 51.7 us
  Pallas kernels  20.4 us (39%)
  starting transfers between devices  18.9 us (36%)
  waiting for transfers between devices  9.29 us (18%)
  other arithmetic  1.27 us (2%)
  local copies, waits for them, and re-layouts  0.94 us (2%)
  between operations  0.88 us (2%)
    pallas_call x2, Pallas kernels, fetch(): pl.pallas_call(functools.partial(fetch_kernel, pieces, order), in_specs=[...  10.9 us
    pallas_call x5, Pallas kernels, on_core(): pl.pallas_call(kernel, in_specs=specs, out_specs=[pl.BlockSpec(memory_spa...  9.54 us
    ppermute x8, starting transfers between devices, swap_ranks(): return lax.ppermute(block, 'expert', [(i, i ^ bit) for i in ranks])  8.2 us
    ppermute x3, starting transfers between devices, move(): return lax.ppermute(block, ('section', 'expert'), route)  5.99 us
    ppermute x8, waiting for transfers between devices, swap_ranks(): return lax.ppermute(block, 'expert', [(i, i ^ bit) for i in ranks])  5.04 us
    ppermute x6, starting transfers between devices, swap_cores(): return lax.ppermute(block, 'section', [(i, i ^ 1) for i in sections])  4.7 us
    ppermute x6, waiting for transfers between devices, swap_cores(): return lax.ppermute(block, 'section', [(i, i ^ 1) for i in sections])  2.74 us
    ppermute x3, waiting for transfers between devices, move(): return lax.ppermute(block, ('section', 'expert'), route)  1.51 us
  transfers between devices with their start and end apart: 17, of which 8 were waited for; matrix products, arithmetic and copies ran while one was open for 2% of the time, Pallas kernels for 22%

profile of v6, /device:TPU:1, one launch (start us, length us, event | category | flops | bytes accessed | tf_op | source)
XLA Modules:
  0.0 51.7 jit_solution(11661164246141650833)
XLA Ops:
  0.6 0.1 collective-permute-start
  0.8 0.5 collective-permute-start.1
  1.2 0.1 collective-permute-start.2
  1.3 0.9 %pad_maximum_fusion = bf16[6,7168]{1,0:T(8,128)(2,1)S(1)} fusion(bf16[2,7168]{1,0:T(2,128)(2,1)} %bitcast.43, bf16[2,7168]{1,0:T(2,128)(2,1)} %bitcast.41, bf16[2,7168]{1,0:T(2,128)(2,1)} %bitcast.39), kind=kLoop, calls=%fused_computation | loop fusion | flops 258048 | bytes 172032 | tf_op jit(solution)/shard_map/concatenate | solution.py:359
  2.2 0.1 pad_add_fusion.place
  2.3 0.0 collective-permute-done
  2.3 0.0 collective-permute-done.1
  2.3 0.3 collective-permute-done.2
  2.6 0.1 pad_maximum_fusion.1
  2.9 4.5 %collective-permute-start.5 = (bf16[16,896]{1,0:T(8,128)(2,1)S(1)}, bf16[16,896]{1,0:T(8,128)(2,1)S(1)}, u32[]{:S(2)}, u32[]{:S(2)}) collective-permute-start(bf16[16,896]{1,0:T(8,128)(2,1)S(1)} %pad_select_fusion), channel_id=1, source_target_pairs={{0,20},{1,21},{2,22},{3,23},{4,16},{5,17},{6,18},{7,19},{8,28},{9,... | collective-permute-start | bytes 86024 | tf_op jit(solution)/shard_map/ppermute | solution.py:42
  7.4 0.3 collective-permute-start.3
  7.7 0.2 collective-permute-start.4
  7.8 4.8 %shard_map.113 = (bf16[3584,1024]{1,0:T(8,128)(2,1)S(1)}, bf16[1024,3584]{1,0:T(8,128)(2,1)S(1)}, bf16[896,1024]{1,0:T(8,128)(2,1)S(1)}, bf16[1024,896]{1,0:T(8,...) custom-call(s32[3]{0:T(128)S(1)} %pad_add_fusion.place, bf16[7168,1024]{1,0:T(8,128)(2,1)} %refs_0_.2, ...), custom_call_target="tpu_custom_call" | custom-call | bytes 18350080 | tf_op jit(solution)/shard_map/pallas_call | solution.py:170
  12.7 0.0 collective-permute-done.3
  12.7 0.0 collective-permute-done.4
  12.7 0.0 collective-permute-done.5
  12.8 2.3 %collective-permute-start.8 = (bf16[80,896]{1,0:T(8,128)(2,1)S(1)}, bf16[80,896]{1,0:T(8,128)(2,1)S(1)}, u32[]{:S(2)}, u32[]{:S(2)}) collective-permute-start(bf16[80,896]{1,0:T(8,128)(2,1)S(1)} %add.10.refs_2_.first), channel_id=1, source_target_pairs={{0,3},{1,2},{2,1},{3,0},{4,7},{5,6},{6,5},{7,4},{8,11},{9,10},{10,... | collective-permute-start | bytes 430088 | tf_op jit(solution)/shard_map/ppermute | solution.py:34
  15.1 0.2 collective-permute-start.7
  15.3 0.2 collective-permute-start.6
  15.5 6.1 %shard_map.114 = (bf16[2688,1024]{1,0:T(8,128)(2,1)S(1)}, bf16[1024,2688]{1,0:T(8,128)(2,1)S(1)}, bf16[1024,3584]{1,0:T(8,128)(2,1)S(1)}, bf16[3584,1024]{1,0:T(...) custom-call(s32[3]{0:T(128)S(1)} %pad_add_fusion.place, bf16[7168,1024]{1,0:T(8,128)(2,1)} %refs_0_.3, ...), custom_call_target="tpu_custom_call" | custom-call | bytes 25690112 | tf_op jit(solution)/shard_map/pallas_call | solution.py:170
  21.6 0.0 collective-permute-done.8.fourth
  21.6 0.7 %collective-permute-done.7.third = bf16[80,896]{1,0:T(8,128)(2,1)S(1)} collective-permute-done((bf16[80,896]{1,0:T(8,128)(2,1)S(1)}, bf16[80,896]{1,0:T(8,128)(2,1)S(1)}, u32[]{:S(2)}, u32[]{:S(2)}) %collective-permute-start.7) | collective-permute-done | bytes 143392 | tf_op jit(solution)/shard_map/ppermute | solution.py:34
  22.3 0.0 collective-permute-done.6.second
  22.3 4.3 %shard_map.115.mine = f32[16,8192]{1,0:T(8,128)S(1)} custom-call(bf16[320,320]{1,0:T(8,128)(2,1)S(1)} %get-tuple-element.27.order, bf16[80,896]{1,0:T(8,128)(2,1)S(1)} %add.10.refs_2_.first, bf16[80,896]{1,0:T(8,128)(2,1)S(1)} %collective-permute-done.6.second, bf16[80,896]{1,0:T(8,128)(2,1)S(1)} %collective-permute-done.7.third, ...), custom_call_target="tpu_custom_call" | custom-call | flops 5637144576 | bytes 22020096 | tf_op jit(solution)/shard_map/pallas_call | solution.py:318
  26.6 1.2 %collective-permute-start.9 = (f32[16,8192]{1,0:T(8,128)S(1)}, f32[16,8192]{1,0:T(8,128)S(1)}, u32[]{:S(2)}, u32[]{:S(2)}) collective-permute-start(f32[16,8192]{1,0:T(8,128)S(1)} %shard_map.115.mine), channel_id=1, source_target_pairs={{0,8},{8,0},{16,24},{24,16},{1,9},{9,1},{17,25},{25,17},{2,10},{10... | collective-permute-start | bytes 1572872 | tf_op jit(solution)/shard_map/ppermute | solution.py:20
  27.7 1.5 %collective-permute-done.9.theirs = f32[16,8192]{1,0:T(8,128)S(1)} collective-permute-done((f32[16,8192]{1,0:T(8,128)S(1)}, f32[16,8192]{1,0:T(8,128)S(1)}, u32[]{:S(2)}, u32[]{:S(2)}) %collective-permute-start.9) | collective-permute-done | bytes 524320 | tf_op jit(solution)/shard_map/ppermute | solution.py:20
  29.3 4.3 %shard_map.116 = (bf16[96,896]{1,0:T(8,128)(2,1)S(1)}, bf16[96,896]{1,0:T(8,128)(2,1)S(1)}) custom-call(s32[3]{0:T(128)S(1)} %pad_add_fusion.place, bf16[192,192]{1,0:T(8,128)(2,1)S(1)} %get-tuple-element.25.order, f32[16,8192]{1,0:T(8,128)S(1)} %shard_map.115.mine, f32[16,8192]{1,0:T(8,128)S(1)} %collective-permute-done.9.theirs, ...), custom_call_target="tpu_custom_call" | custom-call | flops 5637144576 | bytes 22020096 | tf_op jit(solution)/shard_map/pallas_call | solution.py:318
  33.6 0.0 copy-done
  33.6 0.0 copy-done.1
  33.7 0.1 fusion
  33.8 0.4 collective-permute-start.10
  34.2 1.4 %collective-permute-start.12 = (bf16[96,896]{1,0:T(8,128)(2,1)S(1)}, bf16[96,896]{1,0:T(8,128)(2,1)S(1)}, u32[]{:S(2)}, u32[]{:S(2)}) collective-permute-start(bf16[96,896]{1,0:T(8,128)(2,1)S(1)} %get-tuple-element.36), channel_id=1, source_target_pairs={{0,1},{1,0},{2,3},{3,2},{4,5},{5,4},{6,7},{7,6},{8,9},{9,8},{10,11... | collective-permute-start | bytes 516104 | tf_op jit(solution)/shard_map/ppermute | solution.py:34
  35.6 0.0 collective-permute-done.10
  35.6 1.3 %collective-permute-start.11 = (f32[2,4]{1,0:T(2,128)S(1)}, f32[2,4]{1,0:T(2,128)S(1)}, u32[]{:S(2)}, u32[]{:S(2)}) collective-permute-start(f32[2,4]{1,0:T(2,128)S(1)} %get-tuple-element.59), channel_id=1, source_target_pairs={{0,16},{1,17},{2,18},{3,19},{4,20},{5,21},{6,22},{7,23},{8,24},{9,... | collective-permute-start | bytes 104 | tf_op jit(solution)/shard_map/ppermute | solution.py:42
  36.9 1.5 %collective-permute-done.11 = f32[2,4]{1,0:T(2,128)S(1)} collective-permute-done((f32[2,4]{1,0:T(2,128)S(1)}, f32[2,4]{1,0:T(2,128)S(1)}, u32[]{:S(2)}, u32[]{:S(2)}) %collective-permute-start.11) | collective-permute-done | bytes 64 | tf_op jit(solution)/shard_map/ppermute | solution.py:42
  38.4 0.1 concatenate.32.weights
  38.5 1.6 %collective-permute-done.12.got = bf16[96,896]{1,0:T(8,128)(2,1)S(1)} collective-permute-done((bf16[96,896]{1,0:T(8,128)(2,1)S(1)}, bf16[96,896]{1,0:T(8,128)(2,1)S(1)}, u32[]{:S(2)}, u32[]{:S(2)}) %collective-permute-start.12) | collective-permute-done | bytes 172064 | tf_op jit(solution)/shard_map/ppermute | solution.py:34
  40.1 3.5 %collective-permute-start.13 = (bf16[24,896]{1,0:T(8,128)(2,1)S(1)}, bf16[24,896]{1,0:T(8,128)(2,1)S(1)}, u32[]{:S(2)}, u32[]{:S(2)}) collective-permute-start(bf16[24,896]{1,0:T(8,128)(2,1)S(1)} %get-tuple-element.43), channel_id=1, source_target_pairs={{0,6},{1,7},{2,4},{3,5},{4,2},{5,3},{6,0},{7,1},{8,14},{9,15},{10,... | collective-permute-start | bytes 129032 | tf_op jit(solution)/shard_map/ppermute | solution.py:34
  43.6 0.0 collective-permute-start.14
  43.6 0.4 collective-permute-start.15
  44.0 0.6 %shard_map.117 = (f32[96,128]{1,0:T(8,128)S(1)}, bf16[32,24]{1,0:T(8,128)(2,1)S(1)}) custom-call(s32[3]{0:T(128)S(1)} %pad_add_fusion.place, f32[24,4]{1,0:T(8,128)S(1)} %concatenate.32.weights), custom_call_target="tpu_custom_call" | custom-call | flops 1835008 | bytes 7168 | tf_op jit(solution)/shard_map/pallas_call | solution.py:318
  44.6 0.4 collective-permute-done.13.refs_1_
  45.0 2.4 %collective-permute-done.14.refs_2_ = bf16[24,896]{1,0:T(8,128)(2,1)S(1)} collective-permute-done((bf16[24,896]{1,0:T(8,128)(2,1)S(1)}, bf16[24,896]{1,0:T(8,128)(2,1)S(1)}, u32[]{:S(2)}, u32[]{:S(2)}) %collective-permute-start.14) | collective-permute-done | bytes 43040 | tf_op jit(solution)/shard_map/ppermute | solution.py:34
  47.4 0.0 collective-permute-done.15.refs_3_
  47.4 0.2 shard_map.119
  47.6 2.4 %collective-permute-start.16 = (bf16[16,896]{1,0:T(8,128)(2,1)S(1)}, bf16[16,896]{1,0:T(8,128)(2,1)S(1)}, u32[]{:S(2)}, u32[]{:S(2)}) collective-permute-start(bf16[16,896]{1,0:T(8,128)(2,1)S(1)} %get-tuple-element.47), channel_id=1, source_target_pairs={{0,8},{8,0},{16,24},{24,16},{1,9},{9,1},{17,25},{25,17},{2,10},{10... | collective-permute-start | bytes 86024 | tf_op jit(solution)/shard_map/ppermute | solution.py:20
  50.1 0.8 %collective-permute-done.16 = bf16[16,896]{1,0:T(8,128)(2,1)S(1)} collective-permute-done((bf16[16,896]{1,0:T(8,128)(2,1)S(1)}, bf16[16,896]{1,0:T(8,128)(2,1)S(1)}, u32[]{:S(2)}, u32[]{:S(2)}) %collective-permute-start.16) | collective-permute-done | bytes 28704 | tf_op jit(solution)/shard_map/ppermute | solution.py:20
  51.0 0.7 %slice_bitcast_fusion = (bf16[1,2,7168]{2,1,0:T(2,128)(2,1)}, bf16[1,2,7168]{2,1,0:T(2,128)(2,1)}) fusion(bf16[4,7168]{1,0:T(4,128)(2,1)S(1)} %maximum_select_fusion), kind=kLoop, calls=%fused_computation.7 | loop fusion | bytes 114688 | tf_op jit(solution)/shard_map/broadcast_in_dim | solution.py:455
  (29 shorter events, 0.4 us)
Async XLA Ops:
  0.6 1.6 %collective-permute-start = (bf16[2,7168]{1,0:T(2,128)(2,1)}, bf16[2,7168]{1,0:T(2,128)(2,1)S(1)}, u32[]{:S(2)}, u32[]{:S(2)}) collective-permute-start(bf16[2,7168]{1,0:T(2,128)(2,1)} %bitcast.38), channel_id=1, source_target_pairs={{0,8},{8,0},{16,24},{24,16},{1,9},{9,1},{17,25},{25,17},{2,10},{10... | collective-permute-start | bytes 86024 | tf_op jit(solution)/shard_map/ppermute | solution.py:20
  0.8 1.5 %collective-permute-start.1 = (bf16[2,7168]{1,0:T(2,128)(2,1)}, bf16[2,7168]{1,0:T(2,128)(2,1)S(1)}, u32[]{:S(2)}, u32[]{:S(2)}) collective-permute-start(bf16[2,7168]{1,0:T(2,128)(2,1)} %bitcast.40), channel_id=1, source_target_pairs={{0,8},{8,0},{16,24},{24,16},{1,9},{9,1},{17,25},{25,17},{2,10},{10... | collective-permute-start | bytes 86024 | tf_op jit(solution)/shard_map/ppermute | solution.py:20
  1.2 1.4 %collective-permute-start.2 = (bf16[2,7168]{1,0:T(2,128)(2,1)}, bf16[2,7168]{1,0:T(2,128)(2,1)S(1)}, u32[]{:S(2)}, u32[]{:S(2)}) collective-permute-start(bf16[2,7168]{1,0:T(2,128)(2,1)} %bitcast.42), channel_id=1, source_target_pairs={{0,8},{8,0},{16,24},{24,16},{1,9},{9,1},{17,25},{25,17},{2,10},{10... | collective-permute-start | bytes 86024 | tf_op jit(solution)/shard_map/ppermute | solution.py:20
  2.9 9.8 %collective-permute-start.5 = (bf16[16,896]{1,0:T(8,128)(2,1)S(1)}, bf16[16,896]{1,0:T(8,128)(2,1)S(1)}, u32[]{:S(2)}, u32[]{:S(2)}) collective-permute-start(bf16[16,896]{1,0:T(8,128)(2,1)S(1)} %pad_select_fusion), channel_id=1, source_target_pairs={{0,20},{1,21},{2,22},{3,23},{4,16},{5,17},{6,18},{7,19},{8,28},{9,... | collective-permute-start | bytes 86024 | tf_op jit(solution)/shard_map/ppermute | solution.py:42
  7.4 5.3 %collective-permute-start.3 = (bf16[16,896]{1,0:T(8,128)(2,1)S(1)}, bf16[16,896]{1,0:T(8,128)(2,1)S(1)}, u32[]{:S(2)}, u32[]{:S(2)}) collective-permute-start(bf16[16,896]{1,0:T(8,128)(2,1)S(1)} %pad_select_fusion), channel_id=1, source_target_pairs={{0,16},{1,17},{2,18},{3,19},{4,20},{5,21},{6,22},{7,23},{8,24},{9,... | collective-permute-start | bytes 86024 | tf_op jit(solution)/shard_map/ppermute | solution.py:42
  7.7 5.0 %collective-permute-start.4 = (bf16[24,896]{1,0:T(8,128)(2,1)S(1)}, bf16[24,896]{1,0:T(8,128)(2,1)S(1)}, u32[]{:S(2)}, u32[]{:S(2)}) collective-permute-start(bf16[24,896]{1,0:T(8,128)(2,1)S(1)} %get-tuple-element.53.refs_2_), channel_id=1, source_target_pairs={{0,4},{1,5},{2,6},{3,7},{4,0},{5,1},{6,2},{7,3},{8,12},{9,13},{10,... | collective-permute-start | bytes 129032 | tf_op jit(solution)/shard_map/ppermute | solution.py:34
  12.8 8.8 %collective-permute-start.8 = (bf16[80,896]{1,0:T(8,128)(2,1)S(1)}, bf16[80,896]{1,0:T(8,128)(2,1)S(1)}, u32[]{:S(2)}, u32[]{:S(2)}) collective-permute-start(bf16[80,896]{1,0:T(8,128)(2,1)S(1)} %add.10.refs_2_.first), channel_id=1, source_target_pairs={{0,3},{1,2},{2,1},{3,0},{4,7},{5,6},{6,5},{7,4},{8,11},{9,10},{10,... | collective-permute-start | bytes 430088 | tf_op jit(solution)/shard_map/ppermute | solution.py:34
  15.1 7.2 %collective-permute-start.7 = (bf16[80,896]{1,0:T(8,128)(2,1)S(1)}, bf16[80,896]{1,0:T(8,128)(2,1)S(1)}, u32[]{:S(2)}, u32[]{:S(2)}) collective-permute-start(bf16[80,896]{1,0:T(8,128)(2,1)S(1)} %add.10.refs_2_.first), channel_id=1, source_target_pairs={{0,1},{1,0},{2,3},{3,2},{4,5},{5,4},{6,7},{7,6},{8,9},{9,8},{10,11... | collective-permute-start | bytes 430088 | tf_op jit(solution)/shard_map/ppermute | solution.py:34
  15.3 6.9 %collective-permute-start.6 = (bf16[80,896]{1,0:T(8,128)(2,1)S(1)}, bf16[80,896]{1,0:T(8,128)(2,1)S(1)}, u32[]{:S(2)}, u32[]{:S(2)}) collective-permute-start(bf16[80,896]{1,0:T(8,128)(2,1)S(1)} %add.10.refs_2_.first), channel_id=1, source_target_pairs={{0,2},{1,3},{2,0},{3,1},{4,6},{5,7},{6,4},{7,5},{8,10},{9,11},{10,... | collective-permute-start | bytes 430088 | tf_op jit(solution)/shard_map/ppermute | solution.py:34
  26.6 2.7 %collective-permute-start.9 = (f32[16,8192]{1,0:T(8,128)S(1)}, f32[16,8192]{1,0:T(8,128)S(1)}, u32[]{:S(2)}, u32[]{:S(2)}) collective-permute-start(f32[16,8192]{1,0:T(8,128)S(1)} %shard_map.115.mine), channel_id=1, source_target_pairs={{0,8},{8,0},{16,24},{24,16},{1,9},{9,1},{17,25},{25,17},{2,10},{10... | collective-permute-start | bytes 1572872 | tf_op jit(solution)/shard_map/ppermute | solution.py:20
  29.3 4.4 %copy-start = (f32[1,2,2]{2,1,0:T(2,128)S(1)}, f32[1,2,2]{2,1,0:T(2,128)}, u32[]{:S(2)}) copy-start(f32[1,2,2]{2,1,0:T(2,128)} %param.12) | copy-start | bytes 52
  29.3 4.4 %copy-start.1 = (s32[1,2,2]{2,1,0:T(2,128)S(1)}, s32[1,2,2]{2,1,0:T(2,128)}, u32[]{:S(2)}) copy-start(s32[1,2,2]{2,1,0:T(2,128)} %param.11) | copy-start | bytes 52
  29.3 4.4 %copy-start.2 = (f32[1,2,2]{2,1,0:T(2,128)S(1)}, f32[1,2,2]{2,1,0:T(2,128)}, u32[]{:S(2)}) copy-start(f32[1,2,2]{2,1,0:T(2,128)} %param.15) | copy-start | bytes 52
  29.3 4.4 %copy-start.3 = (s32[1,2,2]{2,1,0:T(2,128)S(1)}, s32[1,2,2]{2,1,0:T(2,128)}, u32[]{:S(2)}) copy-start(s32[1,2,2]{2,1,0:T(2,128)} %param.14) | copy-start | bytes 52
  33.8 1.8 %collective-permute-start.10 = (f32[4,4]{1,0:T(4,128)S(1)}, f32[4,4]{1,0:T(4,128)S(1)}, u32[]{:S(2)}, u32[]{:S(2)}) collective-permute-start(f32[4,4]{1,0:T(4,128)S(1)} %pad_maximum_fusion.2), channel_id=1, source_target_pairs={{0,8},{8,0},{16,24},{24,16},{1,9},{9,1},{17,25},{25,17},{2,10},{10... | collective-permute-start | bytes 200 | tf_op jit(solution)/shard_map/ppermute | solution.py:20
  34.2 5.8 %collective-permute-start.12 = (bf16[96,896]{1,0:T(8,128)(2,1)S(1)}, bf16[96,896]{1,0:T(8,128)(2,1)S(1)}, u32[]{:S(2)}, u32[]{:S(2)}) collective-permute-start(bf16[96,896]{1,0:T(8,128)(2,1)S(1)} %get-tuple-element.36), channel_id=1, source_target_pairs={{0,1},{1,0},{2,3},{3,2},{4,5},{5,4},{6,7},{7,6},{8,9},{9,8},{10,11... | collective-permute-start | bytes 516104 | tf_op jit(solution)/shard_map/ppermute | solution.py:34
  35.6 2.8 %collective-permute-start.11 = (f32[2,4]{1,0:T(2,128)S(1)}, f32[2,4]{1,0:T(2,128)S(1)}, u32[]{:S(2)}, u32[]{:S(2)}) collective-permute-start(f32[2,4]{1,0:T(2,128)S(1)} %get-tuple-element.59), channel_id=1, source_target_pairs={{0,16},{1,17},{2,18},{3,19},{4,20},{5,21},{6,22},{7,23},{8,24},{9,... | collective-permute-start | bytes 104 | tf_op jit(solution)/shard_map/ppermute | solution.py:42
  40.1 5.0 %collective-permute-start.13 = (bf16[24,896]{1,0:T(8,128)(2,1)S(1)}, bf16[24,896]{1,0:T(8,128)(2,1)S(1)}, u32[]{:S(2)}, u32[]{:S(2)}) collective-permute-start(bf16[24,896]{1,0:T(8,128)(2,1)S(1)} %get-tuple-element.43), channel_id=1, source_target_pairs={{0,6},{1,7},{2,4},{3,5},{4,2},{5,3},{6,0},{7,1},{8,14},{9,15},{10,... | collective-permute-start | bytes 129032 | tf_op jit(solution)/shard_map/ppermute | solution.py:34
  43.6 3.8 %collective-permute-start.14 = (bf16[24,896]{1,0:T(8,128)(2,1)S(1)}, bf16[24,896]{1,0:T(8,128)(2,1)S(1)}, u32[]{:S(2)}, u32[]{:S(2)}) collective-permute-start(bf16[24,896]{1,0:T(8,128)(2,1)S(1)} %get-tuple-element.44), channel_id=1, source_target_pairs={{0,4},{1,5},{2,6},{3,7},{4,0},{5,1},{6,2},{7,3},{8,12},{9,13},{10,... | collective-permute-start | bytes 129032 | tf_op jit(solution)/shard_map/ppermute | solution.py:34
  43.6 3.8 %collective-permute-start.15 = (bf16[24,896]{1,0:T(8,128)(2,1)S(1)}, bf16[24,896]{1,0:T(8,128)(2,1)S(1)}, u32[]{:S(2)}, u32[]{:S(2)}) collective-permute-start(bf16[24,896]{1,0:T(8,128)(2,1)S(1)} %get-tuple-element.45), channel_id=1, source_target_pairs={{0,2},{1,3},{2,0},{3,1},{4,6},{5,7},{6,4},{7,5},{8,10},{9,11},{10,... | collective-permute-start | bytes 129032 | tf_op jit(solution)/shard_map/ppermute | solution.py:34
  47.6 3.3 %collective-permute-start.16 = (bf16[16,896]{1,0:T(8,128)(2,1)S(1)}, bf16[16,896]{1,0:T(8,128)(2,1)S(1)}, u32[]{:S(2)}, u32[]{:S(2)}) collective-permute-start(bf16[16,896]{1,0:T(8,128)(2,1)S(1)} %get-tuple-element.47), channel_id=1, source_target_pairs={{0,8},{8,0},{16,24},{24,16},{1,9},{9,1},{17,25},{25,17},{2,10},{10... | collective-permute-start | bytes 86024 | tf_op jit(solution)/shard_map/ppermute | solution.py:20

commit v7 on v6

--- a/solution.py
+++ b/solution.py
@@ -217,7 +217,7 @@
         out[:, at : at + hid] = dh[i * n : (i + 1) * n]
 
 
-def down_kernel(plan, ranks, place, order, mine, theirs, g_t, u_t_low, u_t_high, d, kept, sent):
+def down_kernel(plan, ranks, place, _, order, mine, theirs, g_t, u_t_low, u_t_high, d, kept, sent):
     hid = d.shape[0]
     groups = plan.fwd + plan.both + plan.bwd
     n = 2 * ranks
@@ -408,20 +408,21 @@
         [((2 * ranks, (groups + len(plan.places)) * hid), F32)],
         3 * hid * half,
     )
+    weights = jnp.concatenate(
+        [
+            expert_weights(after(fwd_routes[0], mine), fwd_probs[0]),
+            expert_weights(after(bwd_routes[0], mine), bwd_probs[0]),
+        ]
+    )
+    others = swap_cores(weights)
+    even, odd = by_section(weights, others, core)
     kept, sent = on_core(
         functools.partial(down_kernel, plan, ranks),
         place,
-        (back_order, mine, swap_cores(mine), g_t, u_t_low, u_t_high, d),
+        (others, back_order, mine, swap_cores(mine), g_t, u_t_low, u_t_high, d),
         [((ranks // 2 * PARTS * groups * 2, half // PARTS), BF16)] * 2,
         3 * hid * half,
     )
-    weights = jnp.concatenate(
-        [
-            expert_weights(after(fwd_routes[0], sent), fwd_probs[0]),
-            expert_weights(after(bwd_routes[0], sent), bwd_probs[0]),
-        ]
-    )
-    even, odd = by_section(weights, swap_cores(weights), core)
     far = to_next_chips(odd[:2], even[2:], 0)
     weights = jnp.concatenate([even[:2], far[0], odd[2:], *far[1:]])
     weights = jnp.concatenate([weights] * PARTS)

time: 52.1 us -> 51.7 us (level)
  no operation moved by 1% of the time
where the time goes in v7:
time: 51.7 us; the launch traced here: 51.2 us
  Pallas kernels  20.4 us (39%)
  starting transfers between devices  18.8 us (36%)
  waiting for transfers between devices  8.92 us (17%)
  other arithmetic  1.27 us (2%)
  local copies, waits for them, and re-layouts  0.94 us (2%)
  between operations  0.85 us (2%)
    pallas_call x2, Pallas kernels, fetch(): pl.pallas_call(functools.partial(fetch_kernel, pieces, order), in_specs=[...  10.9 us
    pallas_call x5, Pallas kernels, on_core(): pl.pallas_call(kernel, in_specs=specs, out_specs=[pl.BlockSpec(memory_spa...  9.56 us
    ppermute x8, starting transfers between devices, swap_ranks(): return lax.ppermute(block, 'expert', [(i, i ^ bit) for i in ranks])  8.28 us
    ppermute x3, starting transfers between devices, move(): return lax.ppermute(block, ('section', 'expert'), route)  5.92 us
    ppermute x8, waiting for transfers between devices, swap_ranks(): return lax.ppermute(block, 'expert', [(i, i ^ bit) for i in ranks])  4.88 us
    ppermute x6, starting transfers between devices, swap_cores(): return lax.ppermute(block, 'section', [(i, i ^ 1) for i in sections])  4.61 us
    ppermute x6, waiting for transfers between devices, swap_cores(): return lax.ppermute(block, 'section', [(i, i ^ 1) for i in sections])  2.54 us
    ppermute x3, waiting for transfers between devices, move(): return lax.ppermute(block, ('section', 'expert'), route)  1.51 us
  transfers between devices with their start and end apart: 17, of which 8 were waited for; matrix products, arithmetic and copies ran while one was open for 2% of the time, Pallas kernels for 22%

profile of v7, /device:TPU:1, one launch (start us, length us, event | category | flops | bytes accessed | tf_op | source)
XLA Modules:
  0.0 51.2 jit_solution(4183260261403320989)
XLA Ops:
  0.6 0.1 collective-permute-start
  0.8 0.5 collective-permute-start.1
  1.2 0.1 collective-permute-start.2
  1.3 0.9 %pad_maximum_fusion = bf16[6,7168]{1,0:T(8,128)(2,1)S(1)} fusion(bf16[2,7168]{1,0:T(2,128)(2,1)} %bitcast.43, bf16[2,7168]{1,0:T(2,128)(2,1)} %bitcast.41, bf16[2,7168]{1,0:T(2,128)(2,1)} %bitcast.39), kind=kLoop, calls=%fused_computation | loop fusion | flops 258048 | bytes 172032 | tf_op jit(solution)/shard_map/concatenate | solution.py:359
  2.2 0.1 pad_add_fusion.place
  2.3 0.0 collective-permute-done
  2.3 0.0 collective-permute-done.1
  2.3 0.3 collective-permute-done.2
  2.6 0.1 pad_maximum_fusion.1
  2.9 4.5 %collective-permute-start.5 = (bf16[16,896]{1,0:T(8,128)(2,1)S(1)}, bf16[16,896]{1,0:T(8,128)(2,1)S(1)}, u32[]{:S(2)}, u32[]{:S(2)}) collective-permute-start(bf16[16,896]{1,0:T(8,128)(2,1)S(1)} %pad_select_fusion), channel_id=1, source_target_pairs={{0,20},{1,21},{2,22},{3,23},{4,16},{5,17},{6,18},{7,19},{8,28},{9,... | collective-permute-start | bytes 86024 | tf_op jit(solution)/shard_map/ppermute | solution.py:42
  7.4 0.3 collective-permute-start.3
  7.7 0.2 collective-permute-start.4
  7.8 4.8 %shard_map.113 = (bf16[3584,1024]{1,0:T(8,128)(2,1)S(1)}, bf16[1024,3584]{1,0:T(8,128)(2,1)S(1)}, bf16[896,1024]{1,0:T(8,128)(2,1)S(1)}, bf16[1024,896]{1,0:T(8,...) custom-call(s32[3]{0:T(128)S(1)} %pad_add_fusion.place, bf16[7168,1024]{1,0:T(8,128)(2,1)} %refs_0_.2, ...), custom_call_target="tpu_custom_call" | custom-call | bytes 18350080 | tf_op jit(solution)/shard_map/pallas_call | solution.py:170
  12.7 0.0 collective-permute-done.3
  12.7 0.0 collective-permute-done.4
  12.7 0.0 collective-permute-done.5
  12.8 2.3 %collective-permute-start.8 = (bf16[80,896]{1,0:T(8,128)(2,1)S(1)}, bf16[80,896]{1,0:T(8,128)(2,1)S(1)}, u32[]{:S(2)}, u32[]{:S(2)}) collective-permute-start(bf16[80,896]{1,0:T(8,128)(2,1)S(1)} %add.10.refs_2_.first), channel_id=1, source_target_pairs={{0,3},{1,2},{2,1},{3,0},{4,7},{5,6},{6,5},{7,4},{8,11},{9,10},{10,... | collective-permute-start | bytes 430088 | tf_op jit(solution)/shard_map/ppermute | solution.py:34
  15.1 0.2 collective-permute-start.7
  15.3 0.2 collective-permute-start.6
  15.5 6.1 %shard_map.114 = (bf16[2688,1024]{1,0:T(8,128)(2,1)S(1)}, bf16[1024,2688]{1,0:T(8,128)(2,1)S(1)}, bf16[1024,3584]{1,0:T(8,128)(2,1)S(1)}, bf16[3584,1024]{1,0:T(...) custom-call(s32[3]{0:T(128)S(1)} %pad_add_fusion.place, bf16[7168,1024]{1,0:T(8,128)(2,1)} %refs_0_.3, ...), custom_call_target="tpu_custom_call" | custom-call | bytes 25690112 | tf_op jit(solution)/shard_map/pallas_call | solution.py:170
  21.6 0.0 collective-permute-done.8.fourth
  21.6 0.7 %collective-permute-done.7.third = bf16[80,896]{1,0:T(8,128)(2,1)S(1)} collective-permute-done((bf16[80,896]{1,0:T(8,128)(2,1)S(1)}, bf16[80,896]{1,0:T(8,128)(2,1)S(1)}, u32[]{:S(2)}, u32[]{:S(2)}) %collective-permute-start.7) | collective-permute-done | bytes 143392 | tf_op jit(solution)/shard_map/ppermute | solution.py:34
  22.3 0.0 collective-permute-done.6.second
  22.3 0.0 copy-start.3
  22.3 4.3 %shard_map.115.mine = f32[16,8192]{1,0:T(8,128)S(1)} custom-call(bf16[320,320]{1,0:T(8,128)(2,1)S(1)} %get-tuple-element.26.order, bf16[80,896]{1,0:T(8,128)(2,1)S(1)} %add.10.refs_2_.first, bf16[80,896]{1,0:T(8,128)(2,1)S(1)} %collective-permute-done.6.second, bf16[80,896]{1,0:T(8,128)(2,1)S(1)} %collective-permute-done.7.third, ...), custom_call_target="tpu_custom_call" | custom-call | flops 5637144576 | bytes 22020096 | tf_op jit(solution)/shard_map/pallas_call | solution.py:318
  26.6 1.2 %collective-permute-start.11 = (f32[16,8192]{1,0:T(8,128)S(1)}, f32[16,8192]{1,0:T(8,128)S(1)}, u32[]{:S(2)}, u32[]{:S(2)}) collective-permute-start(f32[16,8192]{1,0:T(8,128)S(1)} %shard_map.115.mine), channel_id=1, source_target_pairs={{0,8},{8,0},{16,24},{24,16},{1,9},{9,1},{17,25},{25,17},{2,10},{10... | collective-permute-start | bytes 1572872 | tf_op jit(solution)/shard_map/ppermute | solution.py:20
  27.8 0.0 copy-done
  27.8 0.1 fusion
  27.9 0.1 collective-permute-start.9
  28.0 1.3 %collective-permute-done.9._ = f32[4,4]{1,0:T(4,128)S(1)} collective-permute-done((f32[4,4]{1,0:T(4,128)S(1)}, f32[4,4]{1,0:T(4,128)S(1)}, u32[]{:S(2)}, u32[]{:S(2)}) %collective-permute-start.9) | collective-permute-done | bytes 96 | tf_op jit(solution)/shard_map/ppermute | solution.py:20
  29.3 0.0 collective-permute-done.11.theirs
  29.3 4.4 %shard_map.117 = (bf16[96,896]{1,0:T(8,128)(2,1)S(1)}, bf16[96,896]{1,0:T(8,128)(2,1)S(1)}) custom-call(s32[3]{0:T(128)S(1)} %pad_add_fusion.place, f32[4,4]{1,0:T(4,128)S(1)} %collective-permute-done.9._, bf16[192,192]{1,0:T(8,128)(2,1)S(1)} %get-tuple-element.35.order, f32[16,8192]{1,0:T(8,128)S(1)} %shard_map.115.mine, ...), custom_call_target="tpu_custom_call" | custom-call | flops 5637144576 | bytes 22020096 | tf_op jit(solution)/shard_map/pallas_call | solution.py:318
  33.7 1.5 %collective-permute-start.12 = (bf16[96,896]{1,0:T(8,128)(2,1)S(1)}, bf16[96,896]{1,0:T(8,128)(2,1)S(1)}, u32[]{:S(2)}, u32[]{:S(2)}) collective-permute-start(bf16[96,896]{1,0:T(8,128)(2,1)S(1)} %get-tuple-element.41), channel_id=1, source_target_pairs={{0,1},{1,0},{2,3},{3,2},{4,5},{5,4},{6,7},{7,6},{8,9},{9,8},{10,11... | collective-permute-start | bytes 516104 | tf_op jit(solution)/shard_map/ppermute | solution.py:34
  35.2 1.2 %collective-permute-start.10 = (f32[2,4]{1,0:T(2,128)S(1)}, f32[2,4]{1,0:T(2,128)S(1)}, u32[]{:S(2)}, u32[]{:S(2)}) collective-permute-start(f32[2,4]{1,0:T(2,128)S(1)} %get-tuple-element.59), channel_id=1, source_target_pairs={{0,16},{1,17},{2,18},{3,19},{4,20},{5,21},{6,22},{7,23},{8,24},{9,... | collective-permute-start | bytes 104 | tf_op jit(solution)/shard_map/ppermute | solution.py:42
  36.4 1.5 %collective-permute-done.10 = f32[2,4]{1,0:T(2,128)S(1)} collective-permute-done((f32[2,4]{1,0:T(2,128)S(1)}, f32[2,4]{1,0:T(2,128)S(1)}, u32[]{:S(2)}, u32[]{:S(2)}) %collective-permute-start.10) | collective-permute-done | bytes 64 | tf_op jit(solution)/shard_map/ppermute | solution.py:42
  37.9 0.1 concatenate.32.weights
  37.9 1.4 %collective-permute-done.12.got = bf16[96,896]{1,0:T(8,128)(2,1)S(1)} collective-permute-done((bf16[96,896]{1,0:T(8,128)(2,1)S(1)}, bf16[96,896]{1,0:T(8,128)(2,1)S(1)}, u32[]{:S(2)}, u32[]{:S(2)}) %collective-permute-start.12) | collective-permute-done | bytes 172064 | tf_op jit(solution)/shard_map/ppermute | solution.py:34
  39.4 3.6 %collective-permute-start.13 = (bf16[24,896]{1,0:T(8,128)(2,1)S(1)}, bf16[24,896]{1,0:T(8,128)(2,1)S(1)}, u32[]{:S(2)}, u32[]{:S(2)}) collective-permute-start(bf16[24,896]{1,0:T(8,128)(2,1)S(1)} %get-tuple-element.43), channel_id=1, source_target_pairs={{0,6},{1,7},{2,4},{3,5},{4,2},{5,3},{6,0},{7,1},{8,14},{9,15},{10,... | collective-permute-start | bytes 129032 | tf_op jit(solution)/shard_map/ppermute | solution.py:34
  43.0 0.0 collective-permute-start.14
  43.0 0.4 collective-permute-start.15
  43.3 0.6 %shard_map.116 = (f32[96,128]{1,0:T(8,128)S(1)}, bf16[32,24]{1,0:T(8,128)(2,1)S(1)}) custom-call(s32[3]{0:T(128)S(1)} %pad_add_fusion.place, f32[24,4]{1,0:T(8,128)S(1)} %concatenate.32.weights), custom_call_target="tpu_custom_call" | custom-call | flops 1835008 | bytes 7168 | tf_op jit(solution)/shard_map/pallas_call | solution.py:318
  43.9 0.4 collective-permute-done.13.refs_1_
  44.4 2.4 %collective-permute-done.14.refs_2_ = bf16[24,896]{1,0:T(8,128)(2,1)S(1)} collective-permute-done((bf16[24,896]{1,0:T(8,128)(2,1)S(1)}, bf16[24,896]{1,0:T(8,128)(2,1)S(1)}, u32[]{:S(2)}, u32[]{:S(2)}) %collective-permute-start.14) | collective-permute-done | bytes 43040 | tf_op jit(solution)/shard_map/ppermute | solution.py:34
  46.7 0.0 collective-permute-done.15.refs_3_
  46.7 0.2 shard_map.119
  47.0 2.7 %collective-permute-start.16 = (bf16[16,896]{1,0:T(8,128)(2,1)S(1)}, bf16[16,896]{1,0:T(8,128)(2,1)S(1)}, u32[]{:S(2)}, u32[]{:S(2)}) collective-permute-start(bf16[16,896]{1,0:T(8,128)(2,1)S(1)} %get-tuple-element.47), channel_id=1, source_target_pairs={{0,8},{8,0},{16,24},{24,16},{1,9},{9,1},{17,25},{25,17},{2,10},{10... | collective-permute-start | bytes 86024 | tf_op jit(solution)/shard_map/ppermute | solution.py:20
  49.7 0.8 %collective-permute-done.16 = bf16[16,896]{1,0:T(8,128)(2,1)S(1)} collective-permute-done((bf16[16,896]{1,0:T(8,128)(2,1)S(1)}, bf16[16,896]{1,0:T(8,128)(2,1)S(1)}, u32[]{:S(2)}, u32[]{:S(2)}) %collective-permute-start.16) | collective-permute-done | bytes 28704 | tf_op jit(solution)/shard_map/ppermute | solution.py:20
  50.6 0.7 %slice_bitcast_fusion = (bf16[1,2,7168]{2,1,0:T(2,128)(2,1)}, bf16[1,2,7168]{2,1,0:T(2,128)(2,1)}) fusion(bf16[4,7168]{1,0:T(4,128)(2,1)S(1)} %maximum_select_fusion), kind=kLoop, calls=%fused_computation.7 | loop fusion | bytes 114688 | tf_op jit(solution)/shard_map/broadcast_in_dim | solution.py:456
  (29 shorter events, 0.4 us)
Async XLA Ops:
  0.6 1.6 %collective-permute-start = (bf16[2,7168]{1,0:T(2,128)(2,1)}, bf16[2,7168]{1,0:T(2,128)(2,1)S(1)}, u32[]{:S(2)}, u32[]{:S(2)}) collective-permute-start(bf16[2,7168]{1,0:T(2,128)(2,1)} %bitcast.38), channel_id=1, source_target_pairs={{0,8},{8,0},{16,24},{24,16},{1,9},{9,1},{17,25},{25,17},{2,10},{10... | collective-permute-start | bytes 86024 | tf_op jit(solution)/shard_map/ppermute | solution.py:20
  0.8 1.5 %collective-permute-start.1 = (bf16[2,7168]{1,0:T(2,128)(2,1)}, bf16[2,7168]{1,0:T(2,128)(2,1)S(1)}, u32[]{:S(2)}, u32[]{:S(2)}) collective-permute-start(bf16[2,7168]{1,0:T(2,128)(2,1)} %bitcast.40), channel_id=1, source_target_pairs={{0,8},{8,0},{16,24},{24,16},{1,9},{9,1},{17,25},{25,17},{2,10},{10... | collective-permute-start | bytes 86024 | tf_op jit(solution)/shard_map/ppermute | solution.py:20
  1.2 1.4 %collective-permute-start.2 = (bf16[2,7168]{1,0:T(2,128)(2,1)}, bf16[2,7168]{1,0:T(2,128)(2,1)S(1)}, u32[]{:S(2)}, u32[]{:S(2)}) collective-permute-start(bf16[2,7168]{1,0:T(2,128)(2,1)} %bitcast.42), channel_id=1, source_target_pairs={{0,8},{8,0},{16,24},{24,16},{1,9},{9,1},{17,25},{25,17},{2,10},{10... | collective-permute-start | bytes 86024 | tf_op jit(solution)/shard_map/ppermute | solution.py:20
  2.9 9.8 %collective-permute-start.5 = (bf16[16,896]{1,0:T(8,128)(2,1)S(1)}, bf16[16,896]{1,0:T(8,128)(2,1)S(1)}, u32[]{:S(2)}, u32[]{:S(2)}) collective-permute-start(bf16[16,896]{1,0:T(8,128)(2,1)S(1)} %pad_select_fusion), channel_id=1, source_target_pairs={{0,20},{1,21},{2,22},{3,23},{4,16},{5,17},{6,18},{7,19},{8,28},{9,... | collective-permute-start | bytes 86024 | tf_op jit(solution)/shard_map/ppermute | solution.py:42
  7.4 5.3 %collective-permute-start.3 = (bf16[16,896]{1,0:T(8,128)(2,1)S(1)}, bf16[16,896]{1,0:T(8,128)(2,1)S(1)}, u32[]{:S(2)}, u32[]{:S(2)}) collective-permute-start(bf16[16,896]{1,0:T(8,128)(2,1)S(1)} %pad_select_fusion), channel_id=1, source_target_pairs={{0,16},{1,17},{2,18},{3,19},{4,20},{5,21},{6,22},{7,23},{8,24},{9,... | collective-permute-start | bytes 86024 | tf_op jit(solution)/shard_map/ppermute | solution.py:42
  7.7 5.0 %collective-permute-start.4 = (bf16[24,896]{1,0:T(8,128)(2,1)S(1)}, bf16[24,896]{1,0:T(8,128)(2,1)S(1)}, u32[]{:S(2)}, u32[]{:S(2)}) collective-permute-start(bf16[24,896]{1,0:T(8,128)(2,1)S(1)} %get-tuple-element.52.refs_2_), channel_id=1, source_target_pairs={{0,4},{1,5},{2,6},{3,7},{4,0},{5,1},{6,2},{7,3},{8,12},{9,13},{10,... | collective-permute-start | bytes 129032 | tf_op jit(solution)/shard_map/ppermute | solution.py:34
  12.8 8.8 %collective-permute-start.8 = (bf16[80,896]{1,0:T(8,128)(2,1)S(1)}, bf16[80,896]{1,0:T(8,128)(2,1)S(1)}, u32[]{:S(2)}, u32[]{:S(2)}) collective-permute-start(bf16[80,896]{1,0:T(8,128)(2,1)S(1)} %add.10.refs_2_.first), channel_id=1, source_target_pairs={{0,3},{1,2},{2,1},{3,0},{4,7},{5,6},{6,5},{7,4},{8,11},{9,10},{10,... | collective-permute-start | bytes 430088 | tf_op jit(solution)/shard_map/ppermute | solution.py:34
  15.1 7.2 %collective-permute-start.7 = (bf16[80,896]{1,0:T(8,128)(2,1)S(1)}, bf16[80,896]{1,0:T(8,128)(2,1)S(1)}, u32[]{:S(2)}, u32[]{:S(2)}) collective-permute-start(bf16[80,896]{1,0:T(8,128)(2,1)S(1)} %add.10.refs_2_.first), channel_id=1, source_target_pairs={{0,1},{1,0},{2,3},{3,2},{4,5},{5,4},{6,7},{7,6},{8,9},{9,8},{10,11... | collective-permute-start | bytes 430088 | tf_op jit(solution)/shard_map/ppermute | solution.py:34
  15.3 6.9 %collective-permute-start.6 = (bf16[80,896]{1,0:T(8,128)(2,1)S(1)}, bf16[80,896]{1,0:T(8,128)(2,1)S(1)}, u32[]{:S(2)}, u32[]{:S(2)}) collective-permute-start(bf16[80,896]{1,0:T(8,128)(2,1)S(1)} %add.10.refs_2_.first), channel_id=1, source_target_pairs={{0,2},{1,3},{2,0},{3,1},{4,6},{5,7},{6,4},{7,5},{8,10},{9,11},{10,... | collective-permute-start | bytes 430088 | tf_op jit(solution)/shard_map/ppermute | solution.py:34
  22.3 5.5 %copy-start = (f32[1,2,2]{2,1,0:T(2,128)S(1)}, f32[1,2,2]{2,1,0:T(2,128)}, u32[]{:S(2)}) copy-start(f32[1,2,2]{2,1,0:T(2,128)} %param.12) | copy-start | bytes 52
  22.3 5.5 %copy-start.1 = (s32[1,2,2]{2,1,0:T(2,128)S(1)}, s32[1,2,2]{2,1,0:T(2,128)}, u32[]{:S(2)}) copy-start(s32[1,2,2]{2,1,0:T(2,128)} %param.11) | copy-start | bytes 52
  22.3 5.5 %copy-start.2 = (f32[1,2,2]{2,1,0:T(2,128)S(1)}, f32[1,2,2]{2,1,0:T(2,128)}, u32[]{:S(2)}) copy-start(f32[1,2,2]{2,1,0:T(2,128)} %param.15) | copy-start | bytes 52
  22.3 5.5 %copy-start.3 = (s32[1,2,2]{2,1,0:T(2,128)S(1)}, s32[1,2,2]{2,1,0:T(2,128)}, u32[]{:S(2)}) copy-start(s32[1,2,2]{2,1,0:T(2,128)} %param.14) | copy-start | bytes 52
  26.6 2.7 %collective-permute-start.11 = (f32[16,8192]{1,0:T(8,128)S(1)}, f32[16,8192]{1,0:T(8,128)S(1)}, u32[]{:S(2)}, u32[]{:S(2)}) collective-permute-start(f32[16,8192]{1,0:T(8,128)S(1)} %shard_map.115.mine), channel_id=1, source_target_pairs={{0,8},{8,0},{16,24},{24,16},{1,9},{9,1},{17,25},{25,17},{2,10},{10... | collective-permute-start | bytes 1572872 | tf_op jit(solution)/shard_map/ppermute | solution.py:20
  27.9 1.4 %collective-permute-start.9 = (f32[4,4]{1,0:T(4,128)S(1)}, f32[4,4]{1,0:T(4,128)S(1)}, u32[]{:S(2)}, u32[]{:S(2)}) collective-permute-start(f32[4,4]{1,0:T(4,128)S(1)} %pad_maximum_fusion.2), channel_id=1, source_target_pairs={{0,8},{8,0},{16,24},{24,16},{1,9},{9,1},{17,25},{25,17},{2,10},{10... | collective-permute-start | bytes 200 | tf_op jit(solution)/shard_map/ppermute | solution.py:20
  33.7 5.6 %collective-permute-start.12 = (bf16[96,896]{1,0:T(8,128)(2,1)S(1)}, bf16[96,896]{1,0:T(8,128)(2,1)S(1)}, u32[]{:S(2)}, u32[]{:S(2)}) collective-permute-start(bf16[96,896]{1,0:T(8,128)(2,1)S(1)} %get-tuple-element.41), channel_id=1, source_target_pairs={{0,1},{1,0},{2,3},{3,2},{4,5},{5,4},{6,7},{7,6},{8,9},{9,8},{10,11... | collective-permute-start | bytes 516104 | tf_op jit(solution)/shard_map/ppermute | solution.py:34
  35.2 2.7 %collective-permute-start.10 = (f32[2,4]{1,0:T(2,128)S(1)}, f32[2,4]{1,0:T(2,128)S(1)}, u32[]{:S(2)}, u32[]{:S(2)}) collective-permute-start(f32[2,4]{1,0:T(2,128)S(1)} %get-tuple-element.59), channel_id=1, source_target_pairs={{0,16},{1,17},{2,18},{3,19},{4,20},{5,21},{6,22},{7,23},{8,24},{9,... | collective-permute-start | bytes 104 | tf_op jit(solution)/shard_map/ppermute | solution.py:42
  39.4 5.0 %collective-permute-start.13 = (bf16[24,896]{1,0:T(8,128)(2,1)S(1)}, bf16[24,896]{1,0:T(8,128)(2,1)S(1)}, u32[]{:S(2)}, u32[]{:S(2)}) collective-permute-start(bf16[24,896]{1,0:T(8,128)(2,1)S(1)} %get-tuple-element.43), channel_id=1, source_target_pairs={{0,6},{1,7},{2,4},{3,5},{4,2},{5,3},{6,0},{7,1},{8,14},{9,15},{10,... | collective-permute-start | bytes 129032 | tf_op jit(solution)/shard_map/ppermute | solution.py:34
  43.0 3.8 %collective-permute-start.14 = (bf16[24,896]{1,0:T(8,128)(2,1)S(1)}, bf16[24,896]{1,0:T(8,128)(2,1)S(1)}, u32[]{:S(2)}, u32[]{:S(2)}) collective-permute-start(bf16[24,896]{1,0:T(8,128)(2,1)S(1)} %get-tuple-element.44), channel_id=1, source_target_pairs={{0,4},{1,5},{2,6},{3,7},{4,0},{5,1},{6,2},{7,3},{8,12},{9,13},{10,... | collective-permute-start | bytes 129032 | tf_op jit(solution)/shard_map/ppermute | solution.py:34
  43.0 3.8 %collective-permute-start.15 = (bf16[24,896]{1,0:T(8,128)(2,1)S(1)}, bf16[24,896]{1,0:T(8,128)(2,1)S(1)}, u32[]{:S(2)}, u32[]{:S(2)}) collective-permute-start(bf16[24,896]{1,0:T(8,128)(2,1)S(1)} %get-tuple-element.45), channel_id=1, source_target_pairs={{0,2},{1,3},{2,0},{3,1},{4,6},{5,7},{6,4},{7,5},{8,10},{9,11},{10,... | collective-permute-start | bytes 129032 | tf_op jit(solution)/shard_map/ppermute | solution.py:34
  47.0 3.5 %collective-permute-start.16 = (bf16[16,896]{1,0:T(8,128)(2,1)S(1)}, bf16[16,896]{1,0:T(8,128)(2,1)S(1)}, u32[]{:S(2)}, u32[]{:S(2)}) collective-permute-start(bf16[16,896]{1,0:T(8,128)(2,1)S(1)} %get-tuple-element.47), channel_id=1, source_target_pairs={{0,8},{8,0},{16,24},{24,16},{1,9},{9,1},{17,25},{25,17},{2,10},{10... | collective-permute-start | bytes 86024 | tf_op jit(solution)/shard_map/ppermute | solution.py:20

commit v8 on v7

--- a/solution.py
+++ b/solution.py
@@ -268,9 +268,9 @@
 
 def pair_kernel(kept, got, weights, *pairs):
     size = pairs[0].shape[0]
+    total = kept[...].astype(F32) + got[...].astype(F32)
     for i, pair in enumerate(pairs):
-        rows = slice(i * size, (i + 1) * size)
-        pair[...] = (kept[rows].astype(F32) + got[rows].astype(F32)).astype(BF16)
+        pair[...] = total[i * size : (i + 1) * size].astype(BF16)
 
 
 def select_kernel(plan, offsets, shards, place, weights, columns, chosen):

time: 51.7 us -> 51.7 us (level)
  no operation moved by 1% of the time
where the time goes in v8:
time: 51.7 us; the launch traced here: 51.2 us
  Pallas kernels  20.4 us (39%)
  starting transfers between devices  18.8 us (36%)
  waiting for transfers between devices  8.92 us (17%)
  other arithmetic  1.27 us (2%)
  local copies, waits for them, and re-layouts  0.94 us (2%)
  between operations  0.85 us (2%)
    pallas_call x2, Pallas kernels, fetch(): pl.pallas_call(functools.partial(fetch_kernel, pieces, order), in_specs=[...  10.9 us
    pallas_call x5, Pallas kernels, on_core(): pl.pallas_call(kernel, in_specs=specs, out_specs=[pl.BlockSpec(memory_spa...  9.56 us
    ppermute x8, starting transfers between devices, swap_ranks(): return lax.ppermute(block, 'expert', [(i, i ^ bit) for i in ranks])  8.28 us
    ppermute x3, starting transfers between devices, move(): return lax.ppermute(block, ('section', 'expert'), route)  5.92 us
    ppermute x8, waiting for transfers between devices, swap_ranks(): return lax.ppermute(block, 'expert', [(i, i ^ bit) for i in ranks])  4.88 us
    ppermute x6, starting transfers between devices, swap_cores(): return lax.ppermute(block, 'section', [(i, i ^ 1) for i in sections])  4.61 us
    ppermute x6, waiting for transfers between devices, swap_cores(): return lax.ppermute(block, 'section', [(i, i ^ 1) for i in sections])  2.54 us
    ppermute x3, waiting for transfers between devices, move(): return lax.ppermute(block, ('section', 'expert'), route)  1.51 us
  transfers between devices with their start and end apart: 17, of which 8 were waited for; matrix products, arithmetic and copies ran while one was open for 2% of the time, Pallas kernels for 22%

profile of v8, /device:TPU:1, one launch (start us, length us, event | category | flops | bytes accessed | tf_op | source)
XLA Modules:
  0.0 51.2 jit_solution(4183260261403320989)
XLA Ops:
  0.6 0.1 collective-permute-start
  0.8 0.5 collective-permute-start.1
  1.2 0.1 collective-permute-start.2
  1.3 0.9 %pad_maximum_fusion = bf16[6,7168]{1,0:T(8,128)(2,1)S(1)} fusion(bf16[2,7168]{1,0:T(2,128)(2,1)} %bitcast.43, bf16[2,7168]{1,0:T(2,128)(2,1)} %bitcast.41, bf16[2,7168]{1,0:T(2,128)(2,1)} %bitcast.39), kind=kLoop, calls=%fused_computation | loop fusion | flops 258048 | bytes 172032 | tf_op jit(solution)/shard_map/concatenate | solution.py:359
  2.2 0.1 pad_add_fusion.place
  2.3 0.0 collective-permute-done
  2.3 0.0 collective-permute-done.1
  2.3 0.3 collective-permute-done.2
  2.6 0.1 pad_maximum_fusion.1
  2.9 4.5 %collective-permute-start.5 = (bf16[16,896]{1,0:T(8,128)(2,1)S(1)}, bf16[16,896]{1,0:T(8,128)(2,1)S(1)}, u32[]{:S(2)}, u32[]{:S(2)}) collective-permute-start(bf16[16,896]{1,0:T(8,128)(2,1)S(1)} %pad_select_fusion), channel_id=1, source_target_pairs={{0,20},{1,21},{2,22},{3,23},{4,16},{5,17},{6,18},{7,19},{8,28},{9,... | collective-permute-start | bytes 86024 | tf_op jit(solution)/shard_map/ppermute | solution.py:42
  7.4 0.3 collective-permute-start.3
  7.7 0.2 collective-permute-start.4
  7.8 4.8 %shard_map.113 = (bf16[3584,1024]{1,0:T(8,128)(2,1)S(1)}, bf16[1024,3584]{1,0:T(8,128)(2,1)S(1)}, bf16[896,1024]{1,0:T(8,128)(2,1)S(1)}, bf16[1024,896]{1,0:T(8,...) custom-call(s32[3]{0:T(128)S(1)} %pad_add_fusion.place, bf16[7168,1024]{1,0:T(8,128)(2,1)} %refs_0_.2, ...), custom_call_target="tpu_custom_call" | custom-call | bytes 18350080 | tf_op jit(solution)/shard_map/pallas_call | solution.py:170
  12.7 0.0 collective-permute-done.3
  12.7 0.0 collective-permute-done.4
  12.7 0.0 collective-permute-done.5
  12.8 2.3 %collective-permute-start.8 = (bf16[80,896]{1,0:T(8,128)(2,1)S(1)}, bf16[80,896]{1,0:T(8,128)(2,1)S(1)}, u32[]{:S(2)}, u32[]{:S(2)}) collective-permute-start(bf16[80,896]{1,0:T(8,128)(2,1)S(1)} %add.10.refs_2_.first), channel_id=1, source_target_pairs={{0,3},{1,2},{2,1},{3,0},{4,7},{5,6},{6,5},{7,4},{8,11},{9,10},{10,... | collective-permute-start | bytes 430088 | tf_op jit(solution)/shard_map/ppermute | solution.py:34
  15.1 0.2 collective-permute-start.7
  15.3 0.2 collective-permute-start.6
  15.5 6.1 %shard_map.114 = (bf16[2688,1024]{1,0:T(8,128)(2,1)S(1)}, bf16[1024,2688]{1,0:T(8,128)(2,1)S(1)}, bf16[1024,3584]{1,0:T(8,128)(2,1)S(1)}, bf16[3584,1024]{1,0:T(...) custom-call(s32[3]{0:T(128)S(1)} %pad_add_fusion.place, bf16[7168,1024]{1,0:T(8,128)(2,1)} %refs_0_.3, ...), custom_call_target="tpu_custom_call" | custom-call | bytes 25690112 | tf_op jit(solution)/shard_map/pallas_call | solution.py:170
  21.6 0.0 collective-permute-done.8.fourth
  21.6 0.7 %collective-permute-done.7.third = bf16[80,896]{1,0:T(8,128)(2,1)S(1)} collective-permute-done((bf16[80,896]{1,0:T(8,128)(2,1)S(1)}, bf16[80,896]{1,0:T(8,128)(2,1)S(1)}, u32[]{:S(2)}, u32[]{:S(2)}) %collective-permute-start.7) | collective-permute-done | bytes 143392 | tf_op jit(solution)/shard_map/ppermute | solution.py:34
  22.3 0.0 collective-permute-done.6.second
  22.3 0.0 copy-start.3
  22.3 4.3 %shard_map.115.mine = f32[16,8192]{1,0:T(8,128)S(1)} custom-call(bf16[320,320]{1,0:T(8,128)(2,1)S(1)} %get-tuple-element.26.order, bf16[80,896]{1,0:T(8,128)(2,1)S(1)} %add.10.refs_2_.first, bf16[80,896]{1,0:T(8,128)(2,1)S(1)} %collective-permute-done.6.second, bf16[80,896]{1,0:T(8,128)(2,1)S(1)} %collective-permute-done.7.third, ...), custom_call_target="tpu_custom_call" | custom-call | flops 5637144576 | bytes 22020096 | tf_op jit(solution)/shard_map/pallas_call | solution.py:318
  26.6 1.2 %collective-permute-start.11 = (f32[16,8192]{1,0:T(8,128)S(1)}, f32[16,8192]{1,0:T(8,128)S(1)}, u32[]{:S(2)}, u32[]{:S(2)}) collective-permute-start(f32[16,8192]{1,0:T(8,128)S(1)} %shard_map.115.mine), channel_id=1, source_target_pairs={{0,8},{8,0},{16,24},{24,16},{1,9},{9,1},{17,25},{25,17},{2,10},{10... | collective-permute-start | bytes 1572872 | tf_op jit(solution)/shard_map/ppermute | solution.py:20
  27.8 0.0 copy-done
  27.8 0.1 fusion
  27.9 0.1 collective-permute-start.9
  28.0 1.3 %collective-permute-done.9._ = f32[4,4]{1,0:T(4,128)S(1)} collective-permute-done((f32[4,4]{1,0:T(4,128)S(1)}, f32[4,4]{1,0:T(4,128)S(1)}, u32[]{:S(2)}, u32[]{:S(2)}) %collective-permute-start.9) | collective-permute-done | bytes 96 | tf_op jit(solution)/shard_map/ppermute | solution.py:20
  29.3 0.0 collective-permute-done.11.theirs
  29.3 4.4 %shard_map.117 = (bf16[96,896]{1,0:T(8,128)(2,1)S(1)}, bf16[96,896]{1,0:T(8,128)(2,1)S(1)}) custom-call(s32[3]{0:T(128)S(1)} %pad_add_fusion.place, f32[4,4]{1,0:T(4,128)S(1)} %collective-permute-done.9._, bf16[192,192]{1,0:T(8,128)(2,1)S(1)} %get-tuple-element.35.order, f32[16,8192]{1,0:T(8,128)S(1)} %shard_map.115.mine, ...), custom_call_target="tpu_custom_call" | custom-call | flops 5637144576 | bytes 22020096 | tf_op jit(solution)/shard_map/pallas_call | solution.py:318
  33.7 1.5 %collective-permute-start.12 = (bf16[96,896]{1,0:T(8,128)(2,1)S(1)}, bf16[96,896]{1,0:T(8,128)(2,1)S(1)}, u32[]{:S(2)}, u32[]{:S(2)}) collective-permute-start(bf16[96,896]{1,0:T(8,128)(2,1)S(1)} %get-tuple-element.41), channel_id=1, source_target_pairs={{0,1},{1,0},{2,3},{3,2},{4,5},{5,4},{6,7},{7,6},{8,9},{9,8},{10,11... | collective-permute-start | bytes 516104 | tf_op jit(solution)/shard_map/ppermute | solution.py:34
  35.2 1.2 %collective-permute-start.10 = (f32[2,4]{1,0:T(2,128)S(1)}, f32[2,4]{1,0:T(2,128)S(1)}, u32[]{:S(2)}, u32[]{:S(2)}) collective-permute-start(f32[2,4]{1,0:T(2,128)S(1)} %get-tuple-element.59), channel_id=1, source_target_pairs={{0,16},{1,17},{2,18},{3,19},{4,20},{5,21},{6,22},{7,23},{8,24},{9,... | collective-permute-start | bytes 104 | tf_op jit(solution)/shard_map/ppermute | solution.py:42
  36.4 1.5 %collective-permute-done.10 = f32[2,4]{1,0:T(2,128)S(1)} collective-permute-done((f32[2,4]{1,0:T(2,128)S(1)}, f32[2,4]{1,0:T(2,128)S(1)}, u32[]{:S(2)}, u32[]{:S(2)}) %collective-permute-start.10) | collective-permute-done | bytes 64 | tf_op jit(solution)/shard_map/ppermute | solution.py:42
  37.9 0.1 concatenate.32.weights
  37.9 1.4 %collective-permute-done.12.got = bf16[96,896]{1,0:T(8,128)(2,1)S(1)} collective-permute-done((bf16[96,896]{1,0:T(8,128)(2,1)S(1)}, bf16[96,896]{1,0:T(8,128)(2,1)S(1)}, u32[]{:S(2)}, u32[]{:S(2)}) %collective-permute-start.12) | collective-permute-done | bytes 172064 | tf_op jit(solution)/shard_map/ppermute | solution.py:34
  39.4 3.6 %collective-permute-start.13 = (bf16[24,896]{1,0:T(8,128)(2,1)S(1)}, bf16[24,896]{1,0:T(8,128)(2,1)S(1)}, u32[]{:S(2)}, u32[]{:S(2)}) collective-permute-start(bf16[24,896]{1,0:T(8,128)(2,1)S(1)} %get-tuple-element.43), channel_id=1, source_target_pairs={{0,6},{1,7},{2,4},{3,5},{4,2},{5,3},{6,0},{7,1},{8,14},{9,15},{10,... | collective-permute-start | bytes 129032 | tf_op jit(solution)/shard_map/ppermute | solution.py:34
  43.0 0.0 collective-permute-start.14
  43.0 0.4 collective-permute-start.15
  43.3 0.6 %shard_map.116 = (f32[96,128]{1,0:T(8,128)S(1)}, bf16[32,24]{1,0:T(8,128)(2,1)S(1)}) custom-call(s32[3]{0:T(128)S(1)} %pad_add_fusion.place, f32[24,4]{1,0:T(8,128)S(1)} %concatenate.32.weights), custom_call_target="tpu_custom_call" | custom-call | flops 1835008 | bytes 7168 | tf_op jit(solution)/shard_map/pallas_call | solution.py:318
  43.9 0.4 collective-permute-done.13.refs_1_
  44.4 2.4 %collective-permute-done.14.refs_2_ = bf16[24,896]{1,0:T(8,128)(2,1)S(1)} collective-permute-done((bf16[24,896]{1,0:T(8,128)(2,1)S(1)}, bf16[24,896]{1,0:T(8,128)(2,1)S(1)}, u32[]{:S(2)}, u32[]{:S(2)}) %collective-permute-start.14) | collective-permute-done | bytes 43040 | tf_op jit(solution)/shard_map/ppermute | solution.py:34
  46.7 0.0 collective-permute-done.15.refs_3_
  46.7 0.2 shard_map.119
  47.0 2.7 %collective-permute-start.16 = (bf16[16,896]{1,0:T(8,128)(2,1)S(1)}, bf16[16,896]{1,0:T(8,128)(2,1)S(1)}, u32[]{:S(2)}, u32[]{:S(2)}) collective-permute-start(bf16[16,896]{1,0:T(8,128)(2,1)S(1)} %get-tuple-element.47), channel_id=1, source_target_pairs={{0,8},{8,0},{16,24},{24,16},{1,9},{9,1},{17,25},{25,17},{2,10},{10... | collective-permute-start | bytes 86024 | tf_op jit(solution)/shard_map/ppermute | solution.py:20
  49.7 0.8 %collective-permute-done.16 = bf16[16,896]{1,0:T(8,128)(2,1)S(1)} collective-permute-done((bf16[16,896]{1,0:T(8,128)(2,1)S(1)}, bf16[16,896]{1,0:T(8,128)(2,1)S(1)}, u32[]{:S(2)}, u32[]{:S(2)}) %collective-permute-start.16) | collective-permute-done | bytes 28704 | tf_op jit(solution)/shard_map/ppermute | solution.py:20
  50.6 0.7 %slice_bitcast_fusion = (bf16[1,2,7168]{2,1,0:T(2,128)(2,1)}, bf16[1,2,7168]{2,1,0:T(2,128)(2,1)}) fusion(bf16[4,7168]{1,0:T(4,128)(2,1)S(1)} %maximum_select_fusion), kind=kLoop, calls=%fused_computation.7 | loop fusion | bytes 114688 | tf_op jit(solution)/shard_map/broadcast_in_dim | solution.py:456
  (29 shorter events, 0.4 us)
Async XLA Ops:
  0.6 1.6 %collective-permute-start = (bf16[2,7168]{1,0:T(2,128)(2,1)}, bf16[2,7168]{1,0:T(2,128)(2,1)S(1)}, u32[]{:S(2)}, u32[]{:S(2)}) collective-permute-start(bf16[2,7168]{1,0:T(2,128)(2,1)} %bitcast.38), channel_id=1, source_target_pairs={{0,8},{8,0},{16,24},{24,16},{1,9},{9,1},{17,25},{25,17},{2,10},{10... | collective-permute-start | bytes 86024 | tf_op jit(solution)/shard_map/ppermute | solution.py:20
  0.8 1.5 %collective-permute-start.1 = (bf16[2,7168]{1,0:T(2,128)(2,1)}, bf16[2,7168]{1,0:T(2,128)(2,1)S(1)}, u32[]{:S(2)}, u32[]{:S(2)}) collective-permute-start(bf16[2,7168]{1,0:T(2,128)(2,1)} %bitcast.40), channel_id=1, source_target_pairs={{0,8},{8,0},{16,24},{24,16},{1,9},{9,1},{17,25},{25,17},{2,10},{10... | collective-permute-start | bytes 86024 | tf_op jit(solution)/shard_map/ppermute | solution.py:20
  1.2 1.4 %collective-permute-start.2 = (bf16[2,7168]{1,0:T(2,128)(2,1)}, bf16[2,7168]{1,0:T(2,128)(2,1)S(1)}, u32[]{:S(2)}, u32[]{:S(2)}) collective-permute-start(bf16[2,7168]{1,0:T(2,128)(2,1)} %bitcast.42), channel_id=1, source_target_pairs={{0,8},{8,0},{16,24},{24,16},{1,9},{9,1},{17,25},{25,17},{2,10},{10... | collective-permute-start | bytes 86024 | tf_op jit(solution)/shard_map/ppermute | solution.py:20
  2.9 9.8 %collective-permute-start.5 = (bf16[16,896]{1,0:T(8,128)(2,1)S(1)}, bf16[16,896]{1,0:T(8,128)(2,1)S(1)}, u32[]{:S(2)}, u32[]{:S(2)}) collective-permute-start(bf16[16,896]{1,0:T(8,128)(2,1)S(1)} %pad_select_fusion), channel_id=1, source_target_pairs={{0,20},{1,21},{2,22},{3,23},{4,16},{5,17},{6,18},{7,19},{8,28},{9,... | collective-permute-start | bytes 86024 | tf_op jit(solution)/shard_map/ppermute | solution.py:42
  7.4 5.3 %collective-permute-start.3 = (bf16[16,896]{1,0:T(8,128)(2,1)S(1)}, bf16[16,896]{1,0:T(8,128)(2,1)S(1)}, u32[]{:S(2)}, u32[]{:S(2)}) collective-permute-start(bf16[16,896]{1,0:T(8,128)(2,1)S(1)} %pad_select_fusion), channel_id=1, source_target_pairs={{0,16},{1,17},{2,18},{3,19},{4,20},{5,21},{6,22},{7,23},{8,24},{9,... | collective-permute-start | bytes 86024 | tf_op jit(solution)/shard_map/ppermute | solution.py:42
  7.7 5.0 %collective-permute-start.4 = (bf16[24,896]{1,0:T(8,128)(2,1)S(1)}, bf16[24,896]{1,0:T(8,128)(2,1)S(1)}, u32[]{:S(2)}, u32[]{:S(2)}) collective-permute-start(bf16[24,896]{1,0:T(8,128)(2,1)S(1)} %get-tuple-element.52.refs_2_), channel_id=1, source_target_pairs={{0,4},{1,5},{2,6},{3,7},{4,0},{5,1},{6,2},{7,3},{8,12},{9,13},{10,... | collective-permute-start | bytes 129032 | tf_op jit(solution)/shard_map/ppermute | solution.py:34
  12.8 8.8 %collective-permute-start.8 = (bf16[80,896]{1,0:T(8,128)(2,1)S(1)}, bf16[80,896]{1,0:T(8,128)(2,1)S(1)}, u32[]{:S(2)}, u32[]{:S(2)}) collective-permute-start(bf16[80,896]{1,0:T(8,128)(2,1)S(1)} %add.10.refs_2_.first), channel_id=1, source_target_pairs={{0,3},{1,2},{2,1},{3,0},{4,7},{5,6},{6,5},{7,4},{8,11},{9,10},{10,... | collective-permute-start | bytes 430088 | tf_op jit(solution)/shard_map/ppermute | solution.py:34
  15.1 7.2 %collective-permute-start.7 = (bf16[80,896]{1,0:T(8,128)(2,1)S(1)}, bf16[80,896]{1,0:T(8,128)(2,1)S(1)}, u32[]{:S(2)}, u32[]{:S(2)}) collective-permute-start(bf16[80,896]{1,0:T(8,128)(2,1)S(1)} %add.10.refs_2_.first), channel_id=1, source_target_pairs={{0,1},{1,0},{2,3},{3,2},{4,5},{5,4},{6,7},{7,6},{8,9},{9,8},{10,11... | collective-permute-start | bytes 430088 | tf_op jit(solution)/shard_map/ppermute | solution.py:34
  15.3 6.9 %collective-permute-start.6 = (bf16[80,896]{1,0:T(8,128)(2,1)S(1)}, bf16[80,896]{1,0:T(8,128)(2,1)S(1)}, u32[]{:S(2)}, u32[]{:S(2)}) collective-permute-start(bf16[80,896]{1,0:T(8,128)(2,1)S(1)} %add.10.refs_2_.first), channel_id=1, source_target_pairs={{0,2},{1,3},{2,0},{3,1},{4,6},{5,7},{6,4},{7,5},{8,10},{9,11},{10,... | collective-permute-start | bytes 430088 | tf_op jit(solution)/shard_map/ppermute | solution.py:34
  22.3 5.5 %copy-start = (f32[1,2,2]{2,1,0:T(2,128)S(1)}, f32[1,2,2]{2,1,0:T(2,128)}, u32[]{:S(2)}) copy-start(f32[1,2,2]{2,1,0:T(2,128)} %param.12) | copy-start | bytes 52
  22.3 5.5 %copy-start.1 = (s32[1,2,2]{2,1,0:T(2,128)S(1)}, s32[1,2,2]{2,1,0:T(2,128)}, u32[]{:S(2)}) copy-start(s32[1,2,2]{2,1,0:T(2,128)} %param.11) | copy-start | bytes 52
  22.3 5.5 %copy-start.2 = (f32[1,2,2]{2,1,0:T(2,128)S(1)}, f32[1,2,2]{2,1,0:T(2,128)}, u32[]{:S(2)}) copy-start(f32[1,2,2]{2,1,0:T(2,128)} %param.15) | copy-start | bytes 52
  22.3 5.5 %copy-start.3 = (s32[1,2,2]{2,1,0:T(2,128)S(1)}, s32[1,2,2]{2,1,0:T(2,128)}, u32[]{:S(2)}) copy-start(s32[1,2,2]{2,1,0:T(2,128)} %param.14) | copy-start | bytes 52
  26.6 2.7 %collective-permute-start.11 = (f32[16,8192]{1,0:T(8,128)S(1)}, f32[16,8192]{1,0:T(8,128)S(1)}, u32[]{:S(2)}, u32[]{:S(2)}) collective-permute-start(f32[16,8192]{1,0:T(8,128)S(1)} %shard_map.115.mine), channel_id=1, source_target_pairs={{0,8},{8,0},{16,24},{24,16},{1,9},{9,1},{17,25},{25,17},{2,10},{10... | collective-permute-start | bytes 1572872 | tf_op jit(solution)/shard_map/ppermute | solution.py:20
  27.9 1.4 %collective-permute-start.9 = (f32[4,4]{1,0:T(4,128)S(1)}, f32[4,4]{1,0:T(4,128)S(1)}, u32[]{:S(2)}, u32[]{:S(2)}) collective-permute-start(f32[4,4]{1,0:T(4,128)S(1)} %pad_maximum_fusion.2), channel_id=1, source_target_pairs={{0,8},{8,0},{16,24},{24,16},{1,9},{9,1},{17,25},{25,17},{2,10},{10... | collective-permute-start | bytes 200 | tf_op jit(solution)/shard_map/ppermute | solution.py:20
  33.7 5.6 %collective-permute-start.12 = (bf16[96,896]{1,0:T(8,128)(2,1)S(1)}, bf16[96,896]{1,0:T(8,128)(2,1)S(1)}, u32[]{:S(2)}, u32[]{:S(2)}) collective-permute-start(bf16[96,896]{1,0:T(8,128)(2,1)S(1)} %get-tuple-element.41), channel_id=1, source_target_pairs={{0,1},{1,0},{2,3},{3,2},{4,5},{5,4},{6,7},{7,6},{8,9},{9,8},{10,11... | collective-permute-start | bytes 516104 | tf_op jit(solution)/shard_map/ppermute | solution.py:34
  35.2 2.7 %collective-permute-start.10 = (f32[2,4]{1,0:T(2,128)S(1)}, f32[2,4]{1,0:T(2,128)S(1)}, u32[]{:S(2)}, u32[]{:S(2)}) collective-permute-start(f32[2,4]{1,0:T(2,128)S(1)} %get-tuple-element.59), channel_id=1, source_target_pairs={{0,16},{1,17},{2,18},{3,19},{4,20},{5,21},{6,22},{7,23},{8,24},{9,... | collective-permute-start | bytes 104 | tf_op jit(solution)/shard_map/ppermute | solution.py:42
  39.4 5.0 %collective-permute-start.13 = (bf16[24,896]{1,0:T(8,128)(2,1)S(1)}, bf16[24,896]{1,0:T(8,128)(2,1)S(1)}, u32[]{:S(2)}, u32[]{:S(2)}) collective-permute-start(bf16[24,896]{1,0:T(8,128)(2,1)S(1)} %get-tuple-element.43), channel_id=1, source_target_pairs={{0,6},{1,7},{2,4},{3,5},{4,2},{5,3},{6,0},{7,1},{8,14},{9,15},{10,... | collective-permute-start | bytes 129032 | tf_op jit(solution)/shard_map/ppermute | solution.py:34
  43.0 3.8 %collective-permute-start.14 = (bf16[24,896]{1,0:T(8,128)(2,1)S(1)}, bf16[24,896]{1,0:T(8,128)(2,1)S(1)}, u32[]{:S(2)}, u32[]{:S(2)}) collective-permute-start(bf16[24,896]{1,0:T(8,128)(2,1)S(1)} %get-tuple-element.44), channel_id=1, source_target_pairs={{0,4},{1,5},{2,6},{3,7},{4,0},{5,1},{6,2},{7,3},{8,12},{9,13},{10,... | collective-permute-start | bytes 129032 | tf_op jit(solution)/shard_map/ppermute | solution.py:34
  43.0 3.8 %collective-permute-start.15 = (bf16[24,896]{1,0:T(8,128)(2,1)S(1)}, bf16[24,896]{1,0:T(8,128)(2,1)S(1)}, u32[]{:S(2)}, u32[]{:S(2)}) collective-permute-start(bf16[24,896]{1,0:T(8,128)(2,1)S(1)} %get-tuple-element.45), channel_id=1, source_target_pairs={{0,2},{1,3},{2,0},{3,1},{4,6},{5,7},{6,4},{7,5},{8,10},{9,11},{10,... | collective-permute-start | bytes 129032 | tf_op jit(solution)/shard_map/ppermute | solution.py:34
  47.0 3.5 %collective-permute-start.16 = (bf16[16,896]{1,0:T(8,128)(2,1)S(1)}, bf16[16,896]{1,0:T(8,128)(2,1)S(1)}, u32[]{:S(2)}, u32[]{:S(2)}) collective-permute-start(bf16[16,896]{1,0:T(8,128)(2,1)S(1)} %get-tuple-element.47), channel_id=1, source_target_pairs={{0,8},{8,0},{16,24},{24,16},{1,9},{9,1},{17,25},{25,17},{2,10},{10... | collective-permute-start | bytes 86024 | tf_op jit(solution)/shard_map/ppermute | solution.py:20

commit v9 on v8

--- a/solution.py
+++ b/solution.py
@@ -391,10 +391,10 @@
     fourth = swap_ranks(blocks, 3)
     second = swap_ranks(blocks, 2)
     third = swap_ranks(blocks, 1)
-    u_high, u_t_high, d, d_t, _, got_order = fetch(
+    d, d_t, u_high, u_t_high, _, got_order = fetch(
         place,
         (w_up, w_down),
-        (Piece(0, 0, piece, half - piece, 3), Piece(1, 1, 0, half, 4)),
+        (Piece(1, 1, 0, half, 4), Piece(0, 0, piece, half - piece, 3)),
         blocks,
         (16, 128),
         lambda place: gathered_order(plan, place[2]),

time: 51.7 us -> 51.7 us (level)
  no operation moved by 1% of the time
where the time goes in v9:
time: 51.7 us; the launch traced here: 51.2 us
  Pallas kernels  20.4 us (39%)
  starting transfers between devices  18.8 us (36%)
  waiting for transfers between devices  8.96 us (17%)
  other arithmetic  1.27 us (2%)
  local copies, waits for them, and re-layouts  0.94 us (2%)
  between operations  0.85 us (2%)
    pallas_call x2, Pallas kernels, fetch(): pl.pallas_call(functools.partial(fetch_kernel, pieces, order), in_specs=[...  10.8 us
    pallas_call x5, Pallas kernels, on_core(): pl.pallas_call(kernel, in_specs=specs, out_specs=[pl.BlockSpec(memory_spa...  9.56 us
    ppermute x8, starting transfers between devices, swap_ranks(): return lax.ppermute(block, 'expert', [(i, i ^ bit) for i in ranks])  8.27 us
    ppermute x3, starting transfers between devices, move(): return lax.ppermute(block, ('section', 'expert'), route)  5.92 us
    ppermute x8, waiting for transfers between devices, swap_ranks(): return lax.ppermute(block, 'expert', [(i, i ^ bit) for i in ranks])  4.91 us
    ppermute x6, starting transfers between devices, swap_cores(): return lax.ppermute(block, 'section', [(i, i ^ 1) for i in sections])  4.58 us
    ppermute x6, waiting for transfers between devices, swap_cores(): return lax.ppermute(block, 'section', [(i, i ^ 1) for i in sections])  2.54 us
    ppermute x3, waiting for transfers between devices, move(): return lax.ppermute(block, ('section', 'expert'), route)  1.51 us
  transfers between devices with their start and end apart: 17, of which 8 were waited for; matrix products, arithmetic and copies ran while one was open for 2% of the time, Pallas kernels for 22%

profile of v9, /device:TPU:1, one launch (start us, length us, event | category | flops | bytes accessed | tf_op | source)
XLA Modules:
  0.0 51.2 jit_solution(17237831108627712519)
XLA Ops:
  0.6 0.1 collective-permute-start
  0.8 0.5 collective-permute-start.1
  1.2 0.1 collective-permute-start.2
  1.3 0.9 %pad_maximum_fusion = bf16[6,7168]{1,0:T(8,128)(2,1)S(1)} fusion(bf16[2,7168]{1,0:T(2,128)(2,1)} %bitcast.43, bf16[2,7168]{1,0:T(2,128)(2,1)} %bitcast.41, bf16[2,7168]{1,0:T(2,128)(2,1)} %bitcast.39), kind=kLoop, calls=%fused_computation | loop fusion | flops 258048 | bytes 172032 | tf_op jit(solution)/shard_map/concatenate | solution.py:359
  2.2 0.1 pad_add_fusion.place
  2.3 0.0 collective-permute-done
  2.3 0.0 collective-permute-done.1
  2.3 0.3 collective-permute-done.2
  2.6 0.1 pad_maximum_fusion.1
  2.9 4.5 %collective-permute-start.5 = (bf16[16,896]{1,0:T(8,128)(2,1)S(1)}, bf16[16,896]{1,0:T(8,128)(2,1)S(1)}, u32[]{:S(2)}, u32[]{:S(2)}) collective-permute-start(bf16[16,896]{1,0:T(8,128)(2,1)S(1)} %pad_select_fusion), channel_id=1, source_target_pairs={{0,20},{1,21},{2,22},{3,23},{4,16},{5,17},{6,18},{7,19},{8,28},{9,... | collective-permute-start | bytes 86024 | tf_op jit(solution)/shard_map/ppermute | solution.py:42
  7.4 0.3 collective-permute-start.3
  7.7 0.2 collective-permute-start.4
  7.8 4.8 %shard_map.113 = (bf16[3584,1024]{1,0:T(8,128)(2,1)S(1)}, bf16[1024,3584]{1,0:T(8,128)(2,1)S(1)}, bf16[896,1024]{1,0:T(8,128)(2,1)S(1)}, bf16[1024,896]{1,0:T(8,...) custom-call(s32[3]{0:T(128)S(1)} %pad_add_fusion.place, bf16[7168,1024]{1,0:T(8,128)(2,1)} %refs_0_.2, ...), custom_call_target="tpu_custom_call" | custom-call | bytes 18350080 | tf_op jit(solution)/shard_map/pallas_call | solution.py:170
  12.7 0.0 collective-permute-done.3
  12.7 0.0 collective-permute-done.4
  12.7 0.0 collective-permute-done.5
  12.8 2.3 %collective-permute-start.8 = (bf16[80,896]{1,0:T(8,128)(2,1)S(1)}, bf16[80,896]{1,0:T(8,128)(2,1)S(1)}, u32[]{:S(2)}, u32[]{:S(2)}) collective-permute-start(bf16[80,896]{1,0:T(8,128)(2,1)S(1)} %add.10.refs_2_.first), channel_id=1, source_target_pairs={{0,3},{1,2},{2,1},{3,0},{4,7},{5,6},{6,5},{7,4},{8,11},{9,10},{10,... | collective-permute-start | bytes 430088 | tf_op jit(solution)/shard_map/ppermute | solution.py:34
  15.1 0.2 collective-permute-start.7
  15.3 0.2 collective-permute-start.6
  15.5 6.0 %shard_map.114 = (bf16[1024,3584]{1,0:T(8,128)(2,1)S(1)}, bf16[3584,1024]{1,0:T(8,128)(2,1)S(1)}, bf16[2688,1024]{1,0:T(8,128)(2,1)S(1)}, bf16[1024,2688]{1,0:T(...) custom-call(s32[3]{0:T(128)S(1)} %pad_add_fusion.place, bf16[7168,1024]{1,0:T(8,128)(2,1)} %refs_0_.3, ...), custom_call_target="tpu_custom_call" | custom-call | bytes 25690112 | tf_op jit(solution)/shard_map/pallas_call | solution.py:170
  21.5 0.0 collective-permute-done.8.fourth
  21.5 0.7 %collective-permute-done.7.third = bf16[80,896]{1,0:T(8,128)(2,1)S(1)} collective-permute-done((bf16[80,896]{1,0:T(8,128)(2,1)S(1)}, bf16[80,896]{1,0:T(8,128)(2,1)S(1)}, u32[]{:S(2)}, u32[]{:S(2)}) %collective-permute-start.7) | collective-permute-done | bytes 143392 | tf_op jit(solution)/shard_map/ppermute | solution.py:34
  22.3 0.0 collective-permute-done.6.second
  22.3 0.0 copy-start.3
  22.3 4.3 %shard_map.115.mine = f32[16,8192]{1,0:T(8,128)S(1)} custom-call(bf16[320,320]{1,0:T(8,128)(2,1)S(1)} %get-tuple-element.26.order, bf16[80,896]{1,0:T(8,128)(2,1)S(1)} %add.10.refs_2_.first, bf16[80,896]{1,0:T(8,128)(2,1)S(1)} %collective-permute-done.6.second, bf16[80,896]{1,0:T(8,128)(2,1)S(1)} %collective-permute-done.7.third, ...), custom_call_target="tpu_custom_call" | custom-call | flops 5637144576 | bytes 22020096 | tf_op jit(solution)/shard_map/pallas_call | solution.py:318
  26.6 1.2 %collective-permute-start.11 = (f32[16,8192]{1,0:T(8,128)S(1)}, f32[16,8192]{1,0:T(8,128)S(1)}, u32[]{:S(2)}, u32[]{:S(2)}) collective-permute-start(f32[16,8192]{1,0:T(8,128)S(1)} %shard_map.115.mine), channel_id=1, source_target_pairs={{0,8},{8,0},{16,24},{24,16},{1,9},{9,1},{17,25},{25,17},{2,10},{10... | collective-permute-start | bytes 1572872 | tf_op jit(solution)/shard_map/ppermute | solution.py:20
  27.7 0.0 copy-done
  27.7 0.1 fusion
  27.8 0.1 collective-permute-start.9
  27.9 1.3 %collective-permute-done.9._ = f32[4,4]{1,0:T(4,128)S(1)} collective-permute-done((f32[4,4]{1,0:T(4,128)S(1)}, f32[4,4]{1,0:T(4,128)S(1)}, u32[]{:S(2)}, u32[]{:S(2)}) %collective-permute-start.9) | collective-permute-done | bytes 96 | tf_op jit(solution)/shard_map/ppermute | solution.py:20
  29.3 0.0 collective-permute-done.11.theirs
  29.3 4.4 %shard_map.117 = (bf16[96,896]{1,0:T(8,128)(2,1)S(1)}, bf16[96,896]{1,0:T(8,128)(2,1)S(1)}) custom-call(s32[3]{0:T(128)S(1)} %pad_add_fusion.place, f32[4,4]{1,0:T(4,128)S(1)} %collective-permute-done.9._, bf16[192,192]{1,0:T(8,128)(2,1)S(1)} %get-tuple-element.35.order, f32[16,8192]{1,0:T(8,128)S(1)} %shard_map.115.mine, ...), custom_call_target="tpu_custom_call" | custom-call | flops 5637144576 | bytes 22020096 | tf_op jit(solution)/shard_map/pallas_call | solution.py:318
  33.7 1.5 %collective-permute-start.12 = (bf16[96,896]{1,0:T(8,128)(2,1)S(1)}, bf16[96,896]{1,0:T(8,128)(2,1)S(1)}, u32[]{:S(2)}, u32[]{:S(2)}) collective-permute-start(bf16[96,896]{1,0:T(8,128)(2,1)S(1)} %get-tuple-element.41), channel_id=1, source_target_pairs={{0,1},{1,0},{2,3},{3,2},{4,5},{5,4},{6,7},{7,6},{8,9},{9,8},{10,11... | collective-permute-start | bytes 516104 | tf_op jit(solution)/shard_map/ppermute | solution.py:34
  35.1 1.2 %collective-permute-start.10 = (f32[2,4]{1,0:T(2,128)S(1)}, f32[2,4]{1,0:T(2,128)S(1)}, u32[]{:S(2)}, u32[]{:S(2)}) collective-permute-start(f32[2,4]{1,0:T(2,128)S(1)} %get-tuple-element.59), channel_id=1, source_target_pairs={{0,16},{1,17},{2,18},{3,19},{4,20},{5,21},{6,22},{7,23},{8,24},{9,... | collective-permute-start | bytes 104 | tf_op jit(solution)/shard_map/ppermute | solution.py:42
  36.3 1.5 %collective-permute-done.10 = f32[2,4]{1,0:T(2,128)S(1)} collective-permute-done((f32[2,4]{1,0:T(2,128)S(1)}, f32[2,4]{1,0:T(2,128)S(1)}, u32[]{:S(2)}, u32[]{:S(2)}) %collective-permute-start.10) | collective-permute-done | bytes 64 | tf_op jit(solution)/shard_map/ppermute | solution.py:42
  37.9 0.1 concatenate.32.weights
  37.9 1.4 %collective-permute-done.12.got = bf16[96,896]{1,0:T(8,128)(2,1)S(1)} collective-permute-done((bf16[96,896]{1,0:T(8,128)(2,1)S(1)}, bf16[96,896]{1,0:T(8,128)(2,1)S(1)}, u32[]{:S(2)}, u32[]{:S(2)}) %collective-permute-start.12) | collective-permute-done | bytes 172064 | tf_op jit(solution)/shard_map/ppermute | solution.py:34
  39.4 3.5 %collective-permute-start.13 = (bf16[24,896]{1,0:T(8,128)(2,1)S(1)}, bf16[24,896]{1,0:T(8,128)(2,1)S(1)}, u32[]{:S(2)}, u32[]{:S(2)}) collective-permute-start(bf16[24,896]{1,0:T(8,128)(2,1)S(1)} %get-tuple-element.43), channel_id=1, source_target_pairs={{0,6},{1,7},{2,4},{3,5},{4,2},{5,3},{6,0},{7,1},{8,14},{9,15},{10,... | collective-permute-start | bytes 129032 | tf_op jit(solution)/shard_map/ppermute | solution.py:34
  42.9 0.0 collective-permute-start.14
  42.9 0.4 collective-permute-start.15
  43.3 0.6 %shard_map.116 = (f32[96,128]{1,0:T(8,128)S(1)}, bf16[32,24]{1,0:T(8,128)(2,1)S(1)}) custom-call(s32[3]{0:T(128)S(1)} %pad_add_fusion.place, f32[24,4]{1,0:T(8,128)S(1)} %concatenate.32.weights), custom_call_target="tpu_custom_call" | custom-call | flops 1835008 | bytes 7168 | tf_op jit(solution)/shard_map/pallas_call | solution.py:318
  43.9 0.4 collective-permute-done.13.refs_1_
  44.3 2.4 %collective-permute-done.14.refs_2_ = bf16[24,896]{1,0:T(8,128)(2,1)S(1)} collective-permute-done((bf16[24,896]{1,0:T(8,128)(2,1)S(1)}, bf16[24,896]{1,0:T(8,128)(2,1)S(1)}, u32[]{:S(2)}, u32[]{:S(2)}) %collective-permute-start.14) | collective-permute-done | bytes 43040 | tf_op jit(solution)/shard_map/ppermute | solution.py:34
  46.7 0.0 collective-permute-done.15.refs_3_
  46.7 0.2 shard_map.119
  46.9 2.7 %collective-permute-start.16 = (bf16[16,896]{1,0:T(8,128)(2,1)S(1)}, bf16[16,896]{1,0:T(8,128)(2,1)S(1)}, u32[]{:S(2)}, u32[]{:S(2)}) collective-permute-start(bf16[16,896]{1,0:T(8,128)(2,1)S(1)} %get-tuple-element.47), channel_id=1, source_target_pairs={{0,8},{8,0},{16,24},{24,16},{1,9},{9,1},{17,25},{25,17},{2,10},{10... | collective-permute-start | bytes 86024 | tf_op jit(solution)/shard_map/ppermute | solution.py:20
  49.6 0.8 %collective-permute-done.16 = bf16[16,896]{1,0:T(8,128)(2,1)S(1)} collective-permute-done((bf16[16,896]{1,0:T(8,128)(2,1)S(1)}, bf16[16,896]{1,0:T(8,128)(2,1)S(1)}, u32[]{:S(2)}, u32[]{:S(2)}) %collective-permute-start.16) | collective-permute-done | bytes 28704 | tf_op jit(solution)/shard_map/ppermute | solution.py:20
  50.5 0.7 %slice_bitcast_fusion = (bf16[1,2,7168]{2,1,0:T(2,128)(2,1)}, bf16[1,2,7168]{2,1,0:T(2,128)(2,1)}) fusion(bf16[4,7168]{1,0:T(4,128)(2,1)S(1)} %maximum_select_fusion), kind=kLoop, calls=%fused_computation.7 | loop fusion | bytes 114688 | tf_op jit(solution)/shard_map/broadcast_in_dim | solution.py:456
  (29 shorter events, 0.4 us)
Async XLA Ops:
  0.6 1.6 %collective-permute-start = (bf16[2,7168]{1,0:T(2,128)(2,1)}, bf16[2,7168]{1,0:T(2,128)(2,1)S(1)}, u32[]{:S(2)}, u32[]{:S(2)}) collective-permute-start(bf16[2,7168]{1,0:T(2,128)(2,1)} %bitcast.38), channel_id=1, source_target_pairs={{0,8},{8,0},{16,24},{24,16},{1,9},{9,1},{17,25},{25,17},{2,10},{10... | collective-permute-start | bytes 86024 | tf_op jit(solution)/shard_map/ppermute | solution.py:20
  0.8 1.5 %collective-permute-start.1 = (bf16[2,7168]{1,0:T(2,128)(2,1)}, bf16[2,7168]{1,0:T(2,128)(2,1)S(1)}, u32[]{:S(2)}, u32[]{:S(2)}) collective-permute-start(bf16[2,7168]{1,0:T(2,128)(2,1)} %bitcast.40), channel_id=1, source_target_pairs={{0,8},{8,0},{16,24},{24,16},{1,9},{9,1},{17,25},{25,17},{2,10},{10... | collective-permute-start | bytes 86024 | tf_op jit(solution)/shard_map/ppermute | solution.py:20
  1.2 1.4 %collective-permute-start.2 = (bf16[2,7168]{1,0:T(2,128)(2,1)}, bf16[2,7168]{1,0:T(2,128)(2,1)S(1)}, u32[]{:S(2)}, u32[]{:S(2)}) collective-permute-start(bf16[2,7168]{1,0:T(2,128)(2,1)} %bitcast.42), channel_id=1, source_target_pairs={{0,8},{8,0},{16,24},{24,16},{1,9},{9,1},{17,25},{25,17},{2,10},{10... | collective-permute-start | bytes 86024 | tf_op jit(solution)/shard_map/ppermute | solution.py:20
  2.9 9.8 %collective-permute-start.5 = (bf16[16,896]{1,0:T(8,128)(2,1)S(1)}, bf16[16,896]{1,0:T(8,128)(2,1)S(1)}, u32[]{:S(2)}, u32[]{:S(2)}) collective-permute-start(bf16[16,896]{1,0:T(8,128)(2,1)S(1)} %pad_select_fusion), channel_id=1, source_target_pairs={{0,20},{1,21},{2,22},{3,23},{4,16},{5,17},{6,18},{7,19},{8,28},{9,... | collective-permute-start | bytes 86024 | tf_op jit(solution)/shard_map/ppermute | solution.py:42
  7.4 5.3 %collective-permute-start.3 = (bf16[16,896]{1,0:T(8,128)(2,1)S(1)}, bf16[16,896]{1,0:T(8,128)(2,1)S(1)}, u32[]{:S(2)}, u32[]{:S(2)}) collective-permute-start(bf16[16,896]{1,0:T(8,128)(2,1)S(1)} %pad_select_fusion), channel_id=1, source_target_pairs={{0,16},{1,17},{2,18},{3,19},{4,20},{5,21},{6,22},{7,23},{8,24},{9,... | collective-permute-start | bytes 86024 | tf_op jit(solution)/shard_map/ppermute | solution.py:42
  7.7 5.0 %collective-permute-start.4 = (bf16[24,896]{1,0:T(8,128)(2,1)S(1)}, bf16[24,896]{1,0:T(8,128)(2,1)S(1)}, u32[]{:S(2)}, u32[]{:S(2)}) collective-permute-start(bf16[24,896]{1,0:T(8,128)(2,1)S(1)} %get-tuple-element.52.refs_2_), channel_id=1, source_target_pairs={{0,4},{1,5},{2,6},{3,7},{4,0},{5,1},{6,2},{7,3},{8,12},{9,13},{10,... | collective-permute-start | bytes 129032 | tf_op jit(solution)/shard_map/ppermute | solution.py:34
  12.8 8.8 %collective-permute-start.8 = (bf16[80,896]{1,0:T(8,128)(2,1)S(1)}, bf16[80,896]{1,0:T(8,128)(2,1)S(1)}, u32[]{:S(2)}, u32[]{:S(2)}) collective-permute-start(bf16[80,896]{1,0:T(8,128)(2,1)S(1)} %add.10.refs_2_.first), channel_id=1, source_target_pairs={{0,3},{1,2},{2,1},{3,0},{4,7},{5,6},{6,5},{7,4},{8,11},{9,10},{10,... | collective-permute-start | bytes 430088 | tf_op jit(solution)/shard_map/ppermute | solution.py:34
  15.1 7.2 %collective-permute-start.7 = (bf16[80,896]{1,0:T(8,128)(2,1)S(1)}, bf16[80,896]{1,0:T(8,128)(2,1)S(1)}, u32[]{:S(2)}, u32[]{:S(2)}) collective-permute-start(bf16[80,896]{1,0:T(8,128)(2,1)S(1)} %add.10.refs_2_.first), channel_id=1, source_target_pairs={{0,1},{1,0},{2,3},{3,2},{4,5},{5,4},{6,7},{7,6},{8,9},{9,8},{10,11... | collective-permute-start | bytes 430088 | tf_op jit(solution)/shard_map/ppermute | solution.py:34
  15.3 6.9 %collective-permute-start.6 = (bf16[80,896]{1,0:T(8,128)(2,1)S(1)}, bf16[80,896]{1,0:T(8,128)(2,1)S(1)}, u32[]{:S(2)}, u32[]{:S(2)}) collective-permute-start(bf16[80,896]{1,0:T(8,128)(2,1)S(1)} %add.10.refs_2_.first), channel_id=1, source_target_pairs={{0,2},{1,3},{2,0},{3,1},{4,6},{5,7},{6,4},{7,5},{8,10},{9,11},{10,... | collective-permute-start | bytes 430088 | tf_op jit(solution)/shard_map/ppermute | solution.py:34
  22.3 5.5 %copy-start = (f32[1,2,2]{2,1,0:T(2,128)S(1)}, f32[1,2,2]{2,1,0:T(2,128)}, u32[]{:S(2)}) copy-start(f32[1,2,2]{2,1,0:T(2,128)} %param.12) | copy-start | bytes 52
  22.3 5.5 %copy-start.1 = (s32[1,2,2]{2,1,0:T(2,128)S(1)}, s32[1,2,2]{2,1,0:T(2,128)}, u32[]{:S(2)}) copy-start(s32[1,2,2]{2,1,0:T(2,128)} %param.11) | copy-start | bytes 52
  22.3 5.5 %copy-start.2 = (f32[1,2,2]{2,1,0:T(2,128)S(1)}, f32[1,2,2]{2,1,0:T(2,128)}, u32[]{:S(2)}) copy-start(f32[1,2,2]{2,1,0:T(2,128)} %param.15) | copy-start | bytes 52
  22.3 5.5 %copy-start.3 = (s32[1,2,2]{2,1,0:T(2,128)S(1)}, s32[1,2,2]{2,1,0:T(2,128)}, u32[]{:S(2)}) copy-start(s32[1,2,2]{2,1,0:T(2,128)} %param.14) | copy-start | bytes 52
  26.6 2.7 %collective-permute-start.11 = (f32[16,8192]{1,0:T(8,128)S(1)}, f32[16,8192]{1,0:T(8,128)S(1)}, u32[]{:S(2)}, u32[]{:S(2)}) collective-permute-start(f32[16,8192]{1,0:T(8,128)S(1)} %shard_map.115.mine), channel_id=1, source_target_pairs={{0,8},{8,0},{16,24},{24,16},{1,9},{9,1},{17,25},{25,17},{2,10},{10... | collective-permute-start | bytes 1572872 | tf_op jit(solution)/shard_map/ppermute | solution.py:20
  27.8 1.4 %collective-permute-start.9 = (f32[4,4]{1,0:T(4,128)S(1)}, f32[4,4]{1,0:T(4,128)S(1)}, u32[]{:S(2)}, u32[]{:S(2)}) collective-permute-start(f32[4,4]{1,0:T(4,128)S(1)} %pad_maximum_fusion.2), channel_id=1, source_target_pairs={{0,8},{8,0},{16,24},{24,16},{1,9},{9,1},{17,25},{25,17},{2,10},{10... | collective-permute-start | bytes 200 | tf_op jit(solution)/shard_map/ppermute | solution.py:20
  33.7 5.6 %collective-permute-start.12 = (bf16[96,896]{1,0:T(8,128)(2,1)S(1)}, bf16[96,896]{1,0:T(8,128)(2,1)S(1)}, u32[]{:S(2)}, u32[]{:S(2)}) collective-permute-start(bf16[96,896]{1,0:T(8,128)(2,1)S(1)} %get-tuple-element.41), channel_id=1, source_target_pairs={{0,1},{1,0},{2,3},{3,2},{4,5},{5,4},{6,7},{7,6},{8,9},{9,8},{10,11... | collective-permute-start | bytes 516104 | tf_op jit(solution)/shard_map/ppermute | solution.py:34
  35.1 2.7 %collective-permute-start.10 = (f32[2,4]{1,0:T(2,128)S(1)}, f32[2,4]{1,0:T(2,128)S(1)}, u32[]{:S(2)}, u32[]{:S(2)}) collective-permute-start(f32[2,4]{1,0:T(2,128)S(1)} %get-tuple-element.59), channel_id=1, source_target_pairs={{0,16},{1,17},{2,18},{3,19},{4,20},{5,21},{6,22},{7,23},{8,24},{9,... | collective-permute-start | bytes 104 | tf_op jit(solution)/shard_map/ppermute | solution.py:42
  39.4 5.0 %collective-permute-start.13 = (bf16[24,896]{1,0:T(8,128)(2,1)S(1)}, bf16[24,896]{1,0:T(8,128)(2,1)S(1)}, u32[]{:S(2)}, u32[]{:S(2)}) collective-permute-start(bf16[24,896]{1,0:T(8,128)(2,1)S(1)} %get-tuple-element.43), channel_id=1, source_target_pairs={{0,6},{1,7},{2,4},{3,5},{4,2},{5,3},{6,0},{7,1},{8,14},{9,15},{10,... | collective-permute-start | bytes 129032 | tf_op jit(solution)/shard_map/ppermute | solution.py:34
  42.9 3.8 %collective-permute-start.14 = (bf16[24,896]{1,0:T(8,128)(2,1)S(1)}, bf16[24,896]{1,0:T(8,128)(2,1)S(1)}, u32[]{:S(2)}, u32[]{:S(2)}) collective-permute-start(bf16[24,896]{1,0:T(8,128)(2,1)S(1)} %get-tuple-element.44), channel_id=1, source_target_pairs={{0,4},{1,5},{2,6},{3,7},{4,0},{5,1},{6,2},{7,3},{8,12},{9,13},{10,... | collective-permute-start | bytes 129032 | tf_op jit(solution)/shard_map/ppermute | solution.py:34
  42.9 3.8 %collective-permute-start.15 = (bf16[24,896]{1,0:T(8,128)(2,1)S(1)}, bf16[24,896]{1,0:T(8,128)(2,1)S(1)}, u32[]{:S(2)}, u32[]{:S(2)}) collective-permute-start(bf16[24,896]{1,0:T(8,128)(2,1)S(1)} %get-tuple-element.45), channel_id=1, source_target_pairs={{0,2},{1,3},{2,0},{3,1},{4,6},{5,7},{6,4},{7,5},{8,10},{9,11},{10,... | collective-permute-start | bytes 129032 | tf_op jit(solution)/shard_map/ppermute | solution.py:34
  46.9 3.5 %collective-permute-start.16 = (bf16[16,896]{1,0:T(8,128)(2,1)S(1)}, bf16[16,896]{1,0:T(8,128)(2,1)S(1)}, u32[]{:S(2)}, u32[]{:S(2)}) collective-permute-start(bf16[16,896]{1,0:T(8,128)(2,1)S(1)} %get-tuple-element.47), channel_id=1, source_target_pairs={{0,8},{8,0},{16,24},{24,16},{1,9},{9,1},{17,25},{25,17},{2,10},{10... | collective-permute-start | bytes 86024 | tf_op jit(solution)/shard_map/ppermute | solution.py:20
